TPU v7x, 32 devices: a whole 2x2x4 slice. The times are simulated.
32 devices in a mesh: row: 4 (over y, x), col: 8 (over z, core).
Axes of the slice: x: 2, y: 2, z: 4, core: 2. Of those that a mesh axis runs over, the one named last changes fastest.
Arguments:
- left_blocks: bfloat16 [4096, 4096], P('row', 'col'), may hold values from -6 to 6
- right_blocks: bfloat16 [4096, 4096], P('row', 'col'), may hold values from -0.125 to 0.125
- a_pattern: int32 [32, 32], P('row', 'col'), may hold values from 0 to 1, as said below
- b_pattern: int32 [32, 32], P('row', 'col'), may hold values 0 or 1
- keep_mask: int32 [32, 32], P('row', 'col'), may hold values 0 or 1
Outputs:
- product: bfloat16 [4096, 4096], P('row', 'col')
Inputs may be any that keep to these rules, and one draw needn't show every extreme that they name: 1 marks a stored block; on average the share of stored blocks rises from about a quarter in the first block rows to about nine tenths in the last. A program may rely on no bound on the sum of `a_pattern` on one device or in one block row.
All inputs are finite; a program needn't handle non-finite values. No bound on the sum of `b_pattern` or of `keep_mask` on one device may be relied on, other than what follows from the above.
Results may differ from a plain program's by a relative error of at most 0.001.
Values may be sent and summed in bfloat16 or wider, within the bound.
No kernel may reach another device: no remote copies, remote signals or barrier semaphores. Data moves between devices by JAX's collectives and lax.ppermute only.
A program may use at most 128 MiB of HBM per device.

v0:
```python
import jax
import jax.numpy as jnp
from jax import lax
from jax.sharding import PartitionSpec as P


def from_behind(block, axis, distance):
    devices = range(lax.axis_size(axis))
    route = [((i - distance) % len(devices), i) for i in devices]
    return lax.ppermute(block, axis, route)


def expand_blocks(pattern_int, block_size):
    return jnp.repeat(jnp.repeat(pattern_int, block_size, axis=0), block_size, axis=1)


def advance_left(shard_data):
    return from_behind(shard_data, "col", -1)


def on_device(left_blocks, right_blocks, a_pattern, b_pattern, keep_mask):
    block_size = left_blocks.shape[0] // a_pattern.shape[0]
    left_part = left_blocks * expand_blocks(a_pattern, block_size).astype(jnp.bfloat16)
    right_part = right_blocks * expand_blocks(b_pattern, block_size).astype(jnp.bfloat16)
    n_row = lax.axis_size("row")
    n_col = lax.axis_size("col")
    panel_ratio = n_col // n_row
    product_sum = jnp.zeros((left_part.shape[0], right_part.shape[1]), jnp.float32)
    row_place = lax.axis_index("row")
    col_place = lax.axis_index("col")
    left_amount = panel_ratio * row_place % n_col
    for power in range((n_col - 1).bit_length()):
        shifted = from_behind(left_part, "col", -(1 << power))
        left_part = jnp.where(left_amount // (1 << power) % 2 == 1, shifted, left_part)
    right_amount = col_place // panel_ratio % n_row
    for power in range((n_row - 1).bit_length()):
        shifted = from_behind(right_part, "row", -(1 << power))
        right_part = jnp.where(right_amount // (1 << power) % 2 == 1, shifted, right_part)
    panel_rows = right_part.shape[0] // panel_ratio
    following = from_behind(right_part, "row", -1)
    joined = jnp.concatenate([right_part, following], axis=0)
    right_part = lax.dynamic_slice_in_dim(
        joined, col_place % panel_ratio * panel_rows, right_part.shape[0], 0
    )

    def run_group(running, left_now, right_now, final_group):
        for within in range(panel_ratio):
            panel_now = right_now[within * panel_rows : (within + 1) * panel_rows]
            running = running + jnp.dot(left_now, panel_now, preferred_element_type=jnp.float32)
            if not final_group or within < panel_ratio - 1:
                left_now = advance_left(left_now)
        return (running, left_now)

    def advance_group(group_index, carried):
        running, left_now, right_now = carried
        running, left_now = run_group(running, left_now, right_now, False)
        right_now = from_behind(right_now, "row", -1)
        return (running, left_now, right_now)

    product_sum, left_part, right_part = lax.fori_loop(
        0, n_row - 1, advance_group, (product_sum, left_part, right_part)
    )
    product_sum, left_part = run_group(product_sum, left_part, right_part, True)
    kept_cells = expand_blocks(keep_mask, block_size).astype(jnp.float32)
    return (product_sum * kept_cells).astype(jnp.bfloat16)


def solution(mesh):
    placed = (P("row", "col"), P("row", "col"), P("row", "col"), P("row", "col"), P("row", "col"))
    return jax.shard_map(
        on_device, mesh=mesh, in_specs=placed, out_specs=P("row", "col"), check_vma=False
    )
```

profile of v0, /device:TPU:0, one launch (start us, length us, event | category | flops | bytes accessed | tf_op | source)
XLA Modules:
  0.0 229.3 jit_solution(5496487261100323617)
XLA Ops:
  0.0 0.8 convert_element_type.39
  0.8 0.1 copy.7
  0.9 2.9 %broadcast_in_dim.25 = bf16[1024,4,128]{2,1,0:T(4,128)(2,1)S(1)} broadcast(bf16[1024,4]{1,0:T(8,128)(2,1)S(1)} %bitcast.26), dimensions={0,1} | broadcast | bytes 1056768 | tf_op jit(solution)/shard_map/broadcast_in_dim | solution.py:14
  3.9 0.2 bitcast_multiply_fusion.1
  4.1 3.9 %collective-permute-start.6 = (bf16[1024,512]{1,0:T(8,128)(2,1)S(1)}, bf16[1024,512]{1,0:T(8,128)(2,1)}, u32[]{:S(2)}, u32[]{:S(2)}) collective-permute-start(bf16[1024,512]{1,0:T(8,128)(2,1)S(1)} %bitcast_multiply_fusion.1), channel_id=1, source_target_pairs={{8,0},{16,8},{24,16},{0,24},{9,1},{17,9},{25,17},{1,25},{10,2},{18... | collective-permute-start | bytes 3145736 | tf_op jit(solution)/shard_map/ppermute | solution.py:10
  8.0 0.1 copy.6
  8.2 2.9 %broadcast_in_dim.23 = bf16[1024,4,128]{2,1,0:T(4,128)(2,1)S(1)} broadcast(bf16[1024,4]{1,0:T(8,128)(2,1)S(1)} %bitcast.27), dimensions={0,1} | broadcast | bytes 1056768 | tf_op jit(solution)/shard_map/broadcast_in_dim | solution.py:14
  11.1 0.2 bitcast_multiply_fusion.2
  11.3 2.8 %collective-permute-start.3 = (bf16[1024,512]{1,0:T(8,128)(2,1)S(1)}, bf16[1024,512]{1,0:T(8,128)(2,1)}, u32[]{:S(2)}, u32[]{:S(2)}) collective-permute-start(bf16[1024,512]{1,0:T(8,128)(2,1)S(1)} %bitcast_multiply_fusion.2), channel_id=1, source_target_pairs={{1,0},{2,1},{3,2},{4,3},{5,4},{6,5},{7,6},{0,7},{9,8},{10,9},{11,1... | collective-permute-start | bytes 3145736 | tf_op jit(solution)/shard_map/ppermute | solution.py:10
  14.1 16.3 %collective-permute-done.6 = bf16[1024,512]{1,0:T(8,128)(2,1)} collective-permute-done((bf16[1024,512]{1,0:T(8,128)(2,1)S(1)}, bf16[1024,512]{1,0:T(8,128)(2,1)}, u32[]{:S(2)}, u32[]{:S(2)}) %collective-permute-start.6) | collective-permute-done | bytes 1048608 | tf_op jit(solution)/shard_map/ppermute | solution.py:10
  30.4 0.1 broadcast_select_fusion
  30.6 1.7 collective-permute-start.7
  32.3 0.1 broadcast_select_fusion.2
  32.4 4.9 %collective-permute-start.4 = (bf16[1024,512]{1,0:T(8,128)(2,1)S(1)}, bf16[1024,512]{1,0:T(8,128)(2,1)}, u32[]{:S(2)}, u32[]{:S(2)}) collective-permute-start(bf16[1024,512]{1,0:T(8,128)(2,1)S(1)} %broadcast_select_fusion.2), channel_id=1, source_target_pairs={{2,0},{3,1},{4,2},{5,3},{6,4},{7,5},{0,6},{1,7},{10,8},{11,9},{12,... | collective-permute-start | bytes 3145736 | tf_op jit(solution)/shard_map/ppermute | solution.py:10
  37.3 17.7 %collective-permute-done.7 = bf16[1024,512]{1,0:T(8,128)(2,1)} collective-permute-done((bf16[1024,512]{1,0:T(8,128)(2,1)S(1)}, bf16[1024,512]{1,0:T(8,128)(2,1)}, u32[]{:S(2)}, u32[]{:S(2)}) %collective-permute-start.7) | collective-permute-done | bytes 1048608 | tf_op jit(solution)/shard_map/ppermute | solution.py:10
  55.0 0.1 broadcast_select_fusion.1
  55.1 3.3 %collective-permute-start.8 = (bf16[1024,512]{1,0:T(8,128)(2,1)S(1)}, bf16[1024,512]{1,0:T(8,128)(2,1)}, u32[]{:S(2)}, u32[]{:S(2)}) collective-permute-start(bf16[1024,512]{1,0:T(8,128)(2,1)S(1)} %broadcast_select_fusion.1), channel_id=1, source_target_pairs={{8,0},{16,8},{24,16},{0,24},{9,1},{17,9},{25,17},{1,25},{10,2},{18... | collective-permute-start | bytes 3145736 | tf_op jit(solution)/shard_map/ppermute | solution.py:10
  58.4 0.1 collective-permute-done.4
  58.5 1.1 broadcast_select_fusion.3
  59.6 3.7 %collective-permute-start.5 = (bf16[1024,512]{1,0:T(8,128)(2,1)}, bf16[1024,512]{1,0:T(8,128)(2,1)S(1)}, u32[]{:S(2)}, u32[]{:S(2)}) collective-permute-start(bf16[1024,512]{1,0:T(8,128)(2,1)} %broadcast_select_fusion.3), channel_id=1, source_target_pairs={{4,0},{5,1},{6,2},{7,3},{0,4},{1,5},{2,6},{3,7},{12,8},{13,9},{14,... | collective-permute-start | bytes 3145736 | tf_op jit(solution)/shard_map/ppermute | solution.py:10
  63.3 15.7 %collective-permute-done.8 = bf16[1024,512]{1,0:T(8,128)(2,1)} collective-permute-done((bf16[1024,512]{1,0:T(8,128)(2,1)S(1)}, bf16[1024,512]{1,0:T(8,128)(2,1)}, u32[]{:S(2)}, u32[]{:S(2)}) %collective-permute-start.8) | collective-permute-done | bytes 1048608 | tf_op jit(solution)/shard_map/ppermute | solution.py:10
  79.0 1.3 fusion.5
  80.3 26.8 %collective-permute-done.5 = bf16[1024,512]{1,0:T(8,128)(2,1)S(1)} collective-permute-done((bf16[1024,512]{1,0:T(8,128)(2,1)}, bf16[1024,512]{1,0:T(8,128)(2,1)S(1)}, u32[]{:S(2)}, u32[]{:S(2)}) %collective-permute-start.5) | collective-permute-done | bytes 1048608 | tf_op jit(solution)/shard_map/ppermute | solution.py:10
  107.1 2.3 %broadcast_select_fusion.4 = bf16[1024,512]{1,0:T(8,128)(2,1)} fusion(bf16[1024,512]{1,0:T(8,128)(2,1)S(1)} %collective-permute-done.5, bf16[1024,512]{1,0:T(8,128)(2,1)} %broadcast_select_fusion.3, pred[]{:T(512)S(6)} %eq.24), kind=kLoop, calls=%fused_computation.16 | loop fusion | flops 524288 | bytes 3145729 | tf_op jit(solution)/shard_map/jit(_where)/select_n | solution.py:34
  109.4 100.6 %while.15 = (s32[]{:T(128)}, f32[1024,512]{1,0:T(8,128)}, bf16[1024,512]{1,0:T(8,128)(2,1)}, bf16[1024,512]{1,0:T(8,128)(2,1)S(1)}, s32[]{:T(128)}, /*index=5*/s32[]{:T(128)}) while((s32[]{:T(128)}, f32[1024,512]{1,0:T(8,128)}, bf16[1024,512]{1,0:T(8,128)(2,1)}, bf16[1024,512]{1,0:T(8,128)(2,1)S(1)}, s32[]{:T(128)}, ...), condition=%wide.region_1.2_spmd.clone, body=%wide.region_0.1_spmd.clone.sunk | while | flops 1075314688 | bytes 45089020 | solution.py:60
  109.4 1.2 copy.21
  110.7 3.2 %collective-permute-start = (bf16[1024,512]{1,0:T(8,128)(2,1)S(1)}, bf16[1024,512]{1,0:T(8,128)(2,1)}, u32[]{:S(2)}, u32[]{:S(2)}) collective-permute-start(bf16[1024,512]{1,0:T(8,128)(2,1)S(1)} %copy.21), channel_id=1, source_target_pairs={{1,0},{2,1},{3,2},{4,3},{5,4},{6,5},{7,6},{0,7},{9,8},{10,9},{11,1... | collective-permute-start | bytes 3145736 | tf_op jit(solution)/shard_map/while/body/eval_jaxpr/ppermute | solution.py:10
  113.8 0.1 copy.22
  113.9 0.4 collective-permute-start.2
  114.3 11.8 %collective-permute-done = bf16[1024,512]{1,0:T(8,128)(2,1)} collective-permute-done((bf16[1024,512]{1,0:T(8,128)(2,1)S(1)}, bf16[1024,512]{1,0:T(8,128)(2,1)}, u32[]{:S(2)}, u32[]{:S(2)}) %collective-permute-start) | collective-permute-done | bytes 1048608 | tf_op jit(solution)/shard_map/while/body/eval_jaxpr/ppermute | solution.py:10
  126.1 3.8 %collective-permute-start.1 = (bf16[1024,512]{1,0:T(8,128)(2,1)}, bf16[1024,512]{1,0:T(8,128)(2,1)}, u32[]{:S(2)}, u32[]{:S(2)}) collective-permute-start(bf16[1024,512]{1,0:T(8,128)(2,1)} %collective-permute-done), channel_id=1, source_target_pairs={{1,0},{2,1},{3,2},{4,3},{5,4},{6,5},{7,6},{0,7},{9,8},{10,9},{11,1... | collective-permute-start | bytes 3145736 | tf_op jit(solution)/shard_map/while/body/eval_jaxpr/ppermute | solution.py:10
  129.9 0.7 fusion.26
  130.6 0.9 copy-done
  131.5 2.1 fusion.27
  133.6 3.5 %collective-permute-done.2 = bf16[1024,512]{1,0:T(8,128)(2,1)S(1)} collective-permute-done((bf16[1024,512]{1,0:T(8,128)(2,1)S(1)}, bf16[1024,512]{1,0:T(8,128)(2,1)S(1)}, u32[]{:S(2)}, u32[]{:S(2)}) %collective-permute-start.2) | collective-permute-done | bytes 1048608 | tf_op jit(solution)/shard_map/while/body/eval_jaxpr/ppermute | solution.py:10
  137.2 5.4 %collective-permute-done.1 = bf16[1024,512]{1,0:T(8,128)(2,1)} collective-permute-done((bf16[1024,512]{1,0:T(8,128)(2,1)}, bf16[1024,512]{1,0:T(8,128)(2,1)}, u32[]{:S(2)}, u32[]{:S(2)}) %collective-permute-start.1) | collective-permute-done | bytes 1048608 | tf_op jit(solution)/shard_map/while/body/eval_jaxpr/ppermute | solution.py:10
  142.6 1.2 copy.21
  143.8 3.7 %collective-permute-start = (bf16[1024,512]{1,0:T(8,128)(2,1)S(1)}, bf16[1024,512]{1,0:T(8,128)(2,1)}, u32[]{:S(2)}, u32[]{:S(2)}) collective-permute-start(bf16[1024,512]{1,0:T(8,128)(2,1)S(1)} %copy.21), channel_id=1, source_target_pairs={{1,0},{2,1},{3,2},{4,3},{5,4},{6,5},{7,6},{0,7},{9,8},{10,9},{11,1... | collective-permute-start | bytes 3145736 | tf_op jit(solution)/shard_map/while/body/eval_jaxpr/ppermute | solution.py:10
  147.5 0.1 copy.22
  147.6 0.4 collective-permute-start.2
  148.0 11.8 %collective-permute-done = bf16[1024,512]{1,0:T(8,128)(2,1)} collective-permute-done((bf16[1024,512]{1,0:T(8,128)(2,1)S(1)}, bf16[1024,512]{1,0:T(8,128)(2,1)}, u32[]{:S(2)}, u32[]{:S(2)}) %collective-permute-start) | collective-permute-done | bytes 1048608 | tf_op jit(solution)/shard_map/while/body/eval_jaxpr/ppermute | solution.py:10
  159.8 3.8 %collective-permute-start.1 = (bf16[1024,512]{1,0:T(8,128)(2,1)}, bf16[1024,512]{1,0:T(8,128)(2,1)}, u32[]{:S(2)}, u32[]{:S(2)}) collective-permute-start(bf16[1024,512]{1,0:T(8,128)(2,1)} %collective-permute-done), channel_id=1, source_target_pairs={{1,0},{2,1},{3,2},{4,3},{5,4},{6,5},{7,6},{0,7},{9,8},{10,9},{11,1... | collective-permute-start | bytes 3145736 | tf_op jit(solution)/shard_map/while/body/eval_jaxpr/ppermute | solution.py:10
  163.6 0.7 fusion.26
  164.4 0.9 copy-done
  165.2 2.1 fusion.27
  167.3 2.2 collective-permute-done.2
  169.5 6.8 %collective-permute-done.1 = bf16[1024,512]{1,0:T(8,128)(2,1)} collective-permute-done((bf16[1024,512]{1,0:T(8,128)(2,1)}, bf16[1024,512]{1,0:T(8,128)(2,1)}, u32[]{:S(2)}, u32[]{:S(2)}) %collective-permute-start.1) | collective-permute-done | bytes 1048608 | tf_op jit(solution)/shard_map/while/body/eval_jaxpr/ppermute | solution.py:10
  176.3 1.2 copy.21
  177.5 3.7 %collective-permute-start = (bf16[1024,512]{1,0:T(8,128)(2,1)S(1)}, bf16[1024,512]{1,0:T(8,128)(2,1)}, u32[]{:S(2)}, u32[]{:S(2)}) collective-permute-start(bf16[1024,512]{1,0:T(8,128)(2,1)S(1)} %copy.21), channel_id=1, source_target_pairs={{1,0},{2,1},{3,2},{4,3},{5,4},{6,5},{7,6},{0,7},{9,8},{10,9},{11,1... | collective-permute-start | bytes 3145736 | tf_op jit(solution)/shard_map/while/body/eval_jaxpr/ppermute | solution.py:10
  181.2 0.1 copy.22
  181.3 0.4 collective-permute-start.2
  181.7 11.8 %collective-permute-done = bf16[1024,512]{1,0:T(8,128)(2,1)} collective-permute-done((bf16[1024,512]{1,0:T(8,128)(2,1)S(1)}, bf16[1024,512]{1,0:T(8,128)(2,1)}, u32[]{:S(2)}, u32[]{:S(2)}) %collective-permute-start) | collective-permute-done | bytes 1048608 | tf_op jit(solution)/shard_map/while/body/eval_jaxpr/ppermute | solution.py:10
  193.5 3.8 %collective-permute-start.1 = (bf16[1024,512]{1,0:T(8,128)(2,1)}, bf16[1024,512]{1,0:T(8,128)(2,1)}, u32[]{:S(2)}, u32[]{:S(2)}) collective-permute-start(bf16[1024,512]{1,0:T(8,128)(2,1)} %collective-permute-done), channel_id=1, source_target_pairs={{1,0},{2,1},{3,2},{4,3},{5,4},{6,5},{7,6},{0,7},{9,8},{10,9},{11,1... | collective-permute-start | bytes 3145736 | tf_op jit(solution)/shard_map/while/body/eval_jaxpr/ppermute | solution.py:10
  197.3 0.7 fusion.26
  198.0 0.9 copy-done
  198.9 2.1 fusion.27
  201.0 2.2 collective-permute-done.2
  203.2 6.8 %collective-permute-done.1 = bf16[1024,512]{1,0:T(8,128)(2,1)} collective-permute-done((bf16[1024,512]{1,0:T(8,128)(2,1)}, bf16[1024,512]{1,0:T(8,128)(2,1)}, u32[]{:S(2)}, u32[]{:S(2)}) %collective-permute-start.1) | collective-permute-done | bytes 1048608 | tf_op jit(solution)/shard_map/while/body/eval_jaxpr/ppermute | solution.py:10
  210.0 3.7 %collective-permute-start.9 = (bf16[1024,512]{1,0:T(8,128)(2,1)}, bf16[1024,512]{1,0:T(8,128)(2,1)S(1)}, u32[]{:S(2)}, u32[]{:S(2)}) collective-permute-start(bf16[1024,512]{1,0:T(8,128)(2,1)} %get-tuple-element.30), channel_id=1, source_target_pairs={{1,0},{2,1},{3,2},{4,3},{5,4},{6,5},{7,6},{0,7},{9,8},{10,9},{11,1... | collective-permute-start | bytes 3145736 | tf_op jit(solution)/shard_map/ppermute | solution.py:10
  213.7 0.1 copy.8
  213.8 1.9 fusion.10
  215.7 10.6 %collective-permute-done.9 = bf16[1024,512]{1,0:T(8,128)(2,1)S(1)} collective-permute-done((bf16[1024,512]{1,0:T(8,128)(2,1)}, bf16[1024,512]{1,0:T(8,128)(2,1)S(1)}, u32[]{:S(2)}, u32[]{:S(2)}) %collective-permute-start.9) | collective-permute-done | bytes 1048608 | tf_op jit(solution)/shard_map/ppermute | solution.py:10
  226.4 1.2 broadcast_in_dim.27
  227.6 1.7 fusion.4
  (26 shorter events, 0.2 us)
Async XLA Ops:
  0.0 3.9 %copy-start.3 = (bf16[1024,512]{1,0:T(8,128)(2,1)S(1)}, bf16[1024,512]{1,0:T(8,128)(2,1)}, u32[]{:S(2)}) copy-start(bf16[1024,512]{1,0:T(8,128)(2,1)} %param.8) | copy-start | bytes 3145732
  0.9 7.1 %copy-start.5 = (s32[8,4]{0,1:T(4,128)S(1)}, s32[8,4]{0,1:T(4,128)}, u32[]{:S(2)}) copy-start(s32[8,4]{0,1:T(4,128)} %param.9) | copy-start | bytes 388
  3.9 7.2 %copy-start.4 = (bf16[1024,512]{1,0:T(8,128)(2,1)S(1)}, bf16[1024,512]{1,0:T(8,128)(2,1)}, u32[]{:S(2)}) copy-start(bf16[1024,512]{1,0:T(8,128)(2,1)} %param.7) | copy-start | bytes 3145732
  4.1 26.4 %collective-permute-start.6 = (bf16[1024,512]{1,0:T(8,128)(2,1)S(1)}, bf16[1024,512]{1,0:T(8,128)(2,1)}, u32[]{:S(2)}, u32[]{:S(2)}) collective-permute-start(bf16[1024,512]{1,0:T(8,128)(2,1)S(1)} %bitcast_multiply_fusion.1), channel_id=1, source_target_pairs={{8,0},{16,8},{24,16},{0,24},{9,1},{17,9},{25,17},{1,25},{10,2},{18... | collective-permute-start | bytes 3145736 | tf_op jit(solution)/shard_map/ppermute | solution.py:10
  11.3 21.0 %collective-permute-start.3 = (bf16[1024,512]{1,0:T(8,128)(2,1)S(1)}, bf16[1024,512]{1,0:T(8,128)(2,1)}, u32[]{:S(2)}, u32[]{:S(2)}) collective-permute-start(bf16[1024,512]{1,0:T(8,128)(2,1)S(1)} %bitcast_multiply_fusion.2), channel_id=1, source_target_pairs={{1,0},{2,1},{3,2},{4,3},{5,4},{6,5},{7,6},{0,7},{9,8},{10,9},{11,1... | collective-permute-start | bytes 3145736 | tf_op jit(solution)/shard_map/ppermute | solution.py:10
  30.6 24.4 %collective-permute-start.7 = (bf16[1024,512]{1,0:T(8,128)(2,1)S(1)}, bf16[1024,512]{1,0:T(8,128)(2,1)}, u32[]{:S(2)}, u32[]{:S(2)}) collective-permute-start(bf16[1024,512]{1,0:T(8,128)(2,1)S(1)} %broadcast_select_fusion), channel_id=1, source_target_pairs={{16,0},{24,8},{0,16},{8,24},{17,1},{25,9},{1,17},{9,25},{18,2},{26... | collective-permute-start | bytes 3145736 | tf_op jit(solution)/shard_map/ppermute | solution.py:10
  32.4 26.1 %collective-permute-start.4 = (bf16[1024,512]{1,0:T(8,128)(2,1)S(1)}, bf16[1024,512]{1,0:T(8,128)(2,1)}, u32[]{:S(2)}, u32[]{:S(2)}) collective-permute-start(bf16[1024,512]{1,0:T(8,128)(2,1)S(1)} %broadcast_select_fusion.2), channel_id=1, source_target_pairs={{2,0},{3,1},{4,2},{5,3},{6,4},{7,5},{0,6},{1,7},{10,8},{11,9},{12,... | collective-permute-start | bytes 3145736 | tf_op jit(solution)/shard_map/ppermute | solution.py:10
  55.1 24.0 %collective-permute-start.8 = (bf16[1024,512]{1,0:T(8,128)(2,1)S(1)}, bf16[1024,512]{1,0:T(8,128)(2,1)}, u32[]{:S(2)}, u32[]{:S(2)}) collective-permute-start(bf16[1024,512]{1,0:T(8,128)(2,1)S(1)} %broadcast_select_fusion.1), channel_id=1, source_target_pairs={{8,0},{16,8},{24,16},{0,24},{9,1},{17,9},{25,17},{1,25},{10,2},{18... | collective-permute-start | bytes 3145736 | tf_op jit(solution)/shard_map/ppermute | solution.py:10
  59.6 47.4 %collective-permute-start.5 = (bf16[1024,512]{1,0:T(8,128)(2,1)}, bf16[1024,512]{1,0:T(8,128)(2,1)S(1)}, u32[]{:S(2)}, u32[]{:S(2)}) collective-permute-start(bf16[1024,512]{1,0:T(8,128)(2,1)} %broadcast_select_fusion.3), channel_id=1, source_target_pairs={{4,0},{5,1},{6,2},{7,3},{0,4},{1,5},{2,6},{3,7},{12,8},{13,9},{14,... | collective-permute-start | bytes 3145736 | tf_op jit(solution)/shard_map/ppermute | solution.py:10
  109.4 104.3 %copy-start.6 = (s32[8,4]{0,1:T(4,128)S(1)}, s32[8,4]{0,1:T(4,128)}, u32[]{:S(2)}) copy-start(s32[8,4]{0,1:T(4,128)} %param.11) | copy-start | bytes 388
  110.7 15.5 %collective-permute-start = (bf16[1024,512]{1,0:T(8,128)(2,1)S(1)}, bf16[1024,512]{1,0:T(8,128)(2,1)}, u32[]{:S(2)}, u32[]{:S(2)}) collective-permute-start(bf16[1024,512]{1,0:T(8,128)(2,1)S(1)} %copy.21), channel_id=1, source_target_pairs={{1,0},{2,1},{3,2},{4,3},{5,4},{6,5},{7,6},{0,7},{9,8},{10,9},{11,1... | collective-permute-start | bytes 3145736 | tf_op jit(solution)/shard_map/while/body/eval_jaxpr/ppermute | solution.py:10
  113.9 23.3 %collective-permute-start.2 = (bf16[1024,512]{1,0:T(8,128)(2,1)S(1)}, bf16[1024,512]{1,0:T(8,128)(2,1)S(1)}, u32[]{:S(2)}, u32[]{:S(2)}) collective-permute-start(bf16[1024,512]{1,0:T(8,128)(2,1)S(1)} %copy.22), channel_id=1, source_target_pairs={{8,0},{16,8},{24,16},{0,24},{9,1},{17,9},{25,17},{1,25},{10,2},{18... | collective-permute-start | bytes 3145736 | tf_op jit(solution)/shard_map/while/body/eval_jaxpr/ppermute | solution.py:10
  126.1 16.4 %collective-permute-start.1 = (bf16[1024,512]{1,0:T(8,128)(2,1)}, bf16[1024,512]{1,0:T(8,128)(2,1)}, u32[]{:S(2)}, u32[]{:S(2)}) collective-permute-start(bf16[1024,512]{1,0:T(8,128)(2,1)} %collective-permute-done), channel_id=1, source_target_pairs={{1,0},{2,1},{3,2},{4,3},{5,4},{6,5},{7,6},{0,7},{9,8},{10,9},{11,1... | collective-permute-start | bytes 3145736 | tf_op jit(solution)/shard_map/while/body/eval_jaxpr/ppermute | solution.py:10
  129.9 1.6 copy-start
  133.6 8.9 %copy-start.1 = (f32[1024,512]{1,0:T(8,128)}, f32[1024,512]{1,0:T(8,128)S(1)}, u32[]{:S(2)}) copy-start(f32[1024,512]{1,0:T(8,128)S(1)} %fusion.27) | copy-start | bytes 6291460 | tf_op jit(solution)/shard_map/while
  143.8 16.0 %collective-permute-start = (bf16[1024,512]{1,0:T(8,128)(2,1)S(1)}, bf16[1024,512]{1,0:T(8,128)(2,1)}, u32[]{:S(2)}, u32[]{:S(2)}) collective-permute-start(bf16[1024,512]{1,0:T(8,128)(2,1)S(1)} %copy.21), channel_id=1, source_target_pairs={{1,0},{2,1},{3,2},{4,3},{5,4},{6,5},{7,6},{0,7},{9,8},{10,9},{11,1... | collective-permute-start | bytes 3145736 | tf_op jit(solution)/shard_map/while/body/eval_jaxpr/ppermute | solution.py:10
  147.6 21.9 %collective-permute-start.2 = (bf16[1024,512]{1,0:T(8,128)(2,1)S(1)}, bf16[1024,512]{1,0:T(8,128)(2,1)S(1)}, u32[]{:S(2)}, u32[]{:S(2)}) collective-permute-start(bf16[1024,512]{1,0:T(8,128)(2,1)S(1)} %copy.22), channel_id=1, source_target_pairs={{8,0},{16,8},{24,16},{0,24},{9,1},{17,9},{25,17},{1,25},{10,2},{18... | collective-permute-start | bytes 3145736 | tf_op jit(solution)/shard_map/while/body/eval_jaxpr/ppermute | solution.py:10
  159.8 16.4 %collective-permute-start.1 = (bf16[1024,512]{1,0:T(8,128)(2,1)}, bf16[1024,512]{1,0:T(8,128)(2,1)}, u32[]{:S(2)}, u32[]{:S(2)}) collective-permute-start(bf16[1024,512]{1,0:T(8,128)(2,1)} %collective-permute-done), channel_id=1, source_target_pairs={{1,0},{2,1},{3,2},{4,3},{5,4},{6,5},{7,6},{0,7},{9,8},{10,9},{11,1... | collective-permute-start | bytes 3145736 | tf_op jit(solution)/shard_map/while/body/eval_jaxpr/ppermute | solution.py:10
  163.6 1.6 copy-start
  167.3 8.9 %copy-start.1 = (f32[1024,512]{1,0:T(8,128)}, f32[1024,512]{1,0:T(8,128)S(1)}, u32[]{:S(2)}) copy-start(f32[1024,512]{1,0:T(8,128)S(1)} %fusion.27) | copy-start | bytes 6291460 | tf_op jit(solution)/shard_map/while
  177.5 16.0 %collective-permute-start = (bf16[1024,512]{1,0:T(8,128)(2,1)S(1)}, bf16[1024,512]{1,0:T(8,128)(2,1)}, u32[]{:S(2)}, u32[]{:S(2)}) collective-permute-start(bf16[1024,512]{1,0:T(8,128)(2,1)S(1)} %copy.21), channel_id=1, source_target_pairs={{1,0},{2,1},{3,2},{4,3},{5,4},{6,5},{7,6},{0,7},{9,8},{10,9},{11,1... | collective-permute-start | bytes 3145736 | tf_op jit(solution)/shard_map/while/body/eval_jaxpr/ppermute | solution.py:10
  181.3 21.9 %collective-permute-start.2 = (bf16[1024,512]{1,0:T(8,128)(2,1)S(1)}, bf16[1024,512]{1,0:T(8,128)(2,1)S(1)}, u32[]{:S(2)}, u32[]{:S(2)}) collective-permute-start(bf16[1024,512]{1,0:T(8,128)(2,1)S(1)} %copy.22), channel_id=1, source_target_pairs={{8,0},{16,8},{24,16},{0,24},{9,1},{17,9},{25,17},{1,25},{10,2},{18... | collective-permute-start | bytes 3145736 | tf_op jit(solution)/shard_map/while/body/eval_jaxpr/ppermute | solution.py:10
  193.5 16.4 %collective-permute-start.1 = (bf16[1024,512]{1,0:T(8,128)(2,1)}, bf16[1024,512]{1,0:T(8,128)(2,1)}, u32[]{:S(2)}, u32[]{:S(2)}) collective-permute-start(bf16[1024,512]{1,0:T(8,128)(2,1)} %collective-permute-done), channel_id=1, source_target_pairs={{1,0},{2,1},{3,2},{4,3},{5,4},{6,5},{7,6},{0,7},{9,8},{10,9},{11,1... | collective-permute-start | bytes 3145736 | tf_op jit(solution)/shard_map/while/body/eval_jaxpr/ppermute | solution.py:10
  197.3 1.6 copy-start
  201.0 8.9 %copy-start.1 = (f32[1024,512]{1,0:T(8,128)}, f32[1024,512]{1,0:T(8,128)S(1)}, u32[]{:S(2)}) copy-start(f32[1024,512]{1,0:T(8,128)S(1)} %fusion.27) | copy-start | bytes 6291460 | tf_op jit(solution)/shard_map/while
  210.0 16.3 %collective-permute-start.9 = (bf16[1024,512]{1,0:T(8,128)(2,1)}, bf16[1024,512]{1,0:T(8,128)(2,1)S(1)}, u32[]{:S(2)}, u32[]{:S(2)}) collective-permute-start(bf16[1024,512]{1,0:T(8,128)(2,1)} %get-tuple-element.30), channel_id=1, source_target_pairs={{1,0},{2,1},{3,2},{4,3},{5,4},{6,5},{7,6},{0,7},{9,8},{10,9},{11,1... | collective-permute-start | bytes 3145736 | tf_op jit(solution)/shard_map/ppermute | solution.py:10
  215.7 11.9 %copy-start.2 = (f32[1024,512]{1,0:T(8,128)S(1)}, f32[1024,512]{1,0:T(8,128)}, u32[]{:S(2)}) copy-start(f32[1024,512]{1,0:T(8,128)} %get-tuple-element.29) | copy-start | bytes 6291460
where the time goes:
time: 230 us; the launch traced here: 229 us
  waiting for transfers between devices  150 us (65%)
  starting transfers between devices  47.3 us (21%)
  local copies, waits for them, and re-layouts  14.1 us (6%)
  matrix products  12 us (5%)
  other arithmetic  6.16 us (3%)
    ppermute x16, waiting for transfers between devices, from_behind(): return lax.ppermute(block, axis, route)  150 us
    ppermute x16, starting transfers between devices, from_behind(): return lax.ppermute(block, axis, route)  47.3 us
    dot_general x8, matrix products, run_group(): jnp.dot(left_now, panel_now, preferred_element_type=jnp.float32)  12 us
    broadcast_in_dim x3, local copies, waits for them, and re-layouts, expand_blocks(): jnp.repeat(jnp.repeat(pattern_int, block_size, axis=0), block_size, axis=1)  7.12 us
    while x18, local copies, waits for them, and re-layouts  6.57 us
  transfers between devices with their start and end apart: 16, of which 15 were waited for; matrix products, arithmetic and copies ran while one was open for 7% of the time, Pallas kernels for 0%

commit v1 on v0

v1 whole, which is shorter than its diff:
```python
import jax
import jax.numpy as jnp
from jax import lax
from jax.experimental import pallas as pl
from jax.experimental.pallas import tpu as pltpu
from jax.sharding import PartitionSpec as P


def masked_chunks(blocks, pattern, chunks):
    brows, bcols = pattern.shape
    rows, cols = blocks.shape
    size = rows // brows
    per = brows // chunks

    def body(pat_ref, x_ref, o_ref):
        g = pl.program_id(0)
        for p in range(per):
            for q in range(bcols):
                at = (slice(p * size, (p + 1) * size), slice(q * size, (q + 1) * size))
                o_ref[(0, *at)] = jnp.where(pat_ref[g * per + p, q] != 0, x_ref[at], jnp.zeros((), x_ref.dtype))

    return pl.pallas_call(
        body,
        grid=(chunks,),
        in_specs=[pl.BlockSpec(memory_space=pltpu.SMEM), pl.BlockSpec((rows // chunks, cols), lambda g: (g, 0))],
        out_specs=pl.BlockSpec((1, rows // chunks, cols), lambda g: (g, 0, 0)),
        out_shape=jax.ShapeDtypeStruct((chunks, rows // chunks, cols), blocks.dtype),
    )(pattern, blocks)


def on_grid(left, right, a_pattern, b_pattern):
    row, col = lax.axis_index("row"), lax.axis_index("col")
    z = col // 2
    edge = (z == 0) | (z == 3)
    both = lambda pairs: [(2 * s + c, 2 * d + c) for s, d in pairs for c in (0, 1)]
    swap = both([(0, 1), (1, 0), (2, 3), (3, 2)])
    mid = both([(1, 2), (2, 1)])
    out = both([(1, 0), (2, 3)])
    cross = [(i, i ^ 1) for i in range(8)]
    xs = [(i, i ^ 1) for i in range(4)]
    ys = [(i, i ^ 2) for i in range(4)]
    over = lambda v, route: lax.ppermute(v, "col", route)

    a = masked_chunks(left, a_pattern, 2)
    a = [a[0], a[1]]
    s1 = [over(v, swap) for v in a]
    m1 = [over(v, mid) for v in a]
    b = masked_chunks(right, b_pattern, 2)
    bx = lax.ppermute(b, "row", xs)
    by = lax.ppermute(b, "row", ys)
    bd = [lax.ppermute(bx[0], "row", ys), lax.ppermute(by[1], "row", xs)]
    o2 = [over(v, out) for v in m1]
    m2 = [over(v, mid) for v in s1]
    o3 = [over(v, out) for v in m2]
    s2 = [jnp.where(edge, o, m) for o, m in zip(o2, m1)]
    s3 = [jnp.where(edge, o, m) for o, m in zip(o3, m2)]
    z1 = z ^ 1
    z2 = jnp.where(edge, jnp.where(z == 0, 2, 1), 3 - z)
    z3 = jnp.where(edge, 3 - z, 3 - (z ^ 1))
    stack = jnp.stack([b, bx, by, jnp.stack(bd)])
    total = [0.0, 0.0]
    core = col % 2
    for slot, at in ((a, z), (s1, z1), (s2, z2), (s3, z3)):
        panel = lax.dynamic_index_in_dim(stack, at ^ row, 0, keepdims=False)
        mine = lax.dynamic_index_in_dim(panel, core, 0, keepdims=False)
        other = lax.dynamic_index_in_dim(panel, 1 - core, 0, keepdims=False)
        for h in (0, 1):
            total[h] += jnp.dot(slot[h], mine, preferred_element_type=jnp.float32)
            total[h] += jnp.dot(over(slot[h], cross), other, preferred_element_type=jnp.float32)
    return jnp.concatenate(total, axis=0)


def on_any(left, right, a_pattern, b_pattern):
    left = masked_chunks(left, a_pattern, 1)[0]
    right = masked_chunks(right, b_pattern, 1)[0]
    left = lax.all_gather(left, "col", axis=1, tiled=True)
    right = lax.all_gather(right, "row", axis=0, tiled=True)
    return jnp.dot(left, right, preferred_element_type=jnp.float32)


def on_device(left, right, a_pattern, b_pattern, keep_mask):
    tuned = (lax.axis_size("row"), lax.axis_size("col")) == (4, 8)
    total = (on_grid if tuned else on_any)(left, right, a_pattern, b_pattern)
    size = left.shape[0] // a_pattern.shape[0]
    kept = jnp.repeat(jnp.repeat(keep_mask, size, axis=0), size, axis=1).astype(jnp.float32)
    return (total * kept).astype(jnp.bfloat16)


def solution(mesh):
    placed = (P("row", "col"),) * 5
    return jax.shard_map(on_device, mesh=mesh, in_specs=placed, out_specs=P("row", "col"), check_vma=False)
```

time: 230 us -> 129 us (0.56)
  waiting for transfers between devices: 150 us -> 64.2 us
  local copies, waits for them, and re-layouts: 14.1 us -> 7.01 us
  starting transfers between devices: 47.3 us -> 40.8 us
  Pallas kernels: 0 us -> 4.31 us
  matrix products: 12 us -> 8.18 us
  other arithmetic: 6.16 us -> 3.27 us
    ppermute x16 -> x22, waiting for transfers between devices: 150 us -> 64.2 us  [the longest x18 64.2 us: on_grid(): over = lambda v, route: lax.ppermute(v, 'col', route)]
    while x18 -> x0, local copies, waits for them, and re-layouts: 6.57 us -> none
    ppermute x16 -> x22, starting transfers between devices: 47.3 us -> 40.8 us  [the longest x18 35.3 us: on_grid(): over = lambda v, route: lax.ppermute(v, 'col', route)]
    broadcast_in_dim x6 -> x2, local copies, waits for them, and re-layouts: 7.23 us -> 1.27 us  [the longest x1 1.23 us: on_device(): jnp.repeat(jnp.repeat(keep_mask, size, axis=0), size, axis=1)]
    pallas_call x0 -> x2, Pallas kernels: none -> 4.31 us  [masked_chunks(): pl.pallas_call(body, grid=(chunks,), in_specs=[pl.BlockSpec(memory_space=...]
    dot_general x8 -> x16, matrix products: 12 us -> 8.18 us  [the longest x8 4.58 us: on_grid(): total[h] += jnp.dot(slot[h], mine, preferred_element_type=jnp.float32)]
    unnamed x10 -> x8, local copies, waits for them, and re-layouts: 0.02 us -> 3.35 us
    select_n x5 -> x4, other arithmetic: 3.77 us -> 1.27 us  [the longest x2 1.16 us: on_grid(): s2 = [jnp.where(edge, o, m) for o, m in zip(o2, m1)]]
  transfers between devices with their start and end apart: 16 -> 22, of which waited for: 15 -> 4; matrix products, arithmetic and copies ran while one was open for 7% -> 10% of each run, Pallas kernels for 0% -> 2%
where the time goes in v1:
time: 129 us; the launch traced here: 128 us
  waiting for transfers between devices  64.2 us (50%)
  starting transfers between devices  40.8 us (32%)
  matrix products  8.18 us (6%)
  local copies, waits for them, and re-layouts  7.01 us (5%)
  Pallas kernels  4.31 us (3%)
  other arithmetic  3.27 us (3%)
    ppermute x18, waiting for transfers between devices, on_grid(): over = lambda v, route: lax.ppermute(v, 'col', route)  64.2 us
    ppermute x18, starting transfers between devices, on_grid(): over = lambda v, route: lax.ppermute(v, 'col', route)  35.3 us
    dot_general x8, matrix products, on_grid(): total[h] += jnp.dot(slot[h], mine, preferred_element_type=jnp.float32)  4.58 us
    pallas_call x2, Pallas kernels, masked_chunks(): pl.pallas_call(body, grid=(chunks,), in_specs=[pl.BlockSpec(memory_space=...  4.31 us
    dot_general x8, matrix products, on_grid(): jnp.dot(over(slot[h], cross), other, preferred_element_type=jnp.float32)  3.6 us
    unnamed x8, local copies, waits for them, and re-layouts  3.35 us
    ppermute x1, starting transfers between devices, on_grid(): bx = lax.ppermute(b, 'row', xs)  2.94 us
  transfers between devices with their start and end apart: 22, of which 4 were waited for; matrix products, arithmetic and copies ran while one was open for 10% of the time, Pallas kernels for 2%

profile of v1, /device:TPU:0, one launch (start us, length us, event | category | flops | bytes accessed | tf_op | source)
XLA Modules:
  0.0 128.1 jit_solution(10477821661495885351)
XLA Ops:
  0.0 1.4 %copy.7.pat_ref = s32[8,4]{1,0:T(8,128)} copy(s32[8,4]{0,1:T(4,128)} %param.8) | data formatting | bytes 256 | tf_op args[3]
  1.4 2.2 %shard_map.56 = bf16[2,512,512]{2,1,0:T(8,128)(2,1)} custom-call(s32[8,4]{1,0:T(8,128)} %copy.7.pat_ref, bf16[1024,512]{1,0:T(8,128)(2,1)} %x_ref.3), custom_call_target="tpu_custom_call" | custom-call | tf_op jit(solution)/shard_map/pallas_call | solution.py:22
  3.5 2.9 %collective-permute-start = (bf16[2,512,512]{2,1,0:T(8,128)(2,1)}, bf16[2,512,512]{2,1,0:T(8,128)(2,1)S(1)}, u32[]{:S(2)}, u32[]{:S(2)}) collective-permute-start(bf16[2,512,512]{2,1,0:T(8,128)(2,1)} %shard_map.56), channel_id=1, source_target_pairs={{0,8},{8,0},{16,24},{24,16},{1,9},{9,1},{17,25},{25,17},{2,10},{10... | collective-permute-start | bytes 3145736 | tf_op jit(solution)/shard_map/ppermute | solution.py:49
  6.5 1.5 %collective-permute-start.1 = (bf16[2,512,512]{2,1,0:T(8,128)(2,1)}, bf16[2,512,512]{2,1,0:T(8,128)(2,1)S(1)}, u32[]{:S(2)}, u32[]{:S(2)}) collective-permute-start(bf16[2,512,512]{2,1,0:T(8,128)(2,1)} %shard_map.56), channel_id=1, source_target_pairs={{0,16},{8,24},{16,0},{24,8},{1,17},{9,25},{17,1},{25,9},{2,18},{10... | collective-permute-start | bytes 3145736 | tf_op jit(solution)/shard_map/ppermute | solution.py:50
  8.0 1.3 %copy.6.pat_ref = s32[8,4]{1,0:T(8,128)} copy(s32[8,4]{0,1:T(4,128)} %param.7) | data formatting | bytes 256 | tf_op args[2]
  9.3 2.1 %shard_map.55 = bf16[2,512,512]{2,1,0:T(8,128)(2,1)} custom-call(s32[8,4]{1,0:T(8,128)} %copy.6.pat_ref, bf16[1024,512]{1,0:T(8,128)(2,1)} %x_ref.2), custom_call_target="tpu_custom_call" | custom-call | tf_op jit(solution)/shard_map/pallas_call | solution.py:22
  11.5 2.2 %slice_bitcast_fusion.3 = (bf16[512,512]{1,0:T(8,128)(2,1)}, bf16[512,512]{1,0:T(8,128)(2,1)}) fusion(bf16[2,512,512]{2,1,0:T(8,128)(2,1)} %shard_map.55), kind=kLoop, calls=%fused_computation.19 | loop fusion | bytes 2097152 | tf_op jit(solution)/shard_map/squeeze | solution.py:45
  13.7 1.6 %collective-permute-start.7 = (bf16[512,512]{1,0:T(8,128)(2,1)}, bf16[512,512]{1,0:T(8,128)(2,1)}, u32[]{:S(2)}, u32[]{:S(2)}) collective-permute-start(bf16[512,512]{1,0:T(8,128)(2,1)} %get-tuple-element.5), channel_id=1, source_target_pairs={{2,4},{3,5},{4,2},{5,3},{10,12},{11,13},{12,10},{13,11},{18,20},{1... | collective-permute-start | bytes 1572872 | tf_op jit(solution)/shard_map/ppermute | solution.py:42
  15.3 1.5 %collective-permute-start.16 = (bf16[512,512]{1,0:T(8,128)(2,1)}, bf16[512,512]{1,0:T(8,128)(2,1)}, u32[]{:S(2)}, u32[]{:S(2)}) collective-permute-start(bf16[512,512]{1,0:T(8,128)(2,1)} %get-tuple-element.6), channel_id=1, source_target_pairs={{2,4},{3,5},{4,2},{5,3},{10,12},{11,13},{12,10},{13,11},{18,20},{1... | collective-permute-start | bytes 1572872 | tf_op jit(solution)/shard_map/ppermute | solution.py:42
  16.8 0.0 collective-permute-done.7
  16.8 1.3 %collective-permute-start.8 = (bf16[512,512]{1,0:T(8,128)(2,1)}, bf16[512,512]{1,0:T(8,128)(2,1)}, u32[]{:S(2)}, u32[]{:S(2)}) collective-permute-start(bf16[512,512]{1,0:T(8,128)(2,1)} %collective-permute-done.7), channel_id=1, source_target_pairs={{2,0},{3,1},{4,6},{5,7},{10,8},{11,9},{12,14},{13,15},{18,16},{19,... | collective-permute-start | bytes 1572872 | tf_op jit(solution)/shard_map/ppermute | solution.py:42
  18.0 16.5 %collective-permute-start.5 = (bf16[512,512]{1,0:T(8,128)(2,1)}, bf16[512,512]{1,0:T(8,128)(2,1)}, u32[]{:S(2)}, u32[]{:S(2)}) collective-permute-start(bf16[512,512]{1,0:T(8,128)(2,1)} %get-tuple-element.5), channel_id=1, source_target_pairs={{0,2},{1,3},{2,0},{3,1},{4,6},{5,7},{6,4},{7,5},{8,10},{9,11},{10,... | collective-permute-start | bytes 1572872 | tf_op jit(solution)/shard_map/ppermute | solution.py:42
  34.6 0.1 copy.8
  34.7 7.3 %collective-permute-start.14 = (bf16[512,512]{1,0:T(8,128)(2,1)}, bf16[512,512]{1,0:T(8,128)(2,1)S(1)}, u32[]{:S(2)}, u32[]{:S(2)}) collective-permute-start(bf16[512,512]{1,0:T(8,128)(2,1)} %get-tuple-element.6), channel_id=1, source_target_pairs={{0,2},{1,3},{2,0},{3,1},{4,6},{5,7},{6,4},{7,5},{8,10},{9,11},{10,... | collective-permute-start | bytes 1572872 | tf_op jit(solution)/shard_map/ppermute | solution.py:42
  42.0 0.0 collective-permute-done
  42.0 1.3 %collective-permute-start.17 = (bf16[512,512]{1,0:T(8,128)(2,1)}, bf16[512,512]{1,0:T(8,128)(2,1)S(1)}, u32[]{:S(2)}, u32[]{:S(2)}) collective-permute-start(bf16[512,512]{1,0:T(8,128)(2,1)} %collective-permute-done.16), channel_id=1, source_target_pairs={{2,0},{3,1},{4,6},{5,7},{10,8},{11,9},{12,14},{13,15},{18,16},{19,... | collective-permute-start | bytes 1572872 | tf_op jit(solution)/shard_map/ppermute | solution.py:42
  43.3 0.6 collective-permute-start.2
  43.9 3.0 %collective-permute-done.8 = bf16[512,512]{1,0:T(8,128)(2,1)} collective-permute-done((bf16[512,512]{1,0:T(8,128)(2,1)}, bf16[512,512]{1,0:T(8,128)(2,1)}, u32[]{:S(2)}, u32[]{:S(2)}) %collective-permute-start.8) | collective-permute-done | bytes 524320 | tf_op jit(solution)/shard_map/ppermute | solution.py:42
  46.9 0.5 collective-permute-start.3
  47.4 1.1 broadcast_select_fusion.3
  48.6 27.8 %collective-permute-done.17 = bf16[512,512]{1,0:T(8,128)(2,1)S(1)} collective-permute-done((bf16[512,512]{1,0:T(8,128)(2,1)}, bf16[512,512]{1,0:T(8,128)(2,1)S(1)}, u32[]{:S(2)}, u32[]{:S(2)}) %collective-permute-start.17) | collective-permute-done | bytes 524320 | tf_op jit(solution)/shard_map/ppermute | solution.py:42
  76.4 0.0 collective-permute-start.4
  76.4 0.1 broadcast_select_fusion.1
  76.4 0.0 collective-permute-done.5
  76.4 0.6 collective-permute-start.13
  77.0 0.7 collective-permute-start.10
  77.7 0.0 collective-permute-done.2
  77.7 0.7 collective-permute-start.19
  78.4 0.0 collective-permute-done.3
  78.4 0.1 collective-permute-start.9
  78.5 0.1 maximum_bitcast_fusion
  78.6 0.0 copy-start
  78.6 0.6 pad_maximum_fusion
  79.2 0.6 copy-done
  79.9 0.4 fusion.31
  80.3 0.4 fusion.29
  80.7 0.4 fusion.19
  81.2 0.0 collective-permute-done.4
  81.2 0.5 collective-permute-start.6
  81.7 1.3 %collective-permute-start.11 = (bf16[512,512]{1,0:T(8,128)(2,1)S(1)}, bf16[512,512]{1,0:T(8,128)(2,1)S(1)}, u32[]{:S(2)}, u32[]{:S(2)}) collective-permute-start(bf16[512,512]{1,0:T(8,128)(2,1)S(1)} %collective-permute-done.10), channel_id=1, source_target_pairs={{2,0},{3,1},{4,6},{5,7},{10,8},{11,9},{12,14},{13,15},{18,16},{19,... | collective-permute-start | bytes 1572872 | tf_op jit(solution)/shard_map/ppermute | solution.py:42
  83.0 0.4 fusion.27
  83.5 0.1 collective-permute-start.15
  83.6 0.0 collective-permute-done.9
  83.6 1.3 %collective-permute-start.20 = (bf16[512,512]{1,0:T(8,128)(2,1)S(1)}, bf16[512,512]{1,0:T(8,128)(2,1)S(1)}, u32[]{:S(2)}, u32[]{:S(2)}) collective-permute-start(bf16[512,512]{1,0:T(8,128)(2,1)S(1)} %collective-permute-done.19), channel_id=1, source_target_pairs={{2,0},{3,1},{4,6},{5,7},{10,8},{11,9},{12,14},{13,15},{18,16},{19,... | collective-permute-start | bytes 1572872 | tf_op jit(solution)/shard_map/ppermute | solution.py:42
  84.9 0.4 fusion.15
  85.3 20.9 %collective-permute-done.11 = bf16[512,512]{1,0:T(8,128)(2,1)S(1)} collective-permute-done((bf16[512,512]{1,0:T(8,128)(2,1)S(1)}, bf16[512,512]{1,0:T(8,128)(2,1)S(1)}, u32[]{:S(2)}, u32[]{:S(2)}) %collective-permute-start.11) | collective-permute-done | bytes 524320 | tf_op jit(solution)/shard_map/ppermute | solution.py:42
  106.2 0.0 collective-permute-start.18
  106.2 0.1 broadcast_select_fusion.2
  106.2 12.5 %collective-permute-done.20 = bf16[512,512]{1,0:T(8,128)(2,1)S(1)} collective-permute-done((bf16[512,512]{1,0:T(8,128)(2,1)S(1)}, bf16[512,512]{1,0:T(8,128)(2,1)S(1)}, u32[]{:S(2)}, u32[]{:S(2)}) %collective-permute-start.20) | collective-permute-done | bytes 524320 | tf_op jit(solution)/shard_map/ppermute | solution.py:42
  118.7 0.1 broadcast_select_fusion
  118.8 0.6 collective-permute-start.21
  119.4 0.4 fusion.25
  119.8 1.5 %convolution_add_fusion.5 = f32[512,512]{1,0:T(8,128)S(1)} fusion(bf16[512,512]{1,0:T(8,128)(2,1)} %collective-permute-done.5, f32[512,512]{1,0:T(8,128)S(1)} %fusion.31, f32[512,512]{1,0:T(8,128)S(1)} %fusion.27, bf16[4,2,512,512]{3,2,1,0:T(8,128)(2,1)S(1)} %pad_maximum_fusion, s32[]{:T(128)S(6)} %select_n.89, s32[]{:T(128)S(6)} %select_n.85), kind=kOutput, calls=%fused_computation.14 | convolution fusion | flops 268959744 | bytes 4194312 | tf_op jit(solution)/shard_map/dot_general | solution.py:68
  121.3 0.5 fusion.6
  121.8 0.4 convolution_add_fusion.2
  122.3 0.4 fusion.17
  122.7 0.4 fusion.13
  123.2 0.5 fusion.3
  123.7 0.4 fusion.9
  124.1 0.4 fusion.4
  124.6 0.4 fusion.7
  125.0 0.4 fusion.1
  125.5 1.2 broadcast_in_dim.7
  126.8 1.3 %fusion = bf16[1024,512]{1,0:T(8,128)(2,1)} fusion(f32[128,8,4,128]{3,2,1,0:T(4,128)S(1)} %bitcast.77, f32[512,512]{1,0:T(8,128)S(1)} %fusion.1, f32[512,512]{1,0:T(8,128)S(1)} %fusion.4), kind=kLoop, calls=%fused_computation.2 | loop fusion | flops 1572864 | bytes 5242880 | tf_op jit(solution)/shard_map/convert_element_type | solution.py:86
  (20 shorter events, 0.1 us)
Async XLA Ops:
  0.0 34.6 %copy-start.2 = (s32[8,4]{0,1:T(4,128)S(1)}, s32[8,4]{0,1:T(4,128)}, u32[]{:S(2)}) copy-start(s32[8,4]{0,1:T(4,128)} %param.9) | copy-start | bytes 388
  3.5 38.4 %collective-permute-start = (bf16[2,512,512]{2,1,0:T(8,128)(2,1)}, bf16[2,512,512]{2,1,0:T(8,128)(2,1)S(1)}, u32[]{:S(2)}, u32[]{:S(2)}) collective-permute-start(bf16[2,512,512]{2,1,0:T(8,128)(2,1)} %shard_map.56), channel_id=1, source_target_pairs={{0,8},{8,0},{16,24},{24,16},{1,9},{9,1},{17,25},{25,17},{2,10},{10... | collective-permute-start | bytes 3145736 | tf_op jit(solution)/shard_map/ppermute | solution.py:49
  6.5 36.8 %collective-permute-start.1 = (bf16[2,512,512]{2,1,0:T(8,128)(2,1)}, bf16[2,512,512]{2,1,0:T(8,128)(2,1)S(1)}, u32[]{:S(2)}, u32[]{:S(2)}) collective-permute-start(bf16[2,512,512]{2,1,0:T(8,128)(2,1)} %shard_map.56), channel_id=1, source_target_pairs={{0,16},{8,24},{16,0},{24,8},{1,17},{9,25},{17,1},{25,9},{2,18},{10... | collective-permute-start | bytes 3145736 | tf_op jit(solution)/shard_map/ppermute | solution.py:50
  13.7 64.9 %copy-start.1 = (bf16[2,512,512]{2,1,0:T(8,128)(2,1)S(1)}, bf16[2,512,512]{2,1,0:T(8,128)(2,1)}, u32[]{:S(2)}) copy-start(bf16[2,512,512]{2,1,0:T(8,128)(2,1)} %shard_map.56) | copy-start | bytes 3145732
  13.7 3.0 %collective-permute-start.7 = (bf16[512,512]{1,0:T(8,128)(2,1)}, bf16[512,512]{1,0:T(8,128)(2,1)}, u32[]{:S(2)}, u32[]{:S(2)}) collective-permute-start(bf16[512,512]{1,0:T(8,128)(2,1)} %get-tuple-element.5), channel_id=1, source_target_pairs={{2,4},{3,5},{4,2},{5,3},{10,12},{11,13},{12,10},{13,11},{18,20},{1... | collective-permute-start | bytes 1572872 | tf_op jit(solution)/shard_map/ppermute | solution.py:42
  15.3 19.4 %collective-permute-start.16 = (bf16[512,512]{1,0:T(8,128)(2,1)}, bf16[512,512]{1,0:T(8,128)(2,1)}, u32[]{:S(2)}, u32[]{:S(2)}) collective-permute-start(bf16[512,512]{1,0:T(8,128)(2,1)} %get-tuple-element.6), channel_id=1, source_target_pairs={{2,4},{3,5},{4,2},{5,3},{10,12},{11,13},{12,10},{13,11},{18,20},{1... | collective-permute-start | bytes 1572872 | tf_op jit(solution)/shard_map/ppermute | solution.py:42
  16.8 30.2 %collective-permute-start.8 = (bf16[512,512]{1,0:T(8,128)(2,1)}, bf16[512,512]{1,0:T(8,128)(2,1)}, u32[]{:S(2)}, u32[]{:S(2)}) collective-permute-start(bf16[512,512]{1,0:T(8,128)(2,1)} %collective-permute-done.7), channel_id=1, source_target_pairs={{2,0},{3,1},{4,6},{5,7},{10,8},{11,9},{12,14},{13,15},{18,16},{19,... | collective-permute-start | bytes 1572872 | tf_op jit(solution)/shard_map/ppermute | solution.py:42
  18.0 58.4 %collective-permute-start.5 = (bf16[512,512]{1,0:T(8,128)(2,1)}, bf16[512,512]{1,0:T(8,128)(2,1)}, u32[]{:S(2)}, u32[]{:S(2)}) collective-permute-start(bf16[512,512]{1,0:T(8,128)(2,1)} %get-tuple-element.5), channel_id=1, source_target_pairs={{0,2},{1,3},{2,0},{3,1},{4,6},{5,7},{6,4},{7,5},{8,10},{9,11},{10,... | collective-permute-start | bytes 1572872 | tf_op jit(solution)/shard_map/ppermute | solution.py:42
  34.7 42.3 %collective-permute-start.14 = (bf16[512,512]{1,0:T(8,128)(2,1)}, bf16[512,512]{1,0:T(8,128)(2,1)S(1)}, u32[]{:S(2)}, u32[]{:S(2)}) collective-permute-start(bf16[512,512]{1,0:T(8,128)(2,1)} %get-tuple-element.6), channel_id=1, source_target_pairs={{0,2},{1,3},{2,0},{3,1},{4,6},{5,7},{6,4},{7,5},{8,10},{9,11},{10,... | collective-permute-start | bytes 1572872 | tf_op jit(solution)/shard_map/ppermute | solution.py:42
  42.0 34.4 %collective-permute-start.17 = (bf16[512,512]{1,0:T(8,128)(2,1)}, bf16[512,512]{1,0:T(8,128)(2,1)S(1)}, u32[]{:S(2)}, u32[]{:S(2)}) collective-permute-start(bf16[512,512]{1,0:T(8,128)(2,1)} %collective-permute-done.16), channel_id=1, source_target_pairs={{2,0},{3,1},{4,6},{5,7},{10,8},{11,9},{12,14},{13,15},{18,16},{19,... | collective-permute-start | bytes 1572872 | tf_op jit(solution)/shard_map/ppermute | solution.py:42
  43.3 34.4 %collective-permute-start.2 = (bf16[512,512]{1,0:T(8,128)(2,1)S(1)}, bf16[512,512]{1,0:T(8,128)(2,1)S(1)}, u32[]{:S(2)}, u32[]{:S(2)}) collective-permute-start(bf16[512,512]{1,0:T(8,128)(2,1)S(1)} %slice_bitcast_fusion.2), channel_id=1, source_target_pairs={{0,16},{8,24},{16,0},{24,8},{1,17},{9,25},{17,1},{25,9},{2,18},{10... | collective-permute-start | bytes 1572872 | tf_op jit(solution)/shard_map/ppermute | solution.py:51
  46.9 31.5 %collective-permute-start.3 = (bf16[512,512]{1,0:T(8,128)(2,1)S(1)}, bf16[512,512]{1,0:T(8,128)(2,1)S(1)}, u32[]{:S(2)}, u32[]{:S(2)}) collective-permute-start(bf16[512,512]{1,0:T(8,128)(2,1)S(1)} %slice_bitcast_fusion.1), channel_id=1, source_target_pairs={{0,8},{8,0},{16,24},{24,16},{1,9},{9,1},{17,25},{25,17},{2,10},{10... | collective-permute-start | bytes 1572872 | tf_op jit(solution)/shard_map/ppermute | solution.py:51
  76.4 4.8 %collective-permute-start.4 = (bf16[512,512]{1,0:T(8,128)(2,1)}, bf16[512,512]{1,0:T(8,128)(2,1)S(1)}, u32[]{:S(2)}, u32[]{:S(2)}) collective-permute-start(bf16[512,512]{1,0:T(8,128)(2,1)} %get-tuple-element.5), channel_id=1, source_target_pairs={{0,1},{1,0},{2,3},{3,2},{4,5},{5,4},{6,7},{7,6},{8,9},{9,8},{10,11... | collective-permute-start | bytes 1572872 | tf_op jit(solution)/shard_map/ppermute | solution.py:42
  76.4 42.4 %collective-permute-start.13 = (bf16[512,512]{1,0:T(8,128)(2,1)}, bf16[512,512]{1,0:T(8,128)(2,1)S(1)}, u32[]{:S(2)}, u32[]{:S(2)}) collective-permute-start(bf16[512,512]{1,0:T(8,128)(2,1)} %get-tuple-element.6), channel_id=1, source_target_pairs={{0,1},{1,0},{2,3},{3,2},{4,5},{5,4},{6,7},{7,6},{8,9},{9,8},{10,11... | collective-permute-start | bytes 1572872 | tf_op jit(solution)/shard_map/ppermute | solution.py:42
  77.0 4.7 %collective-permute-start.10 = (bf16[512,512]{1,0:T(8,128)(2,1)}, bf16[512,512]{1,0:T(8,128)(2,1)S(1)}, u32[]{:S(2)}, u32[]{:S(2)}) collective-permute-start(bf16[512,512]{1,0:T(8,128)(2,1)} %collective-permute-done.5), channel_id=1, source_target_pairs={{2,4},{3,5},{4,2},{5,3},{10,12},{11,13},{12,10},{13,11},{18,20},{1... | collective-permute-start | bytes 1572872 | tf_op jit(solution)/shard_map/ppermute | solution.py:42
  77.7 5.8 %collective-permute-start.19 = (bf16[512,512]{1,0:T(8,128)(2,1)S(1)}, bf16[512,512]{1,0:T(8,128)(2,1)S(1)}, u32[]{:S(2)}, u32[]{:S(2)}) collective-permute-start(bf16[512,512]{1,0:T(8,128)(2,1)S(1)} %collective-permute-done.14), channel_id=1, source_target_pairs={{2,4},{3,5},{4,2},{5,3},{10,12},{11,13},{12,10},{13,11},{18,20},{1... | collective-permute-start | bytes 1572872 | tf_op jit(solution)/shard_map/ppermute | solution.py:42
  78.4 5.2 %collective-permute-start.9 = (bf16[512,512]{1,0:T(8,128)(2,1)S(1)}, bf16[512,512]{1,0:T(8,128)(2,1)S(1)}, u32[]{:S(2)}, u32[]{:S(2)}) collective-permute-start(bf16[512,512]{1,0:T(8,128)(2,1)S(1)} %broadcast_select_fusion.3), channel_id=1, source_target_pairs={{0,1},{1,0},{2,3},{3,2},{4,5},{5,4},{6,7},{7,6},{8,9},{9,8},{10,11... | collective-permute-start | bytes 1572872 | tf_op jit(solution)/shard_map/ppermute | solution.py:42
  78.6 1.2 copy-start
  81.2 40.1 %collective-permute-start.6 = (bf16[512,512]{1,0:T(8,128)(2,1)}, bf16[512,512]{1,0:T(8,128)(2,1)S(1)}, u32[]{:S(2)}, u32[]{:S(2)}) collective-permute-start(bf16[512,512]{1,0:T(8,128)(2,1)} %collective-permute-done.5), channel_id=1, source_target_pairs={{0,1},{1,0},{2,3},{3,2},{4,5},{5,4},{6,7},{7,6},{8,9},{9,8},{10,11... | collective-permute-start | bytes 1572872 | tf_op jit(solution)/shard_map/ppermute | solution.py:42
  81.7 24.4 %collective-permute-start.11 = (bf16[512,512]{1,0:T(8,128)(2,1)S(1)}, bf16[512,512]{1,0:T(8,128)(2,1)S(1)}, u32[]{:S(2)}, u32[]{:S(2)}) collective-permute-start(bf16[512,512]{1,0:T(8,128)(2,1)S(1)} %collective-permute-done.10), channel_id=1, source_target_pairs={{2,0},{3,1},{4,6},{5,7},{10,8},{11,9},{12,14},{13,15},{18,16},{19,... | collective-permute-start | bytes 1572872 | tf_op jit(solution)/shard_map/ppermute | solution.py:42
  83.5 39.7 %collective-permute-start.15 = (bf16[512,512]{1,0:T(8,128)(2,1)S(1)}, bf16[512,512]{1,0:T(8,128)(2,1)S(1)}, u32[]{:S(2)}, u32[]{:S(2)}) collective-permute-start(bf16[512,512]{1,0:T(8,128)(2,1)S(1)} %collective-permute-done.14), channel_id=1, source_target_pairs={{0,1},{1,0},{2,3},{3,2},{4,5},{5,4},{6,7},{7,6},{8,9},{9,8},{10,11... | collective-permute-start | bytes 1572872 | tf_op jit(solution)/shard_map/ppermute | solution.py:42
  83.6 35.2 %collective-permute-start.20 = (bf16[512,512]{1,0:T(8,128)(2,1)S(1)}, bf16[512,512]{1,0:T(8,128)(2,1)S(1)}, u32[]{:S(2)}, u32[]{:S(2)}) collective-permute-start(bf16[512,512]{1,0:T(8,128)(2,1)S(1)} %collective-permute-done.19), channel_id=1, source_target_pairs={{2,0},{3,1},{4,6},{5,7},{10,8},{11,9},{12,14},{13,15},{18,16},{19,... | collective-permute-start | bytes 1572872 | tf_op jit(solution)/shard_map/ppermute | solution.py:42
  106.2 16.6 %collective-permute-start.18 = (bf16[512,512]{1,0:T(8,128)(2,1)S(1)}, bf16[512,512]{1,0:T(8,128)(2,1)S(1)}, u32[]{:S(2)}, u32[]{:S(2)}) collective-permute-start(bf16[512,512]{1,0:T(8,128)(2,1)S(1)} %broadcast_select_fusion.1), channel_id=1, source_target_pairs={{0,1},{1,0},{2,3},{3,2},{4,5},{5,4},{6,7},{7,6},{8,9},{9,8},{10,11... | collective-permute-start | bytes 1572872 | tf_op jit(solution)/shard_map/ppermute | solution.py:42
  118.7 4.9 %collective-permute-start.12 = (bf16[512,512]{1,0:T(8,128)(2,1)S(1)}, bf16[512,512]{1,0:T(8,128)(2,1)S(1)}, u32[]{:S(2)}, u32[]{:S(2)}) collective-permute-start(bf16[512,512]{1,0:T(8,128)(2,1)S(1)} %broadcast_select_fusion.2), channel_id=1, source_target_pairs={{0,1},{1,0},{2,3},{3,2},{4,5},{5,4},{6,7},{7,6},{8,9},{9,8},{10,11... | collective-permute-start | bytes 1572872 | tf_op jit(solution)/shard_map/ppermute | solution.py:42
  118.8 5.8 %collective-permute-start.21 = (bf16[512,512]{1,0:T(8,128)(2,1)S(1)}, bf16[512,512]{1,0:T(8,128)(2,1)S(1)}, u32[]{:S(2)}, u32[]{:S(2)}) collective-permute-start(bf16[512,512]{1,0:T(8,128)(2,1)S(1)} %broadcast_select_fusion), channel_id=1, source_target_pairs={{0,1},{1,0},{2,3},{3,2},{4,5},{5,4},{6,7},{7,6},{8,9},{9,8},{10,11... | collective-permute-start | bytes 1572872 | tf_op jit(solution)/shard_map/ppermute | solution.py:42

commit v2 on v0

v2 whole, which is shorter than its diff:
```python
import jax
import jax.numpy as jnp
from jax import lax
from jax.experimental import pallas as pl
from jax.experimental.pallas import tpu as pltpu
from jax.sharding import PartitionSpec as P

LIMIT = 48 * 1024 * 1024
SMALL = pl.CostEstimate(flops=1, bytes_accessed=1, transcendentals=0)
FAR = pl.BlockSpec(memory_space=pltpu.HBM)
NEAR = pl.BlockSpec(memory_space=pltpu.VMEM)
COPIES = pltpu.SemaphoreType.DMA


def cells(brows, bcols, size):
    for i in range(brows * bcols):
        p, q = divmod(i, bcols)
        yield p, q, (slice(p * size, (p + 1) * size), slice(q * size, (q + 1) * size))


def masked(blocks, pattern, cut):
    bcols, brows = pattern.shape
    rows, cols = blocks.shape
    size, half, tall = rows // brows, brows // 2, rows // 2

    def body(pat_hbm, x_hbm, *refs):
        outs, (x_ref, pat_ref, sems) = refs[:-3], refs[-3:]
        copies = [pltpu.make_async_copy(pat_hbm, pat_ref, sems.at[0])]
        for i in (0, 1):
            copies.append(pltpu.make_async_copy(x_hbm.at[i * tall : (i + 1) * tall], x_ref.at[i], sems.at[1 + i]))
        for copy in copies:
            copy.start()
        copies[0].wait()
        for i in (0, 1):
            copies[1 + i].wait()
            out = outs[i] if cut else outs[0].at[i * tall : (i + 1) * tall]
            for p, q, at in cells(half, bcols, size):
                stored = pat_ref[q, i * half + p] != 0
                out[at] = jnp.where(stored, x_ref[(i, *at)], jnp.zeros((), blocks.dtype))

    shapes = [jax.ShapeDtypeStruct((tall, cols) if cut else (rows, cols), blocks.dtype)] * (2 if cut else 1)
    return pl.pallas_call(
        body,
        in_specs=[FAR, FAR],
        out_specs=[NEAR] * len(shapes),
        out_shape=shapes,
        scratch_shapes=[
            pltpu.VMEM((2, tall, cols), blocks.dtype),
            pltpu.SMEM(pattern.shape, jnp.int32),
            COPIES((3,)),
        ],
        cost_estimate=SMALL,
    )(pattern, blocks)


def where_now():
    row, col = lax.axis_index("row"), lax.axis_index("col")
    z, core = col // 2, col % 2
    before = jnp.where(z == 0, 2, jnp.where(z == 1, 0, jnp.where(z == 2, 3, 1)))
    return row, core, (z, before, 3 - z, 3 - before)


def early_slots(slots, b):
    depth = slots[0][0][0].shape[1]
    rows, cols = b[0].shape
    dtype = b[0].dtype
    flat = [*b, *(v for slot in slots for panel in slot for v in panel)]

    def body(*refs):
        ins, (total_ref, late_ref), (panels, held, sems) = refs[: len(flat)], refs[-5:-3], refs[-3:]
        moves = [(ins[i], held.at[i]) for i in range(4)]
        ends = []
        for s, slot in enumerate(slots):
            for which, panel in enumerate(slot):
                first = 0
                for piece in panel:
                    last = first + piece.shape[0]
                    moves.append((ins[len(moves)], panels.at[s, which, first:last]))
                    first = last
            ends.append(len(moves))
        copies = [pltpu.make_async_copy(s, d, sems.at[i]) for i, (s, d) in enumerate(moves)]
        for copy in copies:
            copy.start()
        row, core, zs = where_now()
        tile = 256
        done = 0
        for s in range(len(slots)):
            for copy in copies[done : ends[s]]:
                copy.wait()
            done = ends[s]
            here = zs[s] ^ row
            for m in range(rows // tile):
                some = slice(m * tile, (m + 1) * tile)
                sums = jnp.zeros((tile, cols), jnp.float32) if s == 0 else total_ref[some, :]
                for which in (0, 1):
                    first = pl.multiple_of((core if which == 0 else 1 - core) * depth, depth)
                    part = held[here, pl.ds(first, depth), :]
                    sums += jnp.dot(panels[s, which, some, :], part, preferred_element_type=jnp.float32)
                total_ref[some, :] = sums
        late_ref[...] = held[zs[3] ^ row]

    return pl.pallas_call(
        body,
        in_specs=[FAR] * len(flat),
        out_specs=[NEAR, NEAR],
        out_shape=[jax.ShapeDtypeStruct((rows, cols), jnp.float32), jax.ShapeDtypeStruct((rows, cols), dtype)],
        scratch_shapes=[
            pltpu.VMEM((len(slots), 2, rows, depth), dtype),
            pltpu.VMEM((4, rows, cols), dtype),
            COPIES((len(flat),)),
        ],
        compiler_params=pltpu.CompilerParams(vmem_limit_bytes=LIMIT),
        cost_estimate=SMALL,
    )(*flat)


def last_slot(h, keep_mask, total, late, mine, other, product=None):
    rows, cols = total.shape
    tall, depth = mine.shape
    size = rows // keep_mask.shape[1]
    tile = 256
    per, steps = tile // size, tall // tile

    def body(keep_hbm, total_ref, late_ref, mine_ref, other_ref, *refs):
        out_ref, keep_ref, sem = refs[-3:]
        step = pl.program_id(0)
        copy = pltpu.make_async_copy(keep_hbm, keep_ref, sem)

        @pl.when(step == 0)
        def _():
            copy.start()

        core = lax.axis_index("col") % 2
        near = late_ref[pl.ds(pl.multiple_of(core * depth, depth), depth), :]
        far = late_ref[pl.ds(pl.multiple_of((1 - core) * depth, depth), depth), :]
        sums = total_ref[...] + jnp.dot(mine_ref[...], near, preferred_element_type=jnp.float32)
        sums += jnp.dot(other_ref[...], far, preferred_element_type=jnp.float32)

        @pl.when(step == 0)
        def _():
            copy.wait()

        for p, q, at in cells(per, cols // size, size):
            kept = keep_ref[q, (h * steps + step) * per + p].astype(jnp.float32)
            out_ref[at] = (sums[at] * kept).astype(out_ref.dtype)

    here = pl.BlockSpec((tile, cols), lambda i: (h * steps + i, 0))
    tiles = pl.BlockSpec((tile, depth), lambda i: (i, 0))
    given = () if product is None else (product,)
    return pl.pallas_call(
        body,
        grid=(steps,),
        in_specs=[FAR, here, pl.BlockSpec(late.shape, lambda i: (0, 0)), tiles, tiles] + [FAR] * len(given),
        out_specs=here,
        out_shape=jax.ShapeDtypeStruct((rows, cols), jnp.bfloat16),
        scratch_shapes=[pltpu.SMEM(keep_mask.shape, jnp.int32), COPIES(())],
        input_output_aliases={5: 0} if given else {},
        compiler_params=pltpu.CompilerParams(vmem_limit_bytes=LIMIT),
        cost_estimate=SMALL,
    )(keep_mask, total, late, mine, other, *given)


def on_grid(left, right, a_pattern, b_pattern, keep_mask):
    ring = [(2 * s + c, 2 * d + c) for s, d in ((0, 1), (1, 3), (3, 2), (2, 0)) for c in (0, 1)]
    on = lambda v: lax.ppermute(v, "col", ring)
    cross = lambda v: lax.ppermute(v, "col", [(i, i ^ 1) for i in range(8)])
    to_x = lambda v: lax.ppermute(v, "row", [(i, i ^ 1) for i in range(4)])
    to_y = lambda v: lax.ppermute(v, "row", [(i, i ^ 2) for i in range(4)])
    tied = lambda *v: lax.optimization_barrier(v)

    a = masked(left, a_pattern.T, True)
    r1 = [on(v) for v in a]
    right, *a = tied(right, *a)
    (b,) = masked(right, b_pattern.T, False)
    bx, by = to_x(b), to_y(b)
    bd = to_y(bx)
    r2 = [on(v) for v in r1]
    r3 = [on(v) for v in r2]
    total, late = early_slots(
        tuple((tuple(slot), tuple(cross(v) for v in slot)) for slot in (a, r1, r2)),
        (b, bx, by, bd),
    )
    r3[1], total, late = tied(r3[1], total, late)
    product = last_slot(0, keep_mask.T, total, late, r3[0], cross(r3[0]))
    return last_slot(1, keep_mask.T, total, late, r3[1], cross(r3[1]), product)


def on_any(left, right, a_pattern, b_pattern, keep_mask):
    size = left.shape[0] // a_pattern.shape[0]
    wide = lambda v: jnp.repeat(jnp.repeat(v, size, axis=0), size, axis=1)
    left = left * wide(a_pattern).astype(left.dtype)
    right = right * wide(b_pattern).astype(right.dtype)
    n_row, n_col = lax.axis_size("row"), lax.axis_size("col")
    row, col = lax.axis_index("row"), lax.axis_index("col")
    step = lambda v, axis, n: lax.ppermute(v, axis, [(i, (i + 1) % n) for i in range(n)])
    every = jnp.zeros((n_row, *right.shape), right.dtype)
    for i in range(n_row):
        every = lax.dynamic_update_index_in_dim(every, right, (row - i) % n_row, 0)
        if i < n_row - 1:
            right = step(right, "row", n_row)
    every = every.reshape(n_col, -1, right.shape[1])
    total = jnp.zeros((left.shape[0], right.shape[1]), jnp.float32)
    for i in range(n_col):
        panel = lax.dynamic_index_in_dim(every, (col - i) % n_col, 0, keepdims=False)
        total += jnp.dot(left, panel, preferred_element_type=jnp.float32)
        if i < n_col - 1:
            left = step(left, "col", n_col)
    return (total * wide(keep_mask).astype(jnp.float32)).astype(jnp.bfloat16)


def on_device(left, right, a_pattern, b_pattern, keep_mask):
    tuned = (lax.axis_size("row"), lax.axis_size("col")) == (4, 8)
    return (on_grid if tuned else on_any)(left, right, a_pattern, b_pattern, keep_mask)


def solution(mesh):
    placed = (P("row", "col"),) * 5
    return jax.shard_map(on_device, mesh=mesh, in_specs=placed, out_specs=P("row", "col"), check_vma=False)
```

time: 230 us -> 87.1 us (0.38)
  waiting for transfers between devices: 150 us -> 53 us
  starting transfers between devices: 47.3 us -> 13.2 us
  Pallas kernels: 0 us -> 15.8 us
  matrix products: 12 us -> 0 us
  local copies, waits for them, and re-layouts: 14.1 us -> 4.6 us
  other arithmetic: 6.16 us -> 0 us
    ppermute x16 -> x17, waiting for transfers between devices: 150 us -> 53 us  [the longest x6 53 us: on_grid(): on = lambda v: lax.ppermute(v, 'col', ring)]
    ppermute x16 -> x17, starting transfers between devices: 47.3 us -> 13.2 us  [the longest x6 7.31 us: on_grid(): on = lambda v: lax.ppermute(v, 'col', ring)]
    pallas_call x0 -> x5, Pallas kernels: none -> 15.8 us  [the longest x1 7.39 us: early_slots(): pl.pallas_call(body, in_specs=[FAR] * len(flat), out_specs=[NEAR, NEAR],...]
    dot_general x8 -> x0, matrix products: 12 us -> none  [run_group(): jnp.dot(left_now, panel_now, preferred_element_type=jnp.float32)]
    broadcast_in_dim x6 -> x0, local copies, waits for them, and re-layouts: 7.23 us -> none  [the longest x3 7.12 us: expand_blocks(): jnp.repeat(jnp.repeat(pattern_int, block_size, axis=0), block_size, axis=1)]
    while x18 -> x0, local copies, waits for them, and re-layouts: 6.57 us -> none
    unnamed x10 -> x18, local copies, waits for them, and re-layouts: 0.02 us -> 4.6 us
    select_n x5 -> x0, other arithmetic: 3.77 us -> none  [the longest x3 3.54 us: on_device(): jnp.where(left_amount // (1 << power) % 2 == 1, shifted, left_part)]
  transfers between devices with their start and end apart: 16 -> 17, of which waited for: 15 -> 6; matrix products, arithmetic and copies ran while one was open for 7% -> 0% of each run, Pallas kernels for 0% -> 13%
where the time goes in v2:
time: 87.1 us; the launch traced here: 86.8 us
  waiting for transfers between devices  53 us (61%)
  Pallas kernels  15.8 us (18%)
  starting transfers between devices  13.2 us (15%)
  local copies, waits for them, and re-layouts  4.6 us (5%)
    ppermute x6, waiting for transfers between devices, on_grid(): on = lambda v: lax.ppermute(v, 'col', ring)  53 us
    pallas_call x1, Pallas kernels, early_slots(): pl.pallas_call(body, in_specs=[FAR] * len(flat), out_specs=[NEAR, NEAR],...  7.39 us
    ppermute x6, starting transfers between devices, on_grid(): on = lambda v: lax.ppermute(v, 'col', ring)  7.31 us
    pallas_call x2, Pallas kernels, masked(): pl.pallas_call(body, in_specs=[FAR, FAR], out_specs=[NEAR] * len(shapes),...  4.67 us
    unnamed x18, local copies, waits for them, and re-layouts  4.6 us
    pallas_call x2, Pallas kernels, last_slot(): pl.pallas_call(body, grid=(steps,), in_specs=[FAR, here, pl.BlockSpec(lat...  3.77 us
    ppermute x1, starting transfers between devices, on_grid(): to_x = lambda v: lax.ppermute(v, 'row', [(i, i ^ 1) for i in range(4)])  2.64 us
    ppermute x2, starting transfers between devices, on_grid(): to_y = lambda v: lax.ppermute(v, 'row', [(i, i ^ 2) for i in range(4)])  2.09 us
  transfers between devices with their start and end apart: 17, of which 6 were waited for; matrix products, arithmetic and copies ran while one was open for 0% of the time, Pallas kernels for 13%

profile of v2, /device:TPU:0, one launch (start us, length us, event | category | flops | bytes accessed | tf_op | source)
XLA Modules:
  0.0 86.8 jit_solution(4537499308663191845)
XLA Ops:
  0.0 2.4 %shard_map.55 = (bf16[512,512]{1,0:T(8,128)(2,1)}, bf16[512,512]{1,0:T(8,128)(2,1)}) custom-call(s32[4,8]{1,0:T(4,128)} %bitcast.5, bf16[1024,512]{1,0:T(8,128)(2,1)} %x_hbm.1), custom_call_target="tpu_custom_call" | custom-call | flops 1 | bytes 1 | tf_op jit(solution)/shard_map/pallas_call | solution.py:42
  2.4 0.0 copy-start.2
  2.4 0.0 copy-start.3
  2.4 0.5 collective-permute-start.6
  2.9 2.3 %shard_map.56.refs_0_ = bf16[1024,512]{1,0:T(8,128)(2,1)} custom-call(s32[4,8]{1,0:T(4,128)} %bitcast.6, bf16[1024,512]{1,0:T(8,128)(2,1)} %x_hbm.2), custom_call_target="tpu_custom_call" | custom-call | flops 1 | bytes 1 | tf_op jit(solution)/shard_map/pallas_call | solution.py:42
  5.2 0.0 copy-start.4
  5.2 2.6 %collective-permute-start.3 = (bf16[1024,512]{1,0:T(8,128)(2,1)}, bf16[1024,512]{1,0:T(8,128)(2,1)S(1)}, u32[]{:S(2)}, u32[]{:S(2)}) collective-permute-start(bf16[1024,512]{1,0:T(8,128)(2,1)} %shard_map.56.refs_0_), channel_id=1, source_target_pairs={{0,8},{8,0},{16,24},{24,16},{1,9},{9,1},{17,25},{25,17},{2,10},{10... | collective-permute-start | bytes 3145736 | tf_op jit(solution)/shard_map/ppermute | solution.py:167
  7.9 1.5 %collective-permute-start.4 = (bf16[1024,512]{1,0:T(8,128)(2,1)}, bf16[1024,512]{1,0:T(8,128)(2,1)S(1)}, u32[]{:S(2)}, u32[]{:S(2)}) collective-permute-start(bf16[1024,512]{1,0:T(8,128)(2,1)} %shard_map.56.refs_0_), channel_id=1, source_target_pairs={{0,16},{8,24},{16,0},{24,8},{1,17},{9,25},{17,1},{25,9},{2,18},{10... | collective-permute-start | bytes 3145736 | tf_op jit(solution)/shard_map/ppermute | solution.py:168
  9.4 0.0 copy-done.2
  9.4 1.6 %collective-permute-start.8 = (bf16[512,512]{1,0:T(8,128)(2,1)S(1)}, bf16[512,512]{1,0:T(8,128)(2,1)S(1)}, u32[]{:S(2)}, u32[]{:S(2)}) collective-permute-start(bf16[512,512]{1,0:T(8,128)(2,1)S(1)} %copy-done.2), channel_id=1, source_target_pairs={{0,2},{1,3},{2,6},{3,7},{6,4},{7,5},{4,0},{5,1},{8,10},{9,11},{10,... | collective-permute-start | bytes 1572872 | tf_op jit(solution)/shard_map/ppermute | solution.py:165
  11.0 0.0 copy-done.3
  11.0 2.6 %collective-permute-start = (bf16[512,512]{1,0:T(8,128)(2,1)S(1)}, bf16[512,512]{1,0:T(8,128)(2,1)S(1)}, u32[]{:S(2)}, u32[]{:S(2)}) collective-permute-start(bf16[512,512]{1,0:T(8,128)(2,1)S(1)} %copy-done.3), channel_id=1, source_target_pairs={{0,2},{1,3},{2,6},{3,7},{6,4},{7,5},{4,0},{5,1},{8,10},{9,11},{10,... | collective-permute-start | bytes 1572872 | tf_op jit(solution)/shard_map/ppermute | solution.py:165
  13.6 0.0 collective-permute-done.6.refs_6_
  13.6 0.0 collective-permute-start.7
  13.6 11.5 %collective-permute-done.8.refs_8_ = bf16[512,512]{1,0:T(8,128)(2,1)S(1)} collective-permute-done((bf16[512,512]{1,0:T(8,128)(2,1)S(1)}, bf16[512,512]{1,0:T(8,128)(2,1)S(1)}, u32[]{:S(2)}, u32[]{:S(2)}) %collective-permute-start.8) | collective-permute-done | bytes 524320 | tf_op jit(solution)/shard_map/ppermute | solution.py:165
  25.1 0.8 collective-permute-start.11
  25.9 10.4 %collective-permute-done.refs_9_ = bf16[512,512]{1,0:T(8,128)(2,1)S(1)} collective-permute-done((bf16[512,512]{1,0:T(8,128)(2,1)S(1)}, bf16[512,512]{1,0:T(8,128)(2,1)S(1)}, u32[]{:S(2)}, u32[]{:S(2)}) %collective-permute-start) | collective-permute-done | bytes 524320 | tf_op jit(solution)/shard_map/ppermute | solution.py:165
  36.3 0.8 collective-permute-start.1
  37.1 0.0 collective-permute-done.7.refs_7_
  37.1 0.0 collective-permute-start.10
  37.1 0.0 collective-permute-done.3.refs_1_
  37.1 0.0 copy-start.5
  37.1 0.6 collective-permute-start.5
  37.7 0.0 collective-permute-done.4.refs_2_
  37.7 0.0 copy-start.6
  37.7 0.2 collective-permute-start.9
  37.9 9.7 %collective-permute-done.11.refs_12_ = bf16[512,512]{1,0:T(8,128)(2,1)S(1)} collective-permute-done((bf16[512,512]{1,0:T(8,128)(2,1)S(1)}, bf16[512,512]{1,0:T(8,128)(2,1)S(1)}, u32[]{:S(2)}, u32[]{:S(2)}) %collective-permute-start.11) | collective-permute-done | bytes 524320 | tf_op jit(solution)/shard_map/ppermute | solution.py:165
  47.6 0.8 collective-permute-start.15
  48.4 10.4 %collective-permute-done.1.refs_13_ = bf16[512,512]{1,0:T(8,128)(2,1)S(1)} collective-permute-done((bf16[512,512]{1,0:T(8,128)(2,1)S(1)}, bf16[512,512]{1,0:T(8,128)(2,1)S(1)}, u32[]{:S(2)}, u32[]{:S(2)}) %collective-permute-start.1) | collective-permute-done | bytes 524320 | tf_op jit(solution)/shard_map/ppermute | solution.py:165
  58.8 0.0 collective-permute-start.12
  58.8 0.0 collective-permute-done.10.refs_11_
  58.8 0.5 collective-permute-start.13
  59.3 0.0 collective-permute-done.9.refs_10_
  59.3 0.8 collective-permute-start.2
  60.1 9.9 %collective-permute-done.15.mine_ref = bf16[512,512]{1,0:T(8,128)(2,1)S(1)} collective-permute-done((bf16[512,512]{1,0:T(8,128)(2,1)S(1)}, bf16[512,512]{1,0:T(8,128)(2,1)S(1)}, u32[]{:S(2)}, u32[]{:S(2)}) %collective-permute-start.15) | collective-permute-done | bytes 524320 | tf_op jit(solution)/shard_map/ppermute | solution.py:165
  70.0 0.0 collective-permute-start.16
  70.0 0.0 collective-permute-done.12.refs_14_
  70.1 0.0 collective-permute-done.13.refs_15_
  70.1 0.0 copy-start.8
  70.1 0.0 collective-permute-done.5.refs_3_
  70.1 0.0 copy-done.5
  70.1 0.0 copy-done.6
  70.1 0.8 copy-done.8
  70.9 0.0 copy-start.7
  70.9 1.0 %copy-done.7 = bf16[1024,512]{1,0:T(8,128)(2,1)} copy-done((bf16[1024,512]{1,0:T(8,128)(2,1)}, bf16[1024,512]{1,0:T(8,128)(2,1)S(1)}, u32[]{:S(2)}) %copy-start.7) | copy-done | bytes 1048600
  71.9 7.4 %shard_map.57 = (f32[1024,512]{1,0:T(8,128)}, bf16[1024,512]{1,0:T(8,128)(2,1)}) custom-call(bf16[1024,512]{1,0:T(8,128)(2,1)} %shard_map.56.refs_0_, bf16[1024,512]{1,0:T(8,128)(2,1)} %copy-done.5, bf16[1024,512]{1,0:T(8,128)(2,1)} %copy-done.6, bf16[1024,512]{1,0:T(8,128)(2,1)} %copy-done.7, bf16[512,512]{1,0:T(8,128)(2,1)S(1)} %copy-done.2, ...), custom_call_target="tpu_custom_call" | custom-call | flops 1 | bytes 1 | tf_op jit(solution)/shard_map/pallas_call | solution.py:102
  79.3 0.9 %collective-permute-done.2.mine_ref = bf16[512,512]{1,0:T(8,128)(2,1)S(1)} collective-permute-done((bf16[512,512]{1,0:T(8,128)(2,1)S(1)}, bf16[512,512]{1,0:T(8,128)(2,1)S(1)}, u32[]{:S(2)}, u32[]{:S(2)}) %collective-permute-start.2) | collective-permute-done | bytes 524320 | tf_op jit(solution)/shard_map/ppermute | solution.py:165
  80.2 0.0 collective-permute-start.14
  80.2 0.0 collective-permute-done.16.other_ref
  80.2 0.0 copy-done.4
  80.2 0.0 copy-start
  80.2 1.6 %copy-done = f32[1024,512]{1,0:T(8,128)S(1)} copy-done((f32[1024,512]{1,0:T(8,128)S(1)}, f32[1024,512]{1,0:T(8,128)}, u32[]{:S(2)}) %copy-start) | copy-done | bytes 2097176
  81.8 0.0 copy-start.1
  81.8 1.2 %copy-done.1 = bf16[1024,512]{1,0:T(8,128)(2,1)S(1)} copy-done((bf16[1024,512]{1,0:T(8,128)(2,1)S(1)}, bf16[1024,512]{1,0:T(8,128)(2,1)}, u32[]{:S(2)}) %copy-start.1) | copy-done | bytes 1048600
  83.0 1.9 %shard_map.58.refs_0_ = bf16[1024,512]{1,0:T(8,128)(2,1)} custom-call(s32[4,8]{1,0:T(4,128)S(1)} %bitcast.3, f32[1024,512]{1,0:T(8,128)S(1)} %copy-done, bf16[1024,512]{1,0:T(8,128)(2,1)S(1)} %copy-done.1, bf16[512,512]{1,0:T(8,128)(2,1)S(1)} %collective-permute-done.15.mine_ref, bf16[512,512]{1,0:T(8,128)(2,1)S(1)} %collective-permute-done.16.other_ref), custom_call_target="tpu_custom_call" | custom-call | flops 1 | bytes 1 | tf_op jit(solution)/shard_map/pallas_call | solution.py:150
  84.9 0.0 collective-permute-done.14.other_ref
  84.9 1.9 %shard_map.59 = bf16[1024,512]{1,0:T(8,128)(2,1)} custom-call(s32[4,8]{1,0:T(4,128)S(1)} %bitcast.4, f32[1024,512]{1,0:T(8,128)S(1)} %copy-done, bf16[1024,512]{1,0:T(8,128)(2,1)S(1)} %copy-done.1, bf16[512,512]{1,0:T(8,128)(2,1)S(1)} %collective-permute-done.2.mine_ref, ...), custom_call_target="tpu_custom_call", output_to_operand_aliasing={{}: (5, {})} | custom-call | flops 1 | bytes 1 | tf_op jit(solution)/shard_map/pallas_call | solution.py:150
Async XLA Ops:
  2.4 7.0 %copy-start.2 = (bf16[512,512]{1,0:T(8,128)(2,1)S(1)}, bf16[512,512]{1,0:T(8,128)(2,1)}, u32[]{:S(2)}) copy-start(bf16[512,512]{1,0:T(8,128)(2,1)} %get-tuple-element.18.refs_4_) | copy-start | bytes 1572868
  2.4 8.6 %copy-start.3 = (bf16[512,512]{1,0:T(8,128)(2,1)S(1)}, bf16[512,512]{1,0:T(8,128)(2,1)}, u32[]{:S(2)}) copy-start(bf16[512,512]{1,0:T(8,128)(2,1)} %get-tuple-element.19.refs_5_) | copy-start | bytes 1572868
  2.4 11.2 %collective-permute-start.6 = (bf16[512,512]{1,0:T(8,128)(2,1)}, bf16[512,512]{1,0:T(8,128)(2,1)S(1)}, u32[]{:S(2)}, u32[]{:S(2)}) collective-permute-start(bf16[512,512]{1,0:T(8,128)(2,1)} %get-tuple-element.18.refs_4_), channel_id=1, source_target_pairs={{0,1},{1,0},{2,3},{3,2},{4,5},{5,4},{6,7},{7,6},{8,9},{9,8},{10,11... | collective-permute-start | bytes 1572872 | tf_op jit(solution)/shard_map/ppermute | solution.py:166
  5.2 75.0 %copy-start.4 = (s32[8,4]{0,1:T(4,128)S(1)}, s32[8,4]{0,1:T(4,128)}, u32[]{:S(2)}) copy-start(s32[8,4]{0,1:T(4,128)} %param.9) | copy-start | bytes 388
  5.2 31.9 %collective-permute-start.3 = (bf16[1024,512]{1,0:T(8,128)(2,1)}, bf16[1024,512]{1,0:T(8,128)(2,1)S(1)}, u32[]{:S(2)}, u32[]{:S(2)}) collective-permute-start(bf16[1024,512]{1,0:T(8,128)(2,1)} %shard_map.56.refs_0_), channel_id=1, source_target_pairs={{0,8},{8,0},{16,24},{24,16},{1,9},{9,1},{17,25},{25,17},{2,10},{10... | collective-permute-start | bytes 3145736 | tf_op jit(solution)/shard_map/ppermute | solution.py:167
  7.9 29.8 %collective-permute-start.4 = (bf16[1024,512]{1,0:T(8,128)(2,1)}, bf16[1024,512]{1,0:T(8,128)(2,1)S(1)}, u32[]{:S(2)}, u32[]{:S(2)}) collective-permute-start(bf16[1024,512]{1,0:T(8,128)(2,1)} %shard_map.56.refs_0_), channel_id=1, source_target_pairs={{0,16},{8,24},{16,0},{24,8},{1,17},{9,25},{17,1},{25,9},{2,18},{10... | collective-permute-start | bytes 3145736 | tf_op jit(solution)/shard_map/ppermute | solution.py:168
  9.4 15.7 %collective-permute-start.8 = (bf16[512,512]{1,0:T(8,128)(2,1)S(1)}, bf16[512,512]{1,0:T(8,128)(2,1)S(1)}, u32[]{:S(2)}, u32[]{:S(2)}) collective-permute-start(bf16[512,512]{1,0:T(8,128)(2,1)S(1)} %copy-done.2), channel_id=1, source_target_pairs={{0,2},{1,3},{2,6},{3,7},{6,4},{7,5},{4,0},{5,1},{8,10},{9,11},{10,... | collective-permute-start | bytes 1572872 | tf_op jit(solution)/shard_map/ppermute | solution.py:165
  11.0 25.4 %collective-permute-start = (bf16[512,512]{1,0:T(8,128)(2,1)S(1)}, bf16[512,512]{1,0:T(8,128)(2,1)S(1)}, u32[]{:S(2)}, u32[]{:S(2)}) collective-permute-start(bf16[512,512]{1,0:T(8,128)(2,1)S(1)} %copy-done.3), channel_id=1, source_target_pairs={{0,2},{1,3},{2,6},{3,7},{6,4},{7,5},{4,0},{5,1},{8,10},{9,11},{10,... | collective-permute-start | bytes 1572872 | tf_op jit(solution)/shard_map/ppermute | solution.py:165
  13.6 23.6 %collective-permute-start.7 = (bf16[512,512]{1,0:T(8,128)(2,1)S(1)}, bf16[512,512]{1,0:T(8,128)(2,1)S(1)}, u32[]{:S(2)}, u32[]{:S(2)}) collective-permute-start(bf16[512,512]{1,0:T(8,128)(2,1)S(1)} %copy-done.3), channel_id=1, source_target_pairs={{0,1},{1,0},{2,3},{3,2},{4,5},{5,4},{6,7},{7,6},{8,9},{9,8},{10,11... | collective-permute-start | bytes 1572872 | tf_op jit(solution)/shard_map/ppermute | solution.py:166
  25.1 22.5 %collective-permute-start.11 = (bf16[512,512]{1,0:T(8,128)(2,1)S(1)}, bf16[512,512]{1,0:T(8,128)(2,1)S(1)}, u32[]{:S(2)}, u32[]{:S(2)}) collective-permute-start(bf16[512,512]{1,0:T(8,128)(2,1)S(1)} %collective-permute-done.8.refs_8_), channel_id=1, source_target_pairs={{0,2},{1,3},{2,6},{3,7},{6,4},{7,5},{4,0},{5,1},{8,10},{9,11},{10,... | collective-permute-start | bytes 1572872 | tf_op jit(solution)/shard_map/ppermute | solution.py:165
  36.3 22.5 %collective-permute-start.1 = (bf16[512,512]{1,0:T(8,128)(2,1)S(1)}, bf16[512,512]{1,0:T(8,128)(2,1)S(1)}, u32[]{:S(2)}, u32[]{:S(2)}) collective-permute-start(bf16[512,512]{1,0:T(8,128)(2,1)S(1)} %collective-permute-done.refs_9_), channel_id=1, source_target_pairs={{0,2},{1,3},{2,6},{3,7},{6,4},{7,5},{4,0},{5,1},{8,10},{9,11},{10,... | collective-permute-start | bytes 1572872 | tf_op jit(solution)/shard_map/ppermute | solution.py:165
  37.1 21.7 %collective-permute-start.10 = (bf16[512,512]{1,0:T(8,128)(2,1)S(1)}, bf16[512,512]{1,0:T(8,128)(2,1)S(1)}, u32[]{:S(2)}, u32[]{:S(2)}) collective-permute-start(bf16[512,512]{1,0:T(8,128)(2,1)S(1)} %collective-permute-done.refs_9_), channel_id=1, source_target_pairs={{0,1},{1,0},{2,3},{3,2},{4,5},{5,4},{6,7},{7,6},{8,9},{9,8},{10,11... | collective-permute-start | bytes 1572872 | tf_op jit(solution)/shard_map/ppermute | solution.py:166
  37.1 32.9 %copy-start.5 = (bf16[1024,512]{1,0:T(8,128)(2,1)}, bf16[1024,512]{1,0:T(8,128)(2,1)S(1)}, u32[]{:S(2)}) copy-start(bf16[1024,512]{1,0:T(8,128)(2,1)S(1)} %collective-permute-done.3.refs_1_) | copy-start | bytes 3145732
  37.1 32.9 %collective-permute-start.5 = (bf16[1024,512]{1,0:T(8,128)(2,1)S(1)}, bf16[1024,512]{1,0:T(8,128)(2,1)S(1)}, u32[]{:S(2)}, u32[]{:S(2)}) collective-permute-start(bf16[1024,512]{1,0:T(8,128)(2,1)S(1)} %collective-permute-done.3.refs_1_), channel_id=1, source_target_pairs={{0,16},{8,24},{16,0},{24,8},{1,17},{9,25},{17,1},{25,9},{2,18},{10... | collective-permute-start | bytes 3145736 | tf_op jit(solution)/shard_map/ppermute | solution.py:168
  37.7 32.4 %copy-start.6 = (bf16[1024,512]{1,0:T(8,128)(2,1)}, bf16[1024,512]{1,0:T(8,128)(2,1)S(1)}, u32[]{:S(2)}) copy-start(bf16[1024,512]{1,0:T(8,128)(2,1)S(1)} %collective-permute-done.4.refs_2_) | copy-start | bytes 3145732
  37.7 21.6 %collective-permute-start.9 = (bf16[512,512]{1,0:T(8,128)(2,1)S(1)}, bf16[512,512]{1,0:T(8,128)(2,1)S(1)}, u32[]{:S(2)}, u32[]{:S(2)}) collective-permute-start(bf16[512,512]{1,0:T(8,128)(2,1)S(1)} %collective-permute-done.8.refs_8_), channel_id=1, source_target_pairs={{0,1},{1,0},{2,3},{3,2},{4,5},{5,4},{6,7},{7,6},{8,9},{9,8},{10,11... | collective-permute-start | bytes 1572872 | tf_op jit(solution)/shard_map/ppermute | solution.py:166
  47.6 22.5 %collective-permute-start.15 = (bf16[512,512]{1,0:T(8,128)(2,1)S(1)}, bf16[512,512]{1,0:T(8,128)(2,1)S(1)}, u32[]{:S(2)}, u32[]{:S(2)}) collective-permute-start(bf16[512,512]{1,0:T(8,128)(2,1)S(1)} %collective-permute-done.11.refs_12_), channel_id=1, source_target_pairs={{0,2},{1,3},{2,6},{3,7},{6,4},{7,5},{4,0},{5,1},{8,10},{9,11},{10,... | collective-permute-start | bytes 1572872 | tf_op jit(solution)/shard_map/ppermute | solution.py:165
  58.8 11.2 %collective-permute-start.12 = (bf16[512,512]{1,0:T(8,128)(2,1)S(1)}, bf16[512,512]{1,0:T(8,128)(2,1)S(1)}, u32[]{:S(2)}, u32[]{:S(2)}) collective-permute-start(bf16[512,512]{1,0:T(8,128)(2,1)S(1)} %collective-permute-done.11.refs_12_), channel_id=1, source_target_pairs={{0,1},{1,0},{2,3},{3,2},{4,5},{5,4},{6,7},{7,6},{8,9},{9,8},{10,11... | collective-permute-start | bytes 1572872 | tf_op jit(solution)/shard_map/ppermute | solution.py:166
  58.8 11.2 %collective-permute-start.13 = (bf16[512,512]{1,0:T(8,128)(2,1)S(1)}, bf16[512,512]{1,0:T(8,128)(2,1)S(1)}, u32[]{:S(2)}, u32[]{:S(2)}) collective-permute-start(bf16[512,512]{1,0:T(8,128)(2,1)S(1)} %collective-permute-done.1.refs_13_), channel_id=1, source_target_pairs={{0,1},{1,0},{2,3},{3,2},{4,5},{5,4},{6,7},{7,6},{8,9},{9,8},{10,11... | collective-permute-start | bytes 1572872 | tf_op jit(solution)/shard_map/ppermute | solution.py:166
  59.3 20.8 %collective-permute-start.2 = (bf16[512,512]{1,0:T(8,128)(2,1)S(1)}, bf16[512,512]{1,0:T(8,128)(2,1)S(1)}, u32[]{:S(2)}, u32[]{:S(2)}) collective-permute-start(bf16[512,512]{1,0:T(8,128)(2,1)S(1)} %collective-permute-done.1.refs_13_), channel_id=1, source_target_pairs={{0,2},{1,3},{2,6},{3,7},{6,4},{7,5},{4,0},{5,1},{8,10},{9,11},{10,... | collective-permute-start | bytes 1572872 | tf_op jit(solution)/shard_map/ppermute | solution.py:165
  70.0 10.1 %collective-permute-start.16 = (bf16[512,512]{1,0:T(8,128)(2,1)S(1)}, bf16[512,512]{1,0:T(8,128)(2,1)S(1)}, u32[]{:S(2)}, u32[]{:S(2)}) collective-permute-start(bf16[512,512]{1,0:T(8,128)(2,1)S(1)} %collective-permute-done.15.mine_ref), channel_id=1, source_target_pairs={{0,1},{1,0},{2,3},{3,2},{4,5},{5,4},{6,7},{7,6},{8,9},{9,8},{10,11... | collective-permute-start | bytes 1572872 | tf_op jit(solution)/shard_map/ppermute | solution.py:166
  70.1 0.8 copy-start.8
  70.9 1.0 %copy-start.7 = (bf16[1024,512]{1,0:T(8,128)(2,1)}, bf16[1024,512]{1,0:T(8,128)(2,1)S(1)}, u32[]{:S(2)}) copy-start(bf16[1024,512]{1,0:T(8,128)(2,1)S(1)} %collective-permute-done.5.refs_3_) | copy-start | bytes 3145732
  80.2 4.7 %collective-permute-start.14 = (bf16[512,512]{1,0:T(8,128)(2,1)S(1)}, bf16[512,512]{1,0:T(8,128)(2,1)S(1)}, u32[]{:S(2)}, u32[]{:S(2)}) collective-permute-start(bf16[512,512]{1,0:T(8,128)(2,1)S(1)} %collective-permute-done.2.mine_ref), channel_id=1, source_target_pairs={{0,1},{1,0},{2,3},{3,2},{4,5},{5,4},{6,7},{7,6},{8,9},{9,8},{10,11... | collective-permute-start | bytes 1572872 | tf_op jit(solution)/shard_map/ppermute | solution.py:166
  80.2 1.6 %copy-start = (f32[1024,512]{1,0:T(8,128)S(1)}, f32[1024,512]{1,0:T(8,128)}, u32[]{:S(2)}) copy-start(f32[1024,512]{1,0:T(8,128)} %get-tuple-element.22.total_ref) | copy-start | bytes 6291460
  81.8 1.2 %copy-start.1 = (bf16[1024,512]{1,0:T(8,128)(2,1)S(1)}, bf16[1024,512]{1,0:T(8,128)(2,1)}, u32[]{:S(2)}) copy-start(bf16[1024,512]{1,0:T(8,128)(2,1)} %get-tuple-element.23.late_ref) | copy-start | bytes 3145732

commit v3 on v2

v3 whole, which is shorter than its diff:
```python
import jax
import jax.numpy as jnp
from jax import lax
from jax.experimental import pallas as pl
from jax.experimental.pallas import tpu as pltpu
from jax.sharding import PartitionSpec as P

MIB = 1024 * 1024
SMALL = pl.CostEstimate(flops=1, bytes_accessed=1, transcendentals=0)
FAR = pl.BlockSpec(memory_space=pl.ANY)
HOME = pl.BlockSpec(memory_space=pltpu.HBM)
NEAR = pl.BlockSpec(memory_space=pltpu.VMEM)
COPIES = pltpu.SemaphoreType.DMA


def cells(brows, bcols, size):
    for i in range(brows * bcols):
        p, q = divmod(i, bcols)
        yield p, q, (slice(p * size, (p + 1) * size), slice(q * size, (q + 1) * size))


def masked(left, right, a_pattern, b_pattern):
    bcols, brows = a_pattern.shape
    rows, cols = left.shape
    size, half, tall = rows // brows, brows // 2, rows // 2

    def body(*refs):
        (a_hbm, b_hbm, left_hbm, right_hbm), outs, (x_ref, pat_ref, sems) = refs[:4], refs[4:-3], refs[-3:]
        moves = [(a_hbm, pat_ref.at[0]), (b_hbm, pat_ref.at[1])]
        for s, x_hbm in enumerate((left_hbm, right_hbm)):
            moves += [(x_hbm.at[i * tall : (i + 1) * tall], x_ref.at[s, i]) for i in (0, 1)]
        copies = [pltpu.make_async_copy(s, d, sems.at[i]) for i, (s, d) in enumerate(moves)]
        for copy in copies:
            copy.start()
        for copy in copies[:2]:
            copy.wait()
        for s in (0, 1):
            for i in (0, 1):
                copies[2 + 2 * s + i].wait()
                for p, q, at in cells(half, bcols, size):
                    stored = pat_ref[s, q, i * half + p] != 0
                    block = jnp.where(stored, x_ref[(s, i, *at)], jnp.zeros((), left.dtype))
                    outs[1 + 2 * s + i][at] = block
                    if s == 0:
                        outs[0][i * tall + at[0].start : i * tall + at[0].stop, at[1]] = block

    part = jax.ShapeDtypeStruct((tall, cols), left.dtype)
    return pl.pallas_call(
        body,
        in_specs=[FAR] * 4,
        out_specs=[NEAR] * 5,
        out_shape=[jax.ShapeDtypeStruct(left.shape, left.dtype)] + [part] * 4,
        scratch_shapes=[
            pltpu.VMEM((2, 2, tall, cols), left.dtype),
            pltpu.SMEM((2, *a_pattern.shape), jnp.int32),
            COPIES((6,)),
        ],
        cost_estimate=SMALL,
    )(a_pattern, b_pattern, left, right)


def where_now():
    row, col = lax.axis_index("row"), lax.axis_index("col")
    z, core = col // 2, col % 2
    before = jnp.where(z == 0, 2, jnp.where(z == 1, 0, jnp.where(z == 2, 3, 1)))
    return row, core, (z, before, 3 - z, 3 - before)


def early_slots(slots, b):
    depth = slots[0][0][0].shape[1]
    rows, cols = sum(v.shape[0] for v in b[0]), b[0][0].shape[1]
    dtype = b[0][0].dtype
    specs = [HOME if i == 0 else FAR for i, shard in enumerate(b) for _ in shard]
    specs += [HOME if s + w == 0 else FAR for s, slot in enumerate(slots) for w, panel in enumerate(slot) for _ in panel]
    flat = [*(v for shard in b for v in shard), *(v for slot in slots for panel in slot for v in panel)]

    def body(*refs):
        ins, (total_ref, late_ref), (panels, held, sems) = refs[: len(flat)], refs[-5:-3], refs[-3:]
        moves = []
        for i, shard in enumerate(b):
            first = 0
            for piece in shard:
                last = first + piece.shape[0]
                moves.append((ins[len(moves)], held.at[i, first:last]))
                first = last
        ends = []
        for s, slot in enumerate(slots):
            for which, panel in enumerate(slot):
                first = 0
                for piece in panel:
                    last = first + piece.shape[0]
                    moves.append((ins[len(moves)], panels.at[s, which, first:last]))
                    first = last
            ends.append(len(moves))
        copies = [pltpu.make_async_copy(s, d, sems.at[i]) for i, (s, d) in enumerate(moves)]
        for copy in copies:
            copy.start()
        row, core, zs = where_now()
        tile = 256
        done = 0
        for s in range(len(slots)):
            for copy in copies[done : ends[s]]:
                copy.wait()
            done = ends[s]
            here = zs[s] ^ row
            for m in range(rows // tile):
                some = slice(m * tile, (m + 1) * tile)
                sums = jnp.zeros((tile, cols), jnp.float32) if s == 0 else total_ref[some, :]
                for which in (0, 1):
                    first = pl.multiple_of((core if which == 0 else 1 - core) * depth, depth)
                    part = held[here, pl.ds(first, depth), :]
                    sums += jnp.dot(panels[s, which, some, :], part, preferred_element_type=jnp.float32)
                total_ref[some, :] = sums
        late_ref[...] = held[zs[3] ^ row]

    return pl.pallas_call(
        body,
        in_specs=specs,
        out_specs=[NEAR, NEAR],
        out_shape=[jax.ShapeDtypeStruct((rows, cols), jnp.float32), jax.ShapeDtypeStruct((rows, cols), dtype)],
        scratch_shapes=[
            pltpu.VMEM((len(slots), 2, rows, depth), dtype),
            pltpu.VMEM((4, rows, cols), dtype),
            COPIES((len(flat),)),
        ],
        compiler_params=pltpu.CompilerParams(vmem_limit_bytes=20 * MIB),
        cost_estimate=SMALL,
    )(*flat)


def last_slot(keep_mask, total, late, panels):
    rows, cols = total.shape
    tall, depth = panels[0][0].shape
    size = rows // keep_mask.shape[1]
    tile = 256
    per, steps, pieces = tile // size, rows // tile, rows // tall
    flat = [v for pair in zip(*panels) for v in pair]

    def body(keep_hbm, total_hbm, late_hbm, *refs):
        ins, out_hbm = refs[: len(flat)], refs[len(flat)]
        keep_ref, total_ref, late_ref, held, out_ref, sems, out_sems = refs[len(flat) + 1 :]
        load = lambda i, s, d: pltpu.make_async_copy(s, d, sems.at[i])
        copies = [load(0, late_hbm, late_ref), load(1, keep_hbm, keep_ref)]
        for i in range(pieces):
            some = slice(i * tall, (i + 1) * tall)
            copies.append(load(2 + 3 * i, total_hbm.at[some], total_ref.at[some]))
            copies.append(load(3 + 3 * i, ins[2 * i], held.at[0, some]))
            copies.append(load(4 + 3 * i, ins[2 * i + 1], held.at[1, some]))
        for copy in copies:
            copy.start()
        core = lax.axis_index("col") % 2
        for copy in copies[:2]:
            copy.wait()
        writes = []
        for m in range(steps):
            if m * tile % tall == 0:
                i = m * tile // tall
                for copy in copies[2 + 3 * i : 5 + 3 * i]:
                    copy.wait()
            some = slice(m * tile, (m + 1) * tile)
            near = late_ref[pl.ds(pl.multiple_of(core * depth, depth), depth), :]
            far = late_ref[pl.ds(pl.multiple_of((1 - core) * depth, depth), depth), :]
            sums = total_ref[some, :] + jnp.dot(held[0, some, :], near, preferred_element_type=jnp.float32)
            sums += jnp.dot(held[1, some, :], far, preferred_element_type=jnp.float32)
            for p, q, at in cells(per, cols // size, size):
                kept = keep_ref[q, m * per + p].astype(jnp.float32)
                out_ref[m * tile + at[0].start : m * tile + at[0].stop, at[1]] = (sums[at] * kept).astype(out_ref.dtype)
            write = pltpu.make_async_copy(out_ref.at[some], out_hbm.at[some], out_sems.at[m])
            write.start()
            writes.append(write)
        for write in writes:
            write.wait()

    return pl.pallas_call(
        body,
        in_specs=[FAR] + [HOME] * 2 + [FAR] * len(flat),
        out_specs=FAR,
        out_shape=jax.ShapeDtypeStruct((rows, cols), jnp.bfloat16),
        scratch_shapes=[
            pltpu.SMEM(keep_mask.shape, jnp.int32),
            pltpu.VMEM(total.shape, total.dtype),
            pltpu.VMEM(late.shape, late.dtype),
            pltpu.VMEM((2, rows, depth), late.dtype),
            pltpu.VMEM((rows, cols), jnp.bfloat16),
            COPIES((2 + 3 * pieces,)),
            COPIES((steps,)),
        ],
        compiler_params=pltpu.CompilerParams(vmem_limit_bytes=10 * MIB),
        cost_estimate=SMALL,
    )(keep_mask, total, late, *flat)


def on_grid(left, right, a_pattern, b_pattern, keep_mask):
    ring = [(2 * s + c, 2 * d + c) for s, d in ((0, 1), (1, 3), (3, 2), (2, 0)) for c in (0, 1)]
    on = lambda v: lax.ppermute(v, "col", ring)
    cross = lambda v: lax.ppermute(v, "col", [(i, i ^ 1) for i in range(8)])
    to_x = lambda v: lax.ppermute(v, "row", [(i, i ^ 1) for i in range(4)])
    to_y = lambda v: lax.ppermute(v, "row", [(i, i ^ 2) for i in range(4)])
    tied = lambda *v: lax.optimization_barrier(v)

    a, a0, a1, *b = masked(left, right, a_pattern.T, b_pattern.T)
    r1 = [on(a0), on(a1)]
    ea = cross(a)
    bx, by = [to_x(b[0]), None], [None, to_y(b[1])]
    r1[0], ea, bx[0], by[1], *b = tied(r1[0], ea, bx[0], by[1], *b)
    r2 = [on(r1[0])]
    e1 = [cross(r1[0])]
    bx[1], by[0] = to_x(b[1]), to_y(b[0])
    r1[1], e1[0] = tied(r1[1], e1[0])
    r2.append(on(r1[1]))
    e1.append(cross(r1[1]))
    r2[0], e1[1], bx[0], by[1], bx[1], by[0] = tied(r2[0], e1[1], bx[0], by[1], bx[1], by[0])
    r3 = [on(r2[0])]
    e2 = [cross(r2[0])]
    bd = [to_y(bx[0]), to_x(by[1])]
    r2[1], e2[0] = tied(r2[1], e2[0])
    r3.append(on(r2[1]))
    e2.append(cross(r2[1]))
    r3[0], e2[1], *bd = tied(r3[0], e2[1], *bd)
    total, late = early_slots((((a,), (ea,)), (r1, e1), (r2, e2)), (b, bx, by, bd))
    first = cross(r3[0])
    r3[1], first, total, late = tied(r3[1], first, total, late)
    return last_slot(keep_mask.T, total, late, (r3, [first, cross(r3[1])]))


def on_any(left, right, a_pattern, b_pattern, keep_mask):
    size = left.shape[0] // a_pattern.shape[0]
    wide = lambda v: jnp.repeat(jnp.repeat(v, size, axis=0), size, axis=1)
    left = left * wide(a_pattern).astype(left.dtype)
    right = right * wide(b_pattern).astype(right.dtype)
    n_row, n_col = lax.axis_size("row"), lax.axis_size("col")
    row, col = lax.axis_index("row"), lax.axis_index("col")
    step = lambda v, axis, n: lax.ppermute(v, axis, [(i, (i + 1) % n) for i in range(n)])
    every = jnp.zeros((n_row, *right.shape), right.dtype)
    for i in range(n_row):
        every = lax.dynamic_update_index_in_dim(every, right, (row - i) % n_row, 0)
        if i < n_row - 1:
            right = step(right, "row", n_row)
    every = every.reshape(n_col, -1, right.shape[1])
    total = jnp.zeros((left.shape[0], right.shape[1]), jnp.float32)
    for i in range(n_col):
        panel = lax.dynamic_index_in_dim(every, (col - i) % n_col, 0, keepdims=False)
        total += jnp.dot(left, panel, preferred_element_type=jnp.float32)
        if i < n_col - 1:
            left = step(left, "col", n_col)
    return (total * wide(keep_mask).astype(jnp.float32)).astype(jnp.bfloat16)


def on_device(left, right, a_pattern, b_pattern, keep_mask):
    tuned = (lax.axis_size("row"), lax.axis_size("col")) == (4, 8)
    return (on_grid if tuned else on_any)(left, right, a_pattern, b_pattern, keep_mask)


def solution(mesh):
    placed = (P("row", "col"),) * 5
    return jax.shard_map(on_device, mesh=mesh, in_specs=placed, out_specs=P("row", "col"), check_vma=False)
```

time: 87.1 us -> 81.5 us (0.936)
  starting transfers between devices: 13.2 us -> 19.7 us
  waiting for transfers between devices: 53 us -> 47.5 us
  Pallas kernels: 15.8 us -> 10.7 us
  local copies, waits for them, and re-layouts: 4.6 us -> 3.31 us
    ppermute x6, waiting for transfers between devices: 53 us -> 34 us  [on_grid(): on = lambda v: lax.ppermute(v, 'col', ring)]
    ppermute x1 -> x3, waiting for transfers between devices: 0.01 us -> 7.33 us  [on_grid(): to_x = lambda v: lax.ppermute(v, 'row', [(i, i ^ 1) for i in range(4)])]
    pallas_call x5 -> x3, Pallas kernels: 15.8 us -> 10.7 us  [the longest x1 4.49 us: early_slots(): pl.pallas_call(body, in_specs=specs, out_specs=[NEAR, NEAR], out_shape=[j...]
    ppermute x2 -> x3, waiting for transfers between devices: 0.01 us -> 4.29 us  [on_grid(): to_y = lambda v: lax.ppermute(v, 'row', [(i, i ^ 2) for i in range(4)])]
    ppermute x6, starting transfers between devices: 7.31 us -> 11 us  [on_grid(): on = lambda v: lax.ppermute(v, 'col', ring)]
    ppermute x2 -> x3, starting transfers between devices: 2.09 us -> 4.56 us  [on_grid(): to_y = lambda v: lax.ppermute(v, 'row', [(i, i ^ 2) for i in range(4)])]
    ppermute x8 -> x7, waiting for transfers between devices: 0.02 us -> 1.92 us  [on_grid(): cross = lambda v: lax.ppermute(v, 'col', [(i, i ^ 1) for i in range(8)])]
    unnamed x18 -> x8, local copies, waits for them, and re-layouts: 4.6 us -> 3.31 us
  transfers between devices with their start and end apart: 17 -> 19, of which waited for: 6 -> 13; matrix products, arithmetic and copies ran while one was open for 0% -> 0% of each run, Pallas kernels for 13% -> 6%
where the time goes in v3:
time: 81.5 us; the launch traced here: 81.2 us
  waiting for transfers between devices  47.5 us (58%)
  starting transfers between devices  19.7 us (24%)
  Pallas kernels  10.7 us (13%)
  local copies, waits for them, and re-layouts  3.31 us (4%)
    ppermute x6, waiting for transfers between devices, on_grid(): on = lambda v: lax.ppermute(v, 'col', ring)  34 us
    ppermute x6, starting transfers between devices, on_grid(): on = lambda v: lax.ppermute(v, 'col', ring)  11 us
    ppermute x3, waiting for transfers between devices, on_grid(): to_x = lambda v: lax.ppermute(v, 'row', [(i, i ^ 1) for i in range(4)])  7.33 us
    ppermute x3, starting transfers between devices, on_grid(): to_y = lambda v: lax.ppermute(v, 'row', [(i, i ^ 2) for i in range(4)])  4.56 us
    pallas_call x1, Pallas kernels, early_slots(): pl.pallas_call(body, in_specs=specs, out_specs=[NEAR, NEAR], out_shape=[j...  4.49 us
    ppermute x3, waiting for transfers between devices, on_grid(): to_y = lambda v: lax.ppermute(v, 'row', [(i, i ^ 2) for i in range(4)])  4.29 us
    ppermute x3, starting transfers between devices, on_grid(): to_x = lambda v: lax.ppermute(v, 'row', [(i, i ^ 1) for i in range(4)])  3.52 us
    pallas_call x1, Pallas kernels, masked(): pl.pallas_call(body, in_specs=[FAR] * 4, out_specs=[NEAR] * 5, out_shape=...  3.35 us
  transfers between devices with their start and end apart: 19, of which 13 were waited for; matrix products, arithmetic and copies ran while one was open for 0% of the time, Pallas kernels for 6%

profile of v3, /device:TPU:0, one launch (start us, length us, event | category | flops | bytes accessed | tf_op | source)
XLA Modules:
  0.0 81.2 jit_solution(273641396578672047)
XLA Ops:
  0.0 3.3 %shard_map.55 = (bf16[1024,512]{1,0:T(8,128)(2,1)}, bf16[512,512]{1,0:T(8,128)(2,1)}, bf16[512,512]{1,0:T(8,128)(2,1)}, bf16[512,512]{1,0:T(8,128)(2,1)}, bf16[512,512]{1,0:T(8,128)(2,1)}) custom-call(s32[4,8]{1,0:T(4,128)} %bitcast.4, s32[4,8]{1,0:T(4,128)} %bitcast.5, bf16[1024,512]{1,0:T(8,128)(2,1)} %refs_2_.1, bf16[1024,512]{1,0:T(8,128)(2,1)} %refs_3_.1), custom_call_target="tpu_custom_call" | custom-call | flops 1 | bytes 1 | tf_op jit(solution)/shard_map/pallas_call | solution.py:48
  3.4 0.5 collective-permute-start.2
  3.9 2.6 %collective-permute-start.1 = (bf16[512,512]{1,0:T(8,128)(2,1)}, bf16[512,512]{1,0:T(8,128)(2,1)S(1)}, u32[]{:S(2)}, u32[]{:S(2)}) collective-permute-start(bf16[512,512]{1,0:T(8,128)(2,1)} %get-tuple-element.37), channel_id=1, source_target_pairs={{0,2},{1,3},{2,6},{3,7},{6,4},{7,5},{4,0},{5,1},{8,10},{9,11},{10,... | collective-permute-start | bytes 1572872 | tf_op jit(solution)/shard_map/ppermute | solution.py:195
  6.5 1.5 %collective-permute-start.3 = (bf16[512,512]{1,0:T(8,128)(2,1)}, bf16[512,512]{1,0:T(8,128)(2,1)S(1)}, u32[]{:S(2)}, u32[]{:S(2)}) collective-permute-start(bf16[512,512]{1,0:T(8,128)(2,1)} %get-tuple-element.46.refs_0_), channel_id=1, source_target_pairs={{0,8},{8,0},{16,24},{24,16},{1,9},{9,1},{17,25},{25,17},{2,10},{10... | collective-permute-start | bytes 1572872 | tf_op jit(solution)/shard_map/ppermute | solution.py:197
  8.0 0.0 copy-start.3
  8.0 1.5 %collective-permute-start.4 = (bf16[512,512]{1,0:T(8,128)(2,1)}, bf16[512,512]{1,0:T(8,128)(2,1)S(1)}, u32[]{:S(2)}, u32[]{:S(2)}) collective-permute-start(bf16[512,512]{1,0:T(8,128)(2,1)} %get-tuple-element.45.refs_1_), channel_id=1, source_target_pairs={{0,16},{8,24},{16,0},{24,8},{1,17},{9,25},{17,1},{25,9},{2,18},{10... | collective-permute-start | bytes 1572872 | tf_op jit(solution)/shard_map/ppermute | solution.py:198
  9.5 2.6 %collective-permute-start = (bf16[512,512]{1,0:T(8,128)(2,1)}, bf16[512,512]{1,0:T(8,128)(2,1)S(1)}, u32[]{:S(2)}, u32[]{:S(2)}) collective-permute-start(bf16[512,512]{1,0:T(8,128)(2,1)} %get-tuple-element.36), channel_id=1, source_target_pairs={{0,2},{1,3},{2,6},{3,7},{6,4},{7,5},{4,0},{5,1},{8,10},{9,11},{10,... | collective-permute-start | bytes 1572872 | tf_op jit(solution)/shard_map/ppermute | solution.py:195
  12.1 8.4 %collective-permute-done.1.refs_10_ = bf16[512,512]{1,0:T(8,128)(2,1)S(1)} collective-permute-done((bf16[512,512]{1,0:T(8,128)(2,1)}, bf16[512,512]{1,0:T(8,128)(2,1)S(1)}, u32[]{:S(2)}, u32[]{:S(2)}) %collective-permute-start.1) | collective-permute-done | bytes 524320 | tf_op jit(solution)/shard_map/ppermute | solution.py:195
  20.5 0.2 collective-permute-done.3.refs_2_
  20.7 1.2 %collective-permute-done.4.refs_5_ = bf16[512,512]{1,0:T(8,128)(2,1)S(1)} collective-permute-done((bf16[512,512]{1,0:T(8,128)(2,1)}, bf16[512,512]{1,0:T(8,128)(2,1)S(1)}, u32[]{:S(2)}, u32[]{:S(2)}) %collective-permute-start.4) | collective-permute-done | bytes 524320 | tf_op jit(solution)/shard_map/ppermute | solution.py:198
  21.9 0.0 collective-permute-done.2.refs_9_
  21.9 0.0 collective-permute-start.5
  21.9 2.6 %collective-permute-start.7 = (bf16[512,512]{1,0:T(8,128)(2,1)S(1)}, bf16[512,512]{1,0:T(8,128)(2,1)S(1)}, u32[]{:S(2)}, u32[]{:S(2)}) collective-permute-start(bf16[512,512]{1,0:T(8,128)(2,1)S(1)} %collective-permute-done.1.refs_10_), channel_id=1, source_target_pairs={{0,2},{1,3},{2,6},{3,7},{6,4},{7,5},{4,0},{5,1},{8,10},{9,11},{10,... | collective-permute-start | bytes 1572872 | tf_op jit(solution)/shard_map/ppermute | solution.py:195
  24.5 0.5 collective-permute-start.9
  25.1 1.5 %collective-permute-start.10 = (bf16[512,512]{1,0:T(8,128)(2,1)}, bf16[512,512]{1,0:T(8,128)(2,1)S(1)}, u32[]{:S(2)}, u32[]{:S(2)}) collective-permute-start(bf16[512,512]{1,0:T(8,128)(2,1)} %get-tuple-element.46.refs_0_), channel_id=1, source_target_pairs={{0,16},{8,24},{16,0},{24,8},{1,17},{9,25},{17,1},{25,9},{2,18},{10... | collective-permute-start | bytes 1572872 | tf_op jit(solution)/shard_map/ppermute | solution.py:198
  26.6 5.2 %collective-permute-done.refs_11_ = bf16[512,512]{1,0:T(8,128)(2,1)S(1)} collective-permute-done((bf16[512,512]{1,0:T(8,128)(2,1)}, bf16[512,512]{1,0:T(8,128)(2,1)S(1)}, u32[]{:S(2)}, u32[]{:S(2)}) %collective-permute-start) | collective-permute-done | bytes 524320 | tf_op jit(solution)/shard_map/ppermute | solution.py:195
  31.7 0.0 collective-permute-done.5.refs_12_
  31.8 0.0 collective-permute-start.8
  31.8 1.1 %collective-permute-start.6 = (bf16[512,512]{1,0:T(8,128)(2,1)S(1)}, bf16[512,512]{1,0:T(8,128)(2,1)S(1)}, u32[]{:S(2)}, u32[]{:S(2)}) collective-permute-start(bf16[512,512]{1,0:T(8,128)(2,1)S(1)} %collective-permute-done.refs_11_), channel_id=1, source_target_pairs={{0,2},{1,3},{2,6},{3,7},{6,4},{7,5},{4,0},{5,1},{8,10},{9,11},{10,... | collective-permute-start | bytes 1572872 | tf_op jit(solution)/shard_map/ppermute | solution.py:195
  32.9 5.9 %collective-permute-done.9.refs_3_ = bf16[512,512]{1,0:T(8,128)(2,1)S(1)} collective-permute-done((bf16[512,512]{1,0:T(8,128)(2,1)}, bf16[512,512]{1,0:T(8,128)(2,1)S(1)}, u32[]{:S(2)}, u32[]{:S(2)}) %collective-permute-start.9) | collective-permute-done | bytes 524320 | tf_op jit(solution)/shard_map/ppermute | solution.py:197
  38.8 0.3 collective-permute-done.10.refs_4_
  39.0 3.9 %collective-permute-done.7.refs_14_ = bf16[512,512]{1,0:T(8,128)(2,1)S(1)} collective-permute-done((bf16[512,512]{1,0:T(8,128)(2,1)S(1)}, bf16[512,512]{1,0:T(8,128)(2,1)S(1)}, u32[]{:S(2)}, u32[]{:S(2)}) %collective-permute-start.7) | collective-permute-done | bytes 524320 | tf_op jit(solution)/shard_map/ppermute | solution.py:195
  43.0 0.0 collective-permute-done.8.refs_13_
  43.0 0.0 collective-permute-start.11
  43.0 1.0 %collective-permute-start.13 = (bf16[512,512]{1,0:T(8,128)(2,1)S(1)}, bf16[512,512]{1,0:T(8,128)(2,1)S(1)}, u32[]{:S(2)}, u32[]{:S(2)}) collective-permute-start(bf16[512,512]{1,0:T(8,128)(2,1)S(1)} %collective-permute-done.7.refs_14_), channel_id=1, source_target_pairs={{0,2},{1,3},{2,6},{3,7},{6,4},{7,5},{4,0},{5,1},{8,10},{9,11},{10,... | collective-permute-start | bytes 1572872 | tf_op jit(solution)/shard_map/ppermute | solution.py:195
  44.0 1.5 %collective-permute-start.15 = (bf16[512,512]{1,0:T(8,128)(2,1)S(1)}, bf16[512,512]{1,0:T(8,128)(2,1)S(1)}, u32[]{:S(2)}, u32[]{:S(2)}) collective-permute-start(bf16[512,512]{1,0:T(8,128)(2,1)S(1)} %collective-permute-done.3.refs_2_), channel_id=1, source_target_pairs={{0,16},{8,24},{16,0},{24,8},{1,17},{9,25},{17,1},{25,9},{2,18},{10... | collective-permute-start | bytes 1572872 | tf_op jit(solution)/shard_map/ppermute | solution.py:198
  45.6 1.5 %collective-permute-start.16 = (bf16[512,512]{1,0:T(8,128)(2,1)S(1)}, bf16[512,512]{1,0:T(8,128)(2,1)S(1)}, u32[]{:S(2)}, u32[]{:S(2)}) collective-permute-start(bf16[512,512]{1,0:T(8,128)(2,1)S(1)} %collective-permute-done.4.refs_5_), channel_id=1, source_target_pairs={{0,8},{8,0},{16,24},{24,16},{1,9},{9,1},{17,25},{25,17},{2,10},{10... | collective-permute-start | bytes 1572872 | tf_op jit(solution)/shard_map/ppermute | solution.py:197
  47.0 7.2 %collective-permute-done.6.refs_15_ = bf16[512,512]{1,0:T(8,128)(2,1)S(1)} collective-permute-done((bf16[512,512]{1,0:T(8,128)(2,1)S(1)}, bf16[512,512]{1,0:T(8,128)(2,1)S(1)}, u32[]{:S(2)}, u32[]{:S(2)}) %collective-permute-start.6) | collective-permute-done | bytes 524320 | tf_op jit(solution)/shard_map/ppermute | solution.py:195
  54.2 0.0 collective-permute-done.11.refs_16_
  54.2 0.0 collective-permute-start.14
  54.2 1.0 %collective-permute-start.12 = (bf16[512,512]{1,0:T(8,128)(2,1)S(1)}, bf16[512,512]{1,0:T(8,128)(2,1)S(1)}, u32[]{:S(2)}, u32[]{:S(2)}) collective-permute-start(bf16[512,512]{1,0:T(8,128)(2,1)S(1)} %collective-permute-done.6.refs_15_), channel_id=1, source_target_pairs={{0,2},{1,3},{2,6},{3,7},{6,4},{7,5},{4,0},{5,1},{8,10},{9,11},{10,... | collective-permute-start | bytes 1572872 | tf_op jit(solution)/shard_map/ppermute | solution.py:195
  55.3 2.8 %collective-permute-done.15.refs_6_ = bf16[512,512]{1,0:T(8,128)(2,1)S(1)} collective-permute-done((bf16[512,512]{1,0:T(8,128)(2,1)S(1)}, bf16[512,512]{1,0:T(8,128)(2,1)S(1)}, u32[]{:S(2)}, u32[]{:S(2)}) %collective-permute-start.15) | collective-permute-done | bytes 524320 | tf_op jit(solution)/shard_map/ppermute | solution.py:198
  58.1 1.2 %collective-permute-done.16.refs_7_ = bf16[512,512]{1,0:T(8,128)(2,1)S(1)} collective-permute-done((bf16[512,512]{1,0:T(8,128)(2,1)S(1)}, bf16[512,512]{1,0:T(8,128)(2,1)S(1)}, u32[]{:S(2)}, u32[]{:S(2)}) %collective-permute-start.16) | collective-permute-done | bytes 524320 | tf_op jit(solution)/shard_map/ppermute | solution.py:197
  59.3 6.1 %collective-permute-done.13.refs_0_ = bf16[512,512]{1,0:T(8,128)(2,1)S(1)} collective-permute-done((bf16[512,512]{1,0:T(8,128)(2,1)S(1)}, bf16[512,512]{1,0:T(8,128)(2,1)S(1)}, u32[]{:S(2)}, u32[]{:S(2)}) %collective-permute-start.13) | collective-permute-done | bytes 524320 | tf_op jit(solution)/shard_map/ppermute | solution.py:195
  65.5 0.0 collective-permute-done.14.refs_17_
  65.5 0.0 collective-permute-start.17
  65.5 0.0 copy-start
  65.5 1.2 %copy-done = bf16[1024,512]{1,0:T(8,128)(2,1)S(1)} copy-done((bf16[1024,512]{1,0:T(8,128)(2,1)S(1)}, bf16[1024,512]{1,0:T(8,128)(2,1)}, u32[]{:S(2)}) %copy-start) | copy-done | bytes 1048600
  66.7 0.0 copy-start.1
  66.7 1.0 %copy-done.1 = bf16[512,512]{1,0:T(8,128)(2,1)S(1)} copy-done((bf16[512,512]{1,0:T(8,128)(2,1)S(1)}, bf16[512,512]{1,0:T(8,128)(2,1)}, u32[]{:S(2)}) %copy-start.1) | copy-done | bytes 524312
  67.7 0.0 copy-start.2
  67.7 1.0 %copy-done.2 = bf16[512,512]{1,0:T(8,128)(2,1)S(1)} copy-done((bf16[512,512]{1,0:T(8,128)(2,1)S(1)}, bf16[512,512]{1,0:T(8,128)(2,1)}, u32[]{:S(2)}) %copy-start.2) | copy-done | bytes 524312
  68.8 4.5 %shard_map.56 = (f32[1024,512]{1,0:T(8,128)S(1)}, bf16[1024,512]{1,0:T(8,128)(2,1)S(1)}) custom-call(bf16[512,512]{1,0:T(8,128)(2,1)S(1)} %copy-done.1, bf16[512,512]{1,0:T(8,128)(2,1)S(1)} %copy-done.2, bf16[512,512]{1,0:T(8,128)(2,1)S(1)} %collective-permute-done.3.refs_2_, bf16[512,512]{1,0:T(8,128)(2,1)S(1)} %collective-permute-done.9.refs_3_, ...), custom_call_target="tpu_custom_call" | custom-call | flops 1 | bytes 1 | tf_op jit(solution)/shard_map/pallas_call | solution.py:116
  73.3 3.2 %collective-permute-done.12.refs_2_ = bf16[512,512]{1,0:T(8,128)(2,1)S(1)} collective-permute-done((bf16[512,512]{1,0:T(8,128)(2,1)S(1)}, bf16[512,512]{1,0:T(8,128)(2,1)S(1)}, u32[]{:S(2)}, u32[]{:S(2)}) %collective-permute-start.12) | collective-permute-done | bytes 524320 | tf_op jit(solution)/shard_map/ppermute | solution.py:195
  76.4 0.0 collective-permute-done.17.refs_1_
  76.4 0.0 collective-permute-start.18
  76.4 1.9 %collective-permute-done.18.refs_3_ = bf16[512,512]{1,0:T(8,128)(2,1)S(1)} collective-permute-done((bf16[512,512]{1,0:T(8,128)(2,1)S(1)}, bf16[512,512]{1,0:T(8,128)(2,1)S(1)}, u32[]{:S(2)}, u32[]{:S(2)}) %collective-permute-start.18) | collective-permute-done | bytes 524320 | tf_op jit(solution)/shard_map/ppermute | solution.py:196
  78.4 0.0 copy-done.3
  78.4 2.9 %shard_map.57 = bf16[1024,512]{1,0:T(8,128)(2,1)} custom-call(s32[4,8]{1,0:T(4,128)S(1)} %bitcast.3, f32[1024,512]{1,0:T(8,128)S(1)} %get-tuple-element.63.total_hbm, bf16[1024,512]{1,0:T(8,128)(2,1)S(1)} %get-tuple-element.64.late_hbm, bf16[512,512]{1,0:T(8,128)(2,1)S(1)} %collective-permute-done.13.refs_0_, ...), custom_call_target="tpu_custom_call" | custom-call | flops 1 | bytes 1 | tf_op jit(solution)/shard_map/pallas_call | solution.py:174
Async XLA Ops:
  3.4 18.6 %collective-permute-start.2 = (bf16[1024,512]{1,0:T(8,128)(2,1)}, bf16[1024,512]{1,0:T(8,128)(2,1)S(1)}, u32[]{:S(2)}, u32[]{:S(2)}) collective-permute-start(bf16[1024,512]{1,0:T(8,128)(2,1)} %get-tuple-element.38.refs_8_), channel_id=1, source_target_pairs={{0,1},{1,0},{2,3},{3,2},{4,5},{5,4},{6,7},{7,6},{8,9},{9,8},{10,11... | collective-permute-start | bytes 3145736 | tf_op jit(solution)/shard_map/ppermute | solution.py:196
  3.9 16.6 %collective-permute-start.1 = (bf16[512,512]{1,0:T(8,128)(2,1)}, bf16[512,512]{1,0:T(8,128)(2,1)S(1)}, u32[]{:S(2)}, u32[]{:S(2)}) collective-permute-start(bf16[512,512]{1,0:T(8,128)(2,1)} %get-tuple-element.37), channel_id=1, source_target_pairs={{0,2},{1,3},{2,6},{3,7},{6,4},{7,5},{4,0},{5,1},{8,10},{9,11},{10,... | collective-permute-start | bytes 1572872 | tf_op jit(solution)/shard_map/ppermute | solution.py:195
  6.5 14.2 %collective-permute-start.3 = (bf16[512,512]{1,0:T(8,128)(2,1)}, bf16[512,512]{1,0:T(8,128)(2,1)S(1)}, u32[]{:S(2)}, u32[]{:S(2)}) collective-permute-start(bf16[512,512]{1,0:T(8,128)(2,1)} %get-tuple-element.46.refs_0_), channel_id=1, source_target_pairs={{0,8},{8,0},{16,24},{24,16},{1,9},{9,1},{17,25},{25,17},{2,10},{10... | collective-permute-start | bytes 1572872 | tf_op jit(solution)/shard_map/ppermute | solution.py:197
  8.0 70.4 %copy-start.3 = (s32[8,4]{0,1:T(4,128)S(1)}, s32[8,4]{0,1:T(4,128)}, u32[]{:S(2)}) copy-start(s32[8,4]{0,1:T(4,128)} %param.9) | copy-start | bytes 388
  8.0 13.9 %collective-permute-start.4 = (bf16[512,512]{1,0:T(8,128)(2,1)}, bf16[512,512]{1,0:T(8,128)(2,1)S(1)}, u32[]{:S(2)}, u32[]{:S(2)}) collective-permute-start(bf16[512,512]{1,0:T(8,128)(2,1)} %get-tuple-element.45.refs_1_), channel_id=1, source_target_pairs={{0,16},{8,24},{16,0},{24,8},{1,17},{9,25},{17,1},{25,9},{2,18},{10... | collective-permute-start | bytes 1572872 | tf_op jit(solution)/shard_map/ppermute | solution.py:198
  9.5 22.2 %collective-permute-start = (bf16[512,512]{1,0:T(8,128)(2,1)}, bf16[512,512]{1,0:T(8,128)(2,1)S(1)}, u32[]{:S(2)}, u32[]{:S(2)}) collective-permute-start(bf16[512,512]{1,0:T(8,128)(2,1)} %get-tuple-element.36), channel_id=1, source_target_pairs={{0,2},{1,3},{2,6},{3,7},{6,4},{7,5},{4,0},{5,1},{8,10},{9,11},{10,... | collective-permute-start | bytes 1572872 | tf_op jit(solution)/shard_map/ppermute | solution.py:195
  21.9 9.8 %collective-permute-start.5 = (bf16[512,512]{1,0:T(8,128)(2,1)S(1)}, bf16[512,512]{1,0:T(8,128)(2,1)S(1)}, u32[]{:S(2)}, u32[]{:S(2)}) collective-permute-start(bf16[512,512]{1,0:T(8,128)(2,1)S(1)} %collective-permute-done.1.refs_10_), channel_id=1, source_target_pairs={{0,1},{1,0},{2,3},{3,2},{4,5},{5,4},{6,7},{7,6},{8,9},{9,8},{10,11... | collective-permute-start | bytes 1572872 | tf_op jit(solution)/shard_map/ppermute | solution.py:196
  21.9 21.0 %collective-permute-start.7 = (bf16[512,512]{1,0:T(8,128)(2,1)S(1)}, bf16[512,512]{1,0:T(8,128)(2,1)S(1)}, u32[]{:S(2)}, u32[]{:S(2)}) collective-permute-start(bf16[512,512]{1,0:T(8,128)(2,1)S(1)} %collective-permute-done.1.refs_10_), channel_id=1, source_target_pairs={{0,2},{1,3},{2,6},{3,7},{6,4},{7,5},{4,0},{5,1},{8,10},{9,11},{10,... | collective-permute-start | bytes 1572872 | tf_op jit(solution)/shard_map/ppermute | solution.py:195
  24.5 14.3 %collective-permute-start.9 = (bf16[512,512]{1,0:T(8,128)(2,1)}, bf16[512,512]{1,0:T(8,128)(2,1)S(1)}, u32[]{:S(2)}, u32[]{:S(2)}) collective-permute-start(bf16[512,512]{1,0:T(8,128)(2,1)} %get-tuple-element.45.refs_1_), channel_id=1, source_target_pairs={{0,8},{8,0},{16,24},{24,16},{1,9},{9,1},{17,25},{25,17},{2,10},{10... | collective-permute-start | bytes 1572872 | tf_op jit(solution)/shard_map/ppermute | solution.py:197
  25.1 14.0 %collective-permute-start.10 = (bf16[512,512]{1,0:T(8,128)(2,1)}, bf16[512,512]{1,0:T(8,128)(2,1)S(1)}, u32[]{:S(2)}, u32[]{:S(2)}) collective-permute-start(bf16[512,512]{1,0:T(8,128)(2,1)} %get-tuple-element.46.refs_0_), channel_id=1, source_target_pairs={{0,16},{8,24},{16,0},{24,8},{1,17},{9,25},{17,1},{25,9},{2,18},{10... | collective-permute-start | bytes 1572872 | tf_op jit(solution)/shard_map/ppermute | solution.py:198
  31.8 11.2 %collective-permute-start.8 = (bf16[512,512]{1,0:T(8,128)(2,1)S(1)}, bf16[512,512]{1,0:T(8,128)(2,1)S(1)}, u32[]{:S(2)}, u32[]{:S(2)}) collective-permute-start(bf16[512,512]{1,0:T(8,128)(2,1)S(1)} %collective-permute-done.refs_11_), channel_id=1, source_target_pairs={{0,1},{1,0},{2,3},{3,2},{4,5},{5,4},{6,7},{7,6},{8,9},{9,8},{10,11... | collective-permute-start | bytes 1572872 | tf_op jit(solution)/shard_map/ppermute | solution.py:196
  31.8 22.5 %collective-permute-start.6 = (bf16[512,512]{1,0:T(8,128)(2,1)S(1)}, bf16[512,512]{1,0:T(8,128)(2,1)S(1)}, u32[]{:S(2)}, u32[]{:S(2)}) collective-permute-start(bf16[512,512]{1,0:T(8,128)(2,1)S(1)} %collective-permute-done.refs_11_), channel_id=1, source_target_pairs={{0,2},{1,3},{2,6},{3,7},{6,4},{7,5},{4,0},{5,1},{8,10},{9,11},{10,... | collective-permute-start | bytes 1572872 | tf_op jit(solution)/shard_map/ppermute | solution.py:195
  43.0 11.2 %collective-permute-start.11 = (bf16[512,512]{1,0:T(8,128)(2,1)S(1)}, bf16[512,512]{1,0:T(8,128)(2,1)S(1)}, u32[]{:S(2)}, u32[]{:S(2)}) collective-permute-start(bf16[512,512]{1,0:T(8,128)(2,1)S(1)} %collective-permute-done.7.refs_14_), channel_id=1, source_target_pairs={{0,1},{1,0},{2,3},{3,2},{4,5},{5,4},{6,7},{7,6},{8,9},{9,8},{10,11... | collective-permute-start | bytes 1572872 | tf_op jit(solution)/shard_map/ppermute | solution.py:196
  43.0 22.5 %collective-permute-start.13 = (bf16[512,512]{1,0:T(8,128)(2,1)S(1)}, bf16[512,512]{1,0:T(8,128)(2,1)S(1)}, u32[]{:S(2)}, u32[]{:S(2)}) collective-permute-start(bf16[512,512]{1,0:T(8,128)(2,1)S(1)} %collective-permute-done.7.refs_14_), channel_id=1, source_target_pairs={{0,2},{1,3},{2,6},{3,7},{6,4},{7,5},{4,0},{5,1},{8,10},{9,11},{10,... | collective-permute-start | bytes 1572872 | tf_op jit(solution)/shard_map/ppermute | solution.py:195
  44.0 14.1 %collective-permute-start.15 = (bf16[512,512]{1,0:T(8,128)(2,1)S(1)}, bf16[512,512]{1,0:T(8,128)(2,1)S(1)}, u32[]{:S(2)}, u32[]{:S(2)}) collective-permute-start(bf16[512,512]{1,0:T(8,128)(2,1)S(1)} %collective-permute-done.3.refs_2_), channel_id=1, source_target_pairs={{0,16},{8,24},{16,0},{24,8},{1,17},{9,25},{17,1},{25,9},{2,18},{10... | collective-permute-start | bytes 1572872 | tf_op jit(solution)/shard_map/ppermute | solution.py:198
  45.6 13.8 %collective-permute-start.16 = (bf16[512,512]{1,0:T(8,128)(2,1)S(1)}, bf16[512,512]{1,0:T(8,128)(2,1)S(1)}, u32[]{:S(2)}, u32[]{:S(2)}) collective-permute-start(bf16[512,512]{1,0:T(8,128)(2,1)S(1)} %collective-permute-done.4.refs_5_), channel_id=1, source_target_pairs={{0,8},{8,0},{16,24},{24,16},{1,9},{9,1},{17,25},{25,17},{2,10},{10... | collective-permute-start | bytes 1572872 | tf_op jit(solution)/shard_map/ppermute | solution.py:197
  54.2 11.2 %collective-permute-start.14 = (bf16[512,512]{1,0:T(8,128)(2,1)S(1)}, bf16[512,512]{1,0:T(8,128)(2,1)S(1)}, u32[]{:S(2)}, u32[]{:S(2)}) collective-permute-start(bf16[512,512]{1,0:T(8,128)(2,1)S(1)} %collective-permute-done.6.refs_15_), channel_id=1, source_target_pairs={{0,1},{1,0},{2,3},{3,2},{4,5},{5,4},{6,7},{7,6},{8,9},{9,8},{10,11... | collective-permute-start | bytes 1572872 | tf_op jit(solution)/shard_map/ppermute | solution.py:196
  54.2 22.2 %collective-permute-start.12 = (bf16[512,512]{1,0:T(8,128)(2,1)S(1)}, bf16[512,512]{1,0:T(8,128)(2,1)S(1)}, u32[]{:S(2)}, u32[]{:S(2)}) collective-permute-start(bf16[512,512]{1,0:T(8,128)(2,1)S(1)} %collective-permute-done.6.refs_15_), channel_id=1, source_target_pairs={{0,2},{1,3},{2,6},{3,7},{6,4},{7,5},{4,0},{5,1},{8,10},{9,11},{10,... | collective-permute-start | bytes 1572872 | tf_op jit(solution)/shard_map/ppermute | solution.py:195
  65.5 11.0 %collective-permute-start.17 = (bf16[512,512]{1,0:T(8,128)(2,1)S(1)}, bf16[512,512]{1,0:T(8,128)(2,1)S(1)}, u32[]{:S(2)}, u32[]{:S(2)}) collective-permute-start(bf16[512,512]{1,0:T(8,128)(2,1)S(1)} %collective-permute-done.13.refs_0_), channel_id=1, source_target_pairs={{0,1},{1,0},{2,3},{3,2},{4,5},{5,4},{6,7},{7,6},{8,9},{9,8},{10,11... | collective-permute-start | bytes 1572872 | tf_op jit(solution)/shard_map/ppermute | solution.py:196
  65.5 1.2 %copy-start = (bf16[1024,512]{1,0:T(8,128)(2,1)S(1)}, bf16[1024,512]{1,0:T(8,128)(2,1)}, u32[]{:S(2)}) copy-start(bf16[1024,512]{1,0:T(8,128)(2,1)} %get-tuple-element.38.refs_8_) | copy-start | bytes 3145732
  66.7 1.0 %copy-start.1 = (bf16[512,512]{1,0:T(8,128)(2,1)S(1)}, bf16[512,512]{1,0:T(8,128)(2,1)}, u32[]{:S(2)}) copy-start(bf16[512,512]{1,0:T(8,128)(2,1)} %get-tuple-element.46.refs_0_) | copy-start | bytes 1572868
  67.7 1.0 %copy-start.2 = (bf16[512,512]{1,0:T(8,128)(2,1)S(1)}, bf16[512,512]{1,0:T(8,128)(2,1)}, u32[]{:S(2)}) copy-start(bf16[512,512]{1,0:T(8,128)(2,1)} %get-tuple-element.45.refs_1_) | copy-start | bytes 1572868
  76.4 1.9 %collective-permute-start.18 = (bf16[512,512]{1,0:T(8,128)(2,1)S(1)}, bf16[512,512]{1,0:T(8,128)(2,1)S(1)}, u32[]{:S(2)}, u32[]{:S(2)}) collective-permute-start(bf16[512,512]{1,0:T(8,128)(2,1)S(1)} %collective-permute-done.12.refs_2_), channel_id=1, source_target_pairs={{0,1},{1,0},{2,3},{3,2},{4,5},{5,4},{6,7},{7,6},{8,9},{9,8},{10,11... | collective-permute-start | bytes 1572872 | tf_op jit(solution)/shard_map/ppermute | solution.py:196

commit v4 on v3

--- a/solution.py
+++ b/solution.py
@@ -19,44 +19,42 @@
         yield p, q, (slice(p * size, (p + 1) * size), slice(q * size, (q + 1) * size))
 
 
-def masked(left, right, a_pattern, b_pattern):
-    bcols, brows = a_pattern.shape
-    rows, cols = left.shape
-    size, half, tall = rows // brows, brows // 2, rows // 2
+def masked(pieces):
+    n = len(pieces)
+    sources = {}
+    for shard, pattern, _, _ in pieces:
+        sources.setdefault(id(shard), (len(sources), shard, pattern))
+    k = len(sources)
+    bcols, brows = pieces[0][1].shape
+    rows, cols = pieces[0][0].shape
+    size = rows // brows
 
     def body(*refs):
-        (a_hbm, b_hbm, left_hbm, right_hbm), outs, (x_ref, pat_ref, sems) = refs[:4], refs[4:-3], refs[-3:]
-        moves = [(a_hbm, pat_ref.at[0]), (b_hbm, pat_ref.at[1])]
-        for s, x_hbm in enumerate((left_hbm, right_hbm)):
-            moves += [(x_hbm.at[i * tall : (i + 1) * tall], x_ref.at[s, i]) for i in (0, 1)]
-        copies = [pltpu.make_async_copy(s, d, sems.at[i]) for i, (s, d) in enumerate(moves)]
+        shards, patterns, outs, (pat_ref, sems), held = refs[:k], refs[k : 2 * k], refs[2 * k : 2 * k + n], refs[-2:], refs[2 * k + n : -2]
+        copies = [pltpu.make_async_copy(patterns[s], pat_ref.at[s], sems.at[s]) for s in range(k)]
+        for i, (shard, _, first, last) in enumerate(pieces):
+            there = shards[sources[id(shard)][0]].at[first:last]
+            copies.append(pltpu.make_async_copy(there, held[i], sems.at[k + i]))
         for copy in copies:
             copy.start()
-        for copy in copies[:2]:
+        for copy in copies[:k]:
             copy.wait()
-        for s in (0, 1):
-            for i in (0, 1):
-                copies[2 + 2 * s + i].wait()
-                for p, q, at in cells(half, bcols, size):
-                    stored = pat_ref[s, q, i * half + p] != 0
-                    block = jnp.where(stored, x_ref[(s, i, *at)], jnp.zeros((), left.dtype))
-                    outs[1 + 2 * s + i][at] = block
-                    if s == 0:
-                        outs[0][i * tall + at[0].start : i * tall + at[0].stop, at[1]] = block
-
-    part = jax.ShapeDtypeStruct((tall, cols), left.dtype)
+        for i, (shard, _, first, last) in enumerate(pieces):
+            copies[k + i].wait()
+            for p, q, at in cells((last - first) // size, bcols, size):
+                stored = pat_ref[sources[id(shard)][0], q, first // size + p] != 0
+                outs[i][at] = jnp.where(stored, held[i][at], jnp.zeros((), outs[i].dtype))
+
+    shapes = [jax.ShapeDtypeStruct((last - first, cols), shard.dtype) for shard, _, first, last in pieces]
     return pl.pallas_call(
         body,
-        in_specs=[FAR] * 4,
-        out_specs=[NEAR] * 5,
-        out_shape=[jax.ShapeDtypeStruct(left.shape, left.dtype)] + [part] * 4,
-        scratch_shapes=[
-            pltpu.VMEM((2, 2, tall, cols), left.dtype),
-            pltpu.SMEM((2, *a_pattern.shape), jnp.int32),
-            COPIES((6,)),
-        ],
+        in_specs=[FAR] * (2 * k),
+        out_specs=[NEAR] * n,
+        out_shape=shapes,
+        scratch_shapes=[pltpu.VMEM(v.shape, v.dtype) for v in shapes]
+        + [pltpu.SMEM((k, bcols, brows), jnp.int32), COPIES((k + n,))],
         cost_estimate=SMALL,
-    )(a_pattern, b_pattern, left, right)
+    )(*(v[1] for v in sources.values()), *(v[2] for v in sources.values()))
 
 
 def where_now():
@@ -128,44 +126,41 @@
     )(*flat)
 
 
-def last_slot(keep_mask, total, late, panels):
+def last_slot(first, keep_mask, total, late, mine, other, product=None):
     rows, cols = total.shape
-    tall, depth = panels[0][0].shape
+    tall, depth = mine.shape
     size = rows // keep_mask.shape[1]
     tile = 256
-    per, steps, pieces = tile // size, rows // tile, rows // tall
-    flat = [v for pair in zip(*panels) for v in pair]
-
-    def body(keep_hbm, total_hbm, late_hbm, *refs):
-        ins, out_hbm = refs[: len(flat)], refs[len(flat)]
-        keep_ref, total_ref, late_ref, held, out_ref, sems, out_sems = refs[len(flat) + 1 :]
-        load = lambda i, s, d: pltpu.make_async_copy(s, d, sems.at[i])
-        copies = [load(0, late_hbm, late_ref), load(1, keep_hbm, keep_ref)]
-        for i in range(pieces):
-            some = slice(i * tall, (i + 1) * tall)
-            copies.append(load(2 + 3 * i, total_hbm.at[some], total_ref.at[some]))
-            copies.append(load(3 + 3 * i, ins[2 * i], held.at[0, some]))
-            copies.append(load(4 + 3 * i, ins[2 * i + 1], held.at[1, some]))
+    per, steps = tile // size, tall // tile
+    given = () if product is None else (product,)
+
+    def body(keep_hbm, total_hbm, late_hbm, mine_hbm, other_hbm, *refs):
+        out_hbm, keep_ref, total_ref, late_ref, held, out_ref, sems, out_sems = refs[len(given) :]
+        moves = [
+            (late_hbm, late_ref),
+            (mine_hbm, held.at[0]),
+            (other_hbm, held.at[1]),
+            (total_hbm.at[first : first + tall], total_ref),
+            (keep_hbm, keep_ref),
+        ]
+        copies = [pltpu.make_async_copy(s, d, sems.at[i]) for i, (s, d) in enumerate(moves)]
         for copy in copies:
             copy.start()
         core = lax.axis_index("col") % 2
-        for copy in copies[:2]:
+        for copy in copies:
             copy.wait()
         writes = []
         for m in range(steps):
-            if m * tile % tall == 0:
-                i = m * tile // tall
-                for copy in copies[2 + 3 * i : 5 + 3 * i]:
-                    copy.wait()
             some = slice(m * tile, (m + 1) * tile)
             near = late_ref[pl.ds(pl.multiple_of(core * depth, depth), depth), :]
             far = late_ref[pl.ds(pl.multiple_of((1 - core) * depth, depth), depth), :]
             sums = total_ref[some, :] + jnp.dot(held[0, some, :], near, preferred_element_type=jnp.float32)
             sums += jnp.dot(held[1, some, :], far, preferred_element_type=jnp.float32)
             for p, q, at in cells(per, cols // size, size):
-                kept = keep_ref[q, m * per + p].astype(jnp.float32)
+                kept = keep_ref[q, first // size + m * per + p].astype(jnp.float32)
                 out_ref[m * tile + at[0].start : m * tile + at[0].stop, at[1]] = (sums[at] * kept).astype(out_ref.dtype)
-            write = pltpu.make_async_copy(out_ref.at[some], out_hbm.at[some], out_sems.at[m])
+            there = slice(first + m * tile, first + (m + 1) * tile)
+            write = pltpu.make_async_copy(out_ref.at[some], out_hbm.at[there], out_sems.at[m])
             write.start()
             writes.append(write)
         for write in writes:
@@ -173,21 +168,22 @@
 
     return pl.pallas_call(
         body,
-        in_specs=[FAR] + [HOME] * 2 + [FAR] * len(flat),
-        out_specs=FAR,
+        in_specs=[FAR] + [HOME] * 2 + [FAR] * 2 + [HOME] * len(given),
+        out_specs=HOME,
         out_shape=jax.ShapeDtypeStruct((rows, cols), jnp.bfloat16),
         scratch_shapes=[
             pltpu.SMEM(keep_mask.shape, jnp.int32),
-            pltpu.VMEM(total.shape, total.dtype),
+            pltpu.VMEM((tall, cols), total.dtype),
             pltpu.VMEM(late.shape, late.dtype),
-            pltpu.VMEM((2, rows, depth), late.dtype),
-            pltpu.VMEM((rows, cols), jnp.bfloat16),
-            COPIES((2 + 3 * pieces,)),
+            pltpu.VMEM((2, tall, depth), late.dtype),
+            pltpu.VMEM((tall, cols), jnp.bfloat16),
+            COPIES((5,)),
             COPIES((steps,)),
         ],
+        input_output_aliases={5: 0} if given else {},
         compiler_params=pltpu.CompilerParams(vmem_limit_bytes=10 * MIB),
         cost_estimate=SMALL,
-    )(keep_mask, total, late, *flat)
+    )(keep_mask, total, late, mine, other, *given)
 
 
 def on_grid(left, right, a_pattern, b_pattern, keep_mask):
@@ -198,29 +194,32 @@
     to_y = lambda v: lax.ppermute(v, "row", [(i, i ^ 2) for i in range(4)])
     tied = lambda *v: lax.optimization_barrier(v)
 
-    a, a0, a1, *b = masked(left, right, a_pattern.T, b_pattern.T)
+    rows = left.shape[0]
+    half = rows // 2
+    (a0,) = masked([(left, a_pattern.T, 0, half)])
+    left, a0 = tied(left, a0)
+    a1, b = masked([(left, a_pattern.T, half, rows), (right, b_pattern.T, 0, rows)])
     r1 = [on(a0), on(a1)]
-    ea = cross(a)
-    bx, by = [to_x(b[0]), None], [None, to_y(b[1])]
-    r1[0], ea, bx[0], by[1], *b = tied(r1[0], ea, bx[0], by[1], *b)
+    bx, by = to_x(b), to_y(b)
+    ea = [cross(a0)]
+    r1[0], ea[0], a1 = tied(r1[0], ea[0], a1)
     r2 = [on(r1[0])]
+    ea.append(cross(a1))
+    r1[1], ea[1], bx, by, r1[0] = tied(r1[1], ea[1], bx, by, r1[0])
+    r2.append(on(r1[1]))
     e1 = [cross(r1[0])]
-    bx[1], by[0] = to_x(b[1]), to_y(b[0])
-    r1[1], e1[0] = tied(r1[1], e1[0])
-    r2.append(on(r1[1]))
+    bd = [to_y(bx[:half]), to_x(by[half:])]
+    r2[0], e1[0], r1[1] = tied(r2[0], e1[0], r1[1])
+    r3 = [on(r2[0])]
     e1.append(cross(r1[1]))
-    r2[0], e1[1], bx[0], by[1], bx[1], by[0] = tied(r2[0], e1[1], bx[0], by[1], bx[1], by[0])
-    r3 = [on(r2[0])]
-    e2 = [cross(r2[0])]
-    bd = [to_y(bx[0]), to_x(by[1])]
-    r2[1], e2[0] = tied(r2[1], e2[0])
+    r2[1], e1[1], r2[0], *bd = tied(r2[1], e1[1], r2[0], *bd)
     r3.append(on(r2[1]))
-    e2.append(cross(r2[1]))
-    r3[0], e2[1], *bd = tied(r3[0], e2[1], *bd)
-    total, late = early_slots((((a,), (ea,)), (r1, e1), (r2, e2)), (b, bx, by, bd))
-    first = cross(r3[0])
-    r3[1], first, total, late = tied(r3[1], first, total, late)
-    return last_slot(keep_mask.T, total, late, (r3, [first, cross(r3[1])]))
+    e2 = [cross(v) for v in r2]
+    r3[0], *e2 = tied(r3[0], *e2)
+    total, late = early_slots((((a0, a1), ea), (r1, e1), (r2, e2)), ((b,), (bx,), (by,), bd))
+    r3[1], total, late = tied(r3[1], total, late)
+    product = last_slot(0, keep_mask.T, total, late, r3[0], cross(r3[0]))
+    return last_slot(half, keep_mask.T, total, late, r3[1], cross(r3[1]), product)
 
 
 def on_any(left, right, a_pattern, b_pattern, keep_mask):

time: 81.5 us -> 79.2 us (0.972)
  Pallas kernels: 10.7 us -> 14.5 us
  local copies, waits for them, and re-layouts: 3.31 us -> 0.09 us
  waiting for transfers between devices: 47.5 us -> 45.4 us
    ppermute x3 -> x2, waiting for transfers between devices: 4.29 us -> 8.07 us  [on_grid(): to_y = lambda v: lax.ppermute(v, 'row', [(i, i ^ 2) for i in range(4)])]
    unnamed x8, local copies, waits for them, and re-layouts: 3.31 us -> 0.02 us
    pallas_call x2 -> x4, Pallas kernels: 6.22 us -> 9.34 us  [the longest x2 4.82 us: masked(): pl.pallas_call(body, in_specs=[FAR] * (2 * k), out_specs=[NEAR] * n, out_...]
    ppermute x3 -> x2, waiting for transfers between devices: 7.33 us -> 4.87 us  [on_grid(): to_x = lambda v: lax.ppermute(v, 'row', [(i, i ^ 1) for i in range(4)])]
    ppermute x6, starting transfers between devices: 11 us -> 13.1 us  [on_grid(): on = lambda v: lax.ppermute(v, 'col', ring)]
    ppermute x7 -> x8, waiting for transfers between devices: 1.92 us -> 0.02 us  [on_grid(): cross = lambda v: lax.ppermute(v, 'col', [(i, i ^ 1) for i in range(8)])]
    ppermute x6, waiting for transfers between devices: 34 us -> 32.4 us  [on_grid(): on = lambda v: lax.ppermute(v, 'col', ring)]
    ppermute x3 -> x2, starting transfers between devices: 4.56 us -> 3.1 us  [on_grid(): to_y = lambda v: lax.ppermute(v, 'row', [(i, i ^ 2) for i in range(4)])]
  transfers between devices with their start and end apart: 19 -> 18, of which waited for: 13 -> 10; matrix products, arithmetic and copies ran while one was open for 0% -> 0% of each run, Pallas kernels for 6% -> 13%
where the time goes in v4:
time: 79.2 us; the launch traced here: 79 us
  waiting for transfers between devices  45.4 us (57%)
  starting transfers between devices  18.9 us (24%)
  Pallas kernels  14.5 us (18%)
    ppermute x6, waiting for transfers between devices, on_grid(): on = lambda v: lax.ppermute(v, 'col', ring)  32.4 us
    ppermute x6, starting transfers between devices, on_grid(): on = lambda v: lax.ppermute(v, 'col', ring)  13.1 us
    ppermute x2, waiting for transfers between devices, on_grid(): to_y = lambda v: lax.ppermute(v, 'row', [(i, i ^ 2) for i in range(4)])  8.07 us
    pallas_call x1, Pallas kernels, early_slots(): pl.pallas_call(body, in_specs=specs, out_specs=[NEAR, NEAR], out_shape=[j...  5.15 us
    ppermute x2, waiting for transfers between devices, on_grid(): to_x = lambda v: lax.ppermute(v, 'row', [(i, i ^ 1) for i in range(4)])  4.87 us
    pallas_call x2, Pallas kernels, masked(): pl.pallas_call(body, in_specs=[FAR] * (2 * k), out_specs=[NEAR] * n, out_...  4.82 us
    pallas_call x2, Pallas kernels, last_slot(): pl.pallas_call(body, in_specs=[FAR] + [HOME] * 2 + [FAR] * 2 + [HOME] * l...  4.51 us
    ppermute x2, starting transfers between devices, on_grid(): to_y = lambda v: lax.ppermute(v, 'row', [(i, i ^ 2) for i in range(4)])  3.1 us
  transfers between devices with their start and end apart: 18, of which 10 were waited for; matrix products, arithmetic and copies ran while one was open for 0% of the time, Pallas kernels for 13%

profile of v4, /device:TPU:0, one launch (start us, length us, event | category | flops | bytes accessed | tf_op | source)
XLA Modules:
  0.0 79.0 jit_solution(14979086574642145148)
XLA Ops:
  0.0 2.0 %shard_map.55.refs_5_ = bf16[512,512]{1,0:T(8,128)(2,1)} custom-call(bf16[1024,512]{1,0:T(8,128)(2,1)} %refs_0_.2, s32[4,8]{1,0:T(4,128)} %bitcast.5), custom_call_target="tpu_custom_call" | custom-call | flops 1 | bytes 1 | tf_op jit(solution)/shard_map/pallas_call | solution.py:49
  2.0 3.1 %collective-permute-start.1 = (bf16[512,512]{1,0:T(8,128)(2,1)}, bf16[512,512]{1,0:T(8,128)(2,1)S(1)}, u32[]{:S(2)}, u32[]{:S(2)}) collective-permute-start(bf16[512,512]{1,0:T(8,128)(2,1)} %shard_map.55.refs_5_), channel_id=1, source_target_pairs={{0,2},{1,3},{2,6},{3,7},{6,4},{7,5},{4,0},{5,1},{8,10},{9,11},{10,... | collective-permute-start | bytes 1572872 | tf_op jit(solution)/shard_map/ppermute | solution.py:191
  5.1 0.0 collective-permute-start.2
  5.1 0.0 copy-start
  5.1 2.9 %shard_map.56 = (bf16[512,512]{1,0:T(8,128)(2,1)}, bf16[1024,512]{1,0:T(8,128)(2,1)}) custom-call(bf16[1024,512]{1,0:T(8,128)(2,1)} %refs_0_.2, bf16[1024,512]{1,0:T(8,128)(2,1)} %refs_1_.1, s32[4,8]{1,0:T(4,128)} %bitcast.6, s32[4,8]{1,0:T(4,128)} %bitcast.7), custom_call_target="tpu_custom_call" | custom-call | flops 1 | bytes 1 | tf_op jit(solution)/shard_map/pallas_call | solution.py:49
  7.9 0.0 copy-start.1
  7.9 0.0 copy-start.2
  7.9 1.6 %collective-permute-start.4 = (bf16[1024,512]{1,0:T(8,128)(2,1)}, bf16[1024,512]{1,0:T(8,128)(2,1)S(1)}, u32[]{:S(2)}, u32[]{:S(2)}) collective-permute-start(bf16[1024,512]{1,0:T(8,128)(2,1)} %get-tuple-element.37.refs_0_), channel_id=1, source_target_pairs={{0,8},{8,0},{16,24},{24,16},{1,9},{9,1},{17,25},{25,17},{2,10},{10... | collective-permute-start | bytes 3145736 | tf_op jit(solution)/shard_map/ppermute | solution.py:193
  9.5 1.5 %collective-permute-start.5 = (bf16[1024,512]{1,0:T(8,128)(2,1)}, bf16[1024,512]{1,0:T(8,128)(2,1)S(1)}, u32[]{:S(2)}, u32[]{:S(2)}) collective-permute-start(bf16[1024,512]{1,0:T(8,128)(2,1)} %get-tuple-element.37.refs_0_), channel_id=1, source_target_pairs={{0,16},{8,24},{16,0},{24,8},{1,17},{9,25},{17,1},{25,9},{2,18},{10... | collective-permute-start | bytes 3145736 | tf_op jit(solution)/shard_map/ppermute | solution.py:194
  11.0 2.6 %collective-permute-start = (bf16[512,512]{1,0:T(8,128)(2,1)}, bf16[512,512]{1,0:T(8,128)(2,1)S(1)}, u32[]{:S(2)}, u32[]{:S(2)}) collective-permute-start(bf16[512,512]{1,0:T(8,128)(2,1)} %get-tuple-element.36.refs_6_), channel_id=1, source_target_pairs={{0,2},{1,3},{2,6},{3,7},{6,4},{7,5},{4,0},{5,1},{8,10},{9,11},{10,... | collective-permute-start | bytes 1572872 | tf_op jit(solution)/shard_map/ppermute | solution.py:191
  13.6 5.4 %collective-permute-done.1.refs_9_ = bf16[512,512]{1,0:T(8,128)(2,1)S(1)} collective-permute-done((bf16[512,512]{1,0:T(8,128)(2,1)}, bf16[512,512]{1,0:T(8,128)(2,1)S(1)}, u32[]{:S(2)}, u32[]{:S(2)}) %collective-permute-start.1) | collective-permute-done | bytes 524320 | tf_op jit(solution)/shard_map/ppermute | solution.py:191
  19.0 0.0 collective-permute-done.2.refs_7_
  19.0 0.0 collective-permute-start.3
  19.0 1.3 %collective-permute-start.7 = (bf16[512,512]{1,0:T(8,128)(2,1)S(1)}, bf16[512,512]{1,0:T(8,128)(2,1)S(1)}, u32[]{:S(2)}, u32[]{:S(2)}) collective-permute-start(bf16[512,512]{1,0:T(8,128)(2,1)S(1)} %collective-permute-done.1.refs_9_), channel_id=1, source_target_pairs={{0,2},{1,3},{2,6},{3,7},{6,4},{7,5},{4,0},{5,1},{8,10},{9,11},{10,... | collective-permute-start | bytes 1572872 | tf_op jit(solution)/shard_map/ppermute | solution.py:191
  20.3 10.0 %collective-permute-done.refs_10_ = bf16[512,512]{1,0:T(8,128)(2,1)S(1)} collective-permute-done((bf16[512,512]{1,0:T(8,128)(2,1)}, bf16[512,512]{1,0:T(8,128)(2,1)S(1)}, u32[]{:S(2)}, u32[]{:S(2)}) %collective-permute-start) | collective-permute-done | bytes 524320 | tf_op jit(solution)/shard_map/ppermute | solution.py:191
  30.3 0.0 collective-permute-done.3.refs_8_
  30.3 3.5 %collective-permute-done.4.refs_1_ = bf16[1024,512]{1,0:T(8,128)(2,1)S(1)} collective-permute-done((bf16[1024,512]{1,0:T(8,128)(2,1)}, bf16[1024,512]{1,0:T(8,128)(2,1)S(1)}, u32[]{:S(2)}, u32[]{:S(2)}) %collective-permute-start.4) | collective-permute-done | bytes 1048608 | tf_op jit(solution)/shard_map/ppermute | solution.py:193
  33.8 1.2 %collective-permute-done.5.refs_2_ = bf16[1024,512]{1,0:T(8,128)(2,1)S(1)} collective-permute-done((bf16[1024,512]{1,0:T(8,128)(2,1)}, bf16[1024,512]{1,0:T(8,128)(2,1)S(1)}, u32[]{:S(2)}, u32[]{:S(2)}) %collective-permute-start.5) | collective-permute-done | bytes 1048608 | tf_op jit(solution)/shard_map/ppermute | solution.py:194
  35.0 0.0 collective-permute-start.8
  35.0 1.6 %collective-permute-start.10 = (bf16[512,512]{1,0:T(8,128)(2,1)S(1)}, bf16[512,512]{1,0:T(8,128)(2,1)S(1)}, u32[]{:S(2)}, u32[]{:S(2)}) collective-permute-start(bf16[512,512]{1,0:T(8,128)(2,1)S(1)} %slice.6), channel_id=1, source_target_pairs={{0,16},{8,24},{16,0},{24,8},{1,17},{9,25},{17,1},{25,9},{2,18},{10... | collective-permute-start | bytes 1572872 | tf_op jit(solution)/shard_map/ppermute | solution.py:194
  36.7 0.0 copy-start.3
  36.7 0.6 collective-permute-start.11
  37.3 2.6 %collective-permute-start.6 = (bf16[512,512]{1,0:T(8,128)(2,1)S(1)}, bf16[512,512]{1,0:T(8,128)(2,1)S(1)}, u32[]{:S(2)}, u32[]{:S(2)}) collective-permute-start(bf16[512,512]{1,0:T(8,128)(2,1)S(1)} %collective-permute-done.refs_10_), channel_id=1, source_target_pairs={{0,2},{1,3},{2,6},{3,7},{6,4},{7,5},{4,0},{5,1},{8,10},{9,11},{10,... | collective-permute-start | bytes 1572872 | tf_op jit(solution)/shard_map/ppermute | solution.py:191
  39.9 0.8 %collective-permute-done.7.refs_13_ = bf16[512,512]{1,0:T(8,128)(2,1)S(1)} collective-permute-done((bf16[512,512]{1,0:T(8,128)(2,1)S(1)}, bf16[512,512]{1,0:T(8,128)(2,1)S(1)}, u32[]{:S(2)}, u32[]{:S(2)}) %collective-permute-start.7) | collective-permute-done | bytes 524320 | tf_op jit(solution)/shard_map/ppermute | solution.py:191
  40.7 0.0 collective-permute-done.8.refs_11_
  40.7 0.0 collective-permute-start.9
  40.7 1.9 %collective-permute-start.13 = (bf16[512,512]{1,0:T(8,128)(2,1)S(1)}, bf16[512,512]{1,0:T(8,128)(2,1)S(1)}, u32[]{:S(2)}, u32[]{:S(2)}) collective-permute-start(bf16[512,512]{1,0:T(8,128)(2,1)S(1)} %collective-permute-done.7.refs_13_), channel_id=1, source_target_pairs={{0,2},{1,3},{2,6},{3,7},{6,4},{7,5},{4,0},{5,1},{8,10},{9,11},{10,... | collective-permute-start | bytes 1572872 | tf_op jit(solution)/shard_map/ppermute | solution.py:191
  42.6 6.9 %collective-permute-done.10.refs_3_ = bf16[512,512]{1,0:T(8,128)(2,1)S(1)} collective-permute-done((bf16[512,512]{1,0:T(8,128)(2,1)S(1)}, bf16[512,512]{1,0:T(8,128)(2,1)S(1)}, u32[]{:S(2)}, u32[]{:S(2)}) %collective-permute-start.10) | collective-permute-done | bytes 524320 | tf_op jit(solution)/shard_map/ppermute | solution.py:194
  49.4 1.4 %collective-permute-done.11.refs_4_ = bf16[512,512]{1,0:T(8,128)(2,1)S(1)} collective-permute-done((bf16[512,512]{1,0:T(8,128)(2,1)S(1)}, bf16[512,512]{1,0:T(8,128)(2,1)S(1)}, u32[]{:S(2)}, u32[]{:S(2)}) %collective-permute-start.11) | collective-permute-done | bytes 524320 | tf_op jit(solution)/shard_map/ppermute | solution.py:193
  50.8 2.2 %collective-permute-done.6.refs_14_ = bf16[512,512]{1,0:T(8,128)(2,1)S(1)} collective-permute-done((bf16[512,512]{1,0:T(8,128)(2,1)S(1)}, bf16[512,512]{1,0:T(8,128)(2,1)S(1)}, u32[]{:S(2)}, u32[]{:S(2)}) %collective-permute-start.6) | collective-permute-done | bytes 524320 | tf_op jit(solution)/shard_map/ppermute | solution.py:191
  53.0 0.0 collective-permute-done.9.refs_12_
  53.0 0.0 collective-permute-start.14
  53.0 0.5 collective-permute-start.15
  53.5 1.7 %collective-permute-start.12 = (bf16[512,512]{1,0:T(8,128)(2,1)S(1)}, bf16[512,512]{1,0:T(8,128)(2,1)S(1)}, u32[]{:S(2)}, u32[]{:S(2)}) collective-permute-start(bf16[512,512]{1,0:T(8,128)(2,1)S(1)} %collective-permute-done.6.refs_14_), channel_id=1, source_target_pairs={{0,2},{1,3},{2,6},{3,7},{6,4},{7,5},{4,0},{5,1},{8,10},{9,11},{10,... | collective-permute-start | bytes 1572872 | tf_op jit(solution)/shard_map/ppermute | solution.py:191
  55.2 9.0 %collective-permute-done.13.mine_hbm = bf16[512,512]{1,0:T(8,128)(2,1)S(1)} collective-permute-done((bf16[512,512]{1,0:T(8,128)(2,1)S(1)}, bf16[512,512]{1,0:T(8,128)(2,1)S(1)}, u32[]{:S(2)}, u32[]{:S(2)}) %collective-permute-start.13) | collective-permute-done | bytes 524320 | tf_op jit(solution)/shard_map/ppermute | solution.py:191
  64.2 0.0 collective-permute-done.14.refs_15_
  64.2 0.0 collective-permute-done.15.refs_16_
  64.2 0.0 collective-permute-start.17
  64.2 0.0 copy-done
  64.2 0.0 copy-done.1
  64.2 0.0 copy-done.2
  64.3 5.1 %shard_map.57 = (f32[1024,512]{1,0:T(8,128)S(1)}, bf16[1024,512]{1,0:T(8,128)(2,1)S(1)}) custom-call(bf16[1024,512]{1,0:T(8,128)(2,1)S(1)} %copy-done.1, bf16[1024,512]{1,0:T(8,128)(2,1)S(1)} %collective-permute-done.4.refs_1_, bf16[1024,512]{1,0:T(8,128)(2,1)S(1)} %collective-permute-done.5.refs_2_, bf16[512,512]{1,0:T(8,128)(2,1)S(1)} %collective-permute-done.10.refs_3_, ...), custom_call_target="tpu_custom_call" | custom-call | flops 1 | bytes 1 | tf_op jit(solution)/shard_map/pallas_call | solution.py:114
  69.4 5.0 %collective-permute-done.12.mine_hbm = bf16[512,512]{1,0:T(8,128)(2,1)S(1)} collective-permute-done((bf16[512,512]{1,0:T(8,128)(2,1)S(1)}, bf16[512,512]{1,0:T(8,128)(2,1)S(1)}, u32[]{:S(2)}, u32[]{:S(2)}) %collective-permute-start.12) | collective-permute-done | bytes 524320 | tf_op jit(solution)/shard_map/ppermute | solution.py:191
  74.4 0.0 collective-permute-start.16
  74.4 0.0 collective-permute-done.17.other_hbm
  74.4 0.0 copy-done.3
  74.4 2.3 %shard_map.58.refs_0_ = bf16[1024,512]{1,0:T(8,128)(2,1)} custom-call(s32[4,8]{1,0:T(4,128)S(1)} %bitcast.3, f32[1024,512]{1,0:T(8,128)S(1)} %get-tuple-element.57.total_hbm, bf16[1024,512]{1,0:T(8,128)(2,1)S(1)} %get-tuple-element.58.late_hbm, bf16[512,512]{1,0:T(8,128)(2,1)S(1)} %collective-permute-done.13.mine_hbm, ...), custom_call_target="tpu_custom_call" | custom-call | flops 1 | bytes 1 | tf_op jit(solution)/shard_map/pallas_call | solution.py:169
  76.7 0.0 collective-permute-done.16.other_hbm
  76.7 2.3 %shard_map.59 = bf16[1024,512]{1,0:T(8,128)(2,1)} custom-call(s32[4,8]{1,0:T(4,128)S(1)} %bitcast.4, f32[1024,512]{1,0:T(8,128)S(1)} %get-tuple-element.57.total_hbm, bf16[1024,512]{1,0:T(8,128)(2,1)S(1)} %get-tuple-element.58.late_hbm, bf16[512,512]{1,0:T(8,128)(2,1)S(1)} %collective-permute-done.12.mine_hbm, ...), custom_call_target="tpu_custom_call", output_to_operand_aliasing={{}: (5, {})} | custom-call | flops 1 | bytes 1 | tf_op jit(solution)/shard_map/pallas_call | solution.py:169
  (2 shorter events, 0.1 us)
Async XLA Ops:
  2.0 17.1 %collective-permute-start.1 = (bf16[512,512]{1,0:T(8,128)(2,1)}, bf16[512,512]{1,0:T(8,128)(2,1)S(1)}, u32[]{:S(2)}, u32[]{:S(2)}) collective-permute-start(bf16[512,512]{1,0:T(8,128)(2,1)} %shard_map.55.refs_5_), channel_id=1, source_target_pairs={{0,2},{1,3},{2,6},{3,7},{6,4},{7,5},{4,0},{5,1},{8,10},{9,11},{10,... | collective-permute-start | bytes 1572872 | tf_op jit(solution)/shard_map/ppermute | solution.py:191
  5.1 14.0 %collective-permute-start.2 = (bf16[512,512]{1,0:T(8,128)(2,1)}, bf16[512,512]{1,0:T(8,128)(2,1)}, u32[]{:S(2)}, u32[]{:S(2)}) collective-permute-start(bf16[512,512]{1,0:T(8,128)(2,1)} %shard_map.55.refs_5_), channel_id=1, source_target_pairs={{0,1},{1,0},{2,3},{3,2},{4,5},{5,4},{6,7},{7,6},{8,9},{9,8},{10,11... | collective-permute-start | bytes 1572872 | tf_op jit(solution)/shard_map/ppermute | solution.py:192
  5.1 59.2 %copy-start = (bf16[512,512]{1,0:T(8,128)(2,1)S(1)}, bf16[512,512]{1,0:T(8,128)(2,1)}, u32[]{:S(2)}) copy-start(bf16[512,512]{1,0:T(8,128)(2,1)} %shard_map.55.refs_5_) | copy-start | bytes 1572868
  7.9 56.3 %copy-start.1 = (bf16[1024,512]{1,0:T(8,128)(2,1)S(1)}, bf16[1024,512]{1,0:T(8,128)(2,1)}, u32[]{:S(2)}) copy-start(bf16[1024,512]{1,0:T(8,128)(2,1)} %get-tuple-element.37.refs_0_) | copy-start | bytes 3145732
  7.9 56.3 %copy-start.2 = (bf16[512,512]{1,0:T(8,128)(2,1)S(1)}, bf16[512,512]{1,0:T(8,128)(2,1)}, u32[]{:S(2)}) copy-start(bf16[512,512]{1,0:T(8,128)(2,1)} %get-tuple-element.36.refs_6_) | copy-start | bytes 1572868
  7.9 25.8 %collective-permute-start.4 = (bf16[1024,512]{1,0:T(8,128)(2,1)}, bf16[1024,512]{1,0:T(8,128)(2,1)S(1)}, u32[]{:S(2)}, u32[]{:S(2)}) collective-permute-start(bf16[1024,512]{1,0:T(8,128)(2,1)} %get-tuple-element.37.refs_0_), channel_id=1, source_target_pairs={{0,8},{8,0},{16,24},{24,16},{1,9},{9,1},{17,25},{25,17},{2,10},{10... | collective-permute-start | bytes 3145736 | tf_op jit(solution)/shard_map/ppermute | solution.py:193
  9.5 25.5 %collective-permute-start.5 = (bf16[1024,512]{1,0:T(8,128)(2,1)}, bf16[1024,512]{1,0:T(8,128)(2,1)S(1)}, u32[]{:S(2)}, u32[]{:S(2)}) collective-permute-start(bf16[1024,512]{1,0:T(8,128)(2,1)} %get-tuple-element.37.refs_0_), channel_id=1, source_target_pairs={{0,16},{8,24},{16,0},{24,8},{1,17},{9,25},{17,1},{25,9},{2,18},{10... | collective-permute-start | bytes 3145736 | tf_op jit(solution)/shard_map/ppermute | solution.py:194
  11.0 19.2 %collective-permute-start = (bf16[512,512]{1,0:T(8,128)(2,1)}, bf16[512,512]{1,0:T(8,128)(2,1)S(1)}, u32[]{:S(2)}, u32[]{:S(2)}) collective-permute-start(bf16[512,512]{1,0:T(8,128)(2,1)} %get-tuple-element.36.refs_6_), channel_id=1, source_target_pairs={{0,2},{1,3},{2,6},{3,7},{6,4},{7,5},{4,0},{5,1},{8,10},{9,11},{10,... | collective-permute-start | bytes 1572872 | tf_op jit(solution)/shard_map/ppermute | solution.py:191
  19.0 11.2 %collective-permute-start.3 = (bf16[512,512]{1,0:T(8,128)(2,1)}, bf16[512,512]{1,0:T(8,128)(2,1)S(1)}, u32[]{:S(2)}, u32[]{:S(2)}) collective-permute-start(bf16[512,512]{1,0:T(8,128)(2,1)} %get-tuple-element.36.refs_6_), channel_id=1, source_target_pairs={{0,1},{1,0},{2,3},{3,2},{4,5},{5,4},{6,7},{7,6},{8,9},{9,8},{10,11... | collective-permute-start | bytes 1572872 | tf_op jit(solution)/shard_map/ppermute | solution.py:192
  19.0 21.6 %collective-permute-start.7 = (bf16[512,512]{1,0:T(8,128)(2,1)S(1)}, bf16[512,512]{1,0:T(8,128)(2,1)S(1)}, u32[]{:S(2)}, u32[]{:S(2)}) collective-permute-start(bf16[512,512]{1,0:T(8,128)(2,1)S(1)} %collective-permute-done.1.refs_9_), channel_id=1, source_target_pairs={{0,2},{1,3},{2,6},{3,7},{6,4},{7,5},{4,0},{5,1},{8,10},{9,11},{10,... | collective-permute-start | bytes 1572872 | tf_op jit(solution)/shard_map/ppermute | solution.py:191
  35.0 5.7 %collective-permute-start.8 = (bf16[512,512]{1,0:T(8,128)(2,1)S(1)}, bf16[512,512]{1,0:T(8,128)(2,1)S(1)}, u32[]{:S(2)}, u32[]{:S(2)}) collective-permute-start(bf16[512,512]{1,0:T(8,128)(2,1)S(1)} %collective-permute-done.1.refs_9_), channel_id=1, source_target_pairs={{0,1},{1,0},{2,3},{3,2},{4,5},{5,4},{6,7},{7,6},{8,9},{9,8},{10,11... | collective-permute-start | bytes 1572872 | tf_op jit(solution)/shard_map/ppermute | solution.py:192
  35.0 14.4 %collective-permute-start.10 = (bf16[512,512]{1,0:T(8,128)(2,1)S(1)}, bf16[512,512]{1,0:T(8,128)(2,1)S(1)}, u32[]{:S(2)}, u32[]{:S(2)}) collective-permute-start(bf16[512,512]{1,0:T(8,128)(2,1)S(1)} %slice.6), channel_id=1, source_target_pairs={{0,16},{8,24},{16,0},{24,8},{1,17},{9,25},{17,1},{25,9},{2,18},{10... | collective-permute-start | bytes 1572872 | tf_op jit(solution)/shard_map/ppermute | solution.py:194
  36.7 37.8 %copy-start.3 = (s32[8,4]{0,1:T(4,128)S(1)}, s32[8,4]{0,1:T(4,128)}, u32[]{:S(2)}) copy-start(s32[8,4]{0,1:T(4,128)} %param.9) | copy-start | bytes 388
  36.7 14.1 %collective-permute-start.11 = (bf16[512,512]{1,0:T(8,128)(2,1)S(1)}, bf16[512,512]{1,0:T(8,128)(2,1)S(1)}, u32[]{:S(2)}, u32[]{:S(2)}) collective-permute-start(bf16[512,512]{1,0:T(8,128)(2,1)S(1)} %slice.7), channel_id=1, source_target_pairs={{0,8},{8,0},{16,24},{24,16},{1,9},{9,1},{17,25},{25,17},{2,10},{10... | collective-permute-start | bytes 1572872 | tf_op jit(solution)/shard_map/ppermute | solution.py:193
  37.3 15.7 %collective-permute-start.6 = (bf16[512,512]{1,0:T(8,128)(2,1)S(1)}, bf16[512,512]{1,0:T(8,128)(2,1)S(1)}, u32[]{:S(2)}, u32[]{:S(2)}) collective-permute-start(bf16[512,512]{1,0:T(8,128)(2,1)S(1)} %collective-permute-done.refs_10_), channel_id=1, source_target_pairs={{0,2},{1,3},{2,6},{3,7},{6,4},{7,5},{4,0},{5,1},{8,10},{9,11},{10,... | collective-permute-start | bytes 1572872 | tf_op jit(solution)/shard_map/ppermute | solution.py:191
  40.7 12.3 %collective-permute-start.9 = (bf16[512,512]{1,0:T(8,128)(2,1)S(1)}, bf16[512,512]{1,0:T(8,128)(2,1)S(1)}, u32[]{:S(2)}, u32[]{:S(2)}) collective-permute-start(bf16[512,512]{1,0:T(8,128)(2,1)S(1)} %collective-permute-done.refs_10_), channel_id=1, source_target_pairs={{0,1},{1,0},{2,3},{3,2},{4,5},{5,4},{6,7},{7,6},{8,9},{9,8},{10,11... | collective-permute-start | bytes 1572872 | tf_op jit(solution)/shard_map/ppermute | solution.py:192
  40.7 23.5 %collective-permute-start.13 = (bf16[512,512]{1,0:T(8,128)(2,1)S(1)}, bf16[512,512]{1,0:T(8,128)(2,1)S(1)}, u32[]{:S(2)}, u32[]{:S(2)}) collective-permute-start(bf16[512,512]{1,0:T(8,128)(2,1)S(1)} %collective-permute-done.7.refs_13_), channel_id=1, source_target_pairs={{0,2},{1,3},{2,6},{3,7},{6,4},{7,5},{4,0},{5,1},{8,10},{9,11},{10,... | collective-permute-start | bytes 1572872 | tf_op jit(solution)/shard_map/ppermute | solution.py:191
  53.0 11.2 %collective-permute-start.14 = (bf16[512,512]{1,0:T(8,128)(2,1)S(1)}, bf16[512,512]{1,0:T(8,128)(2,1)S(1)}, u32[]{:S(2)}, u32[]{:S(2)}) collective-permute-start(bf16[512,512]{1,0:T(8,128)(2,1)S(1)} %collective-permute-done.7.refs_13_), channel_id=1, source_target_pairs={{0,1},{1,0},{2,3},{3,2},{4,5},{5,4},{6,7},{7,6},{8,9},{9,8},{10,11... | collective-permute-start | bytes 1572872 | tf_op jit(solution)/shard_map/ppermute | solution.py:192
  53.0 11.2 %collective-permute-start.15 = (bf16[512,512]{1,0:T(8,128)(2,1)S(1)}, bf16[512,512]{1,0:T(8,128)(2,1)S(1)}, u32[]{:S(2)}, u32[]{:S(2)}) collective-permute-start(bf16[512,512]{1,0:T(8,128)(2,1)S(1)} %collective-permute-done.6.refs_14_), channel_id=1, source_target_pairs={{0,1},{1,0},{2,3},{3,2},{4,5},{5,4},{6,7},{7,6},{8,9},{9,8},{10,11... | collective-permute-start | bytes 1572872 | tf_op jit(solution)/shard_map/ppermute | solution.py:192
  53.5 20.9 %collective-permute-start.12 = (bf16[512,512]{1,0:T(8,128)(2,1)S(1)}, bf16[512,512]{1,0:T(8,128)(2,1)S(1)}, u32[]{:S(2)}, u32[]{:S(2)}) collective-permute-start(bf16[512,512]{1,0:T(8,128)(2,1)S(1)} %collective-permute-done.6.refs_14_), channel_id=1, source_target_pairs={{0,2},{1,3},{2,6},{3,7},{6,4},{7,5},{4,0},{5,1},{8,10},{9,11},{10,... | collective-permute-start | bytes 1572872 | tf_op jit(solution)/shard_map/ppermute | solution.py:191
  64.2 10.2 %collective-permute-start.17 = (bf16[512,512]{1,0:T(8,128)(2,1)S(1)}, bf16[512,512]{1,0:T(8,128)(2,1)S(1)}, u32[]{:S(2)}, u32[]{:S(2)}) collective-permute-start(bf16[512,512]{1,0:T(8,128)(2,1)S(1)} %collective-permute-done.13.mine_hbm), channel_id=1, source_target_pairs={{0,1},{1,0},{2,3},{3,2},{4,5},{5,4},{6,7},{7,6},{8,9},{9,8},{10,11... | collective-permute-start | bytes 1572872 | tf_op jit(solution)/shard_map/ppermute | solution.py:192
  74.4 2.3 %collective-permute-start.16 = (bf16[512,512]{1,0:T(8,128)(2,1)S(1)}, bf16[512,512]{1,0:T(8,128)(2,1)S(1)}, u32[]{:S(2)}, u32[]{:S(2)}) collective-permute-start(bf16[512,512]{1,0:T(8,128)(2,1)S(1)} %collective-permute-done.12.mine_hbm), channel_id=1, source_target_pairs={{0,1},{1,0},{2,3},{3,2},{4,5},{5,4},{6,7},{7,6},{8,9},{9,8},{10,11... | collective-permute-start | bytes 1572872 | tf_op jit(solution)/shard_map/ppermute | solution.py:192

commit v5 on v4

--- a/solution.py
+++ b/solution.py
@@ -28,31 +28,42 @@
     bcols, brows = pieces[0][1].shape
     rows, cols = pieces[0][0].shape
     size = rows // brows
+    strips = [(i, p) for i, (_, _, first, last) in enumerate(pieces) for p in range((last - first) // size)]
 
     def body(*refs):
-        shards, patterns, outs, (pat_ref, sems), held = refs[:k], refs[k : 2 * k], refs[2 * k : 2 * k + n], refs[-2:], refs[2 * k + n : -2]
+        shards, patterns, outs = refs[:k], refs[k : 2 * k], refs[2 * k : 2 * k + n]
+        held, made, (pat_ref, sems, out_sems) = refs[2 * k + n : 2 * k + 2 * n], refs[2 * k + 2 * n : -3], refs[-3:]
         copies = [pltpu.make_async_copy(patterns[s], pat_ref.at[s], sems.at[s]) for s in range(k)]
-        for i, (shard, _, first, last) in enumerate(pieces):
-            there = shards[sources[id(shard)][0]].at[first:last]
-            copies.append(pltpu.make_async_copy(there, held[i], sems.at[k + i]))
+        for j, (i, p) in enumerate(strips):
+            shard, _, first, _ = pieces[i]
+            there = shards[sources[id(shard)][0]].at[first + p * size : first + (p + 1) * size]
+            copies.append(pltpu.make_async_copy(there, held[i].at[p * size : (p + 1) * size], sems.at[k + j]))
         for copy in copies:
             copy.start()
         for copy in copies[:k]:
             copy.wait()
-        for i, (shard, _, first, last) in enumerate(pieces):
-            copies[k + i].wait()
-            for p, q, at in cells((last - first) // size, bcols, size):
+        writes = []
+        for j, (i, p) in enumerate(strips):
+            shard, _, first, _ = pieces[i]
+            copies[k + j].wait()
+            for q in range(bcols):
+                at = (slice(p * size, (p + 1) * size), slice(q * size, (q + 1) * size))
                 stored = pat_ref[sources[id(shard)][0], q, first // size + p] != 0
-                outs[i][at] = jnp.where(stored, held[i][at], jnp.zeros((), outs[i].dtype))
+                made[i][at] = jnp.where(stored, held[i][at], jnp.zeros((), shard.dtype))
+            strip = slice(p * size, (p + 1) * size)
+            writes.append(pltpu.make_async_copy(made[i].at[strip], outs[i].at[strip], out_sems.at[j]))
+            writes[-1].start()
+        for write in writes:
+            write.wait()
 
     shapes = [jax.ShapeDtypeStruct((last - first, cols), shard.dtype) for shard, _, first, last in pieces]
     return pl.pallas_call(
         body,
         in_specs=[FAR] * (2 * k),
-        out_specs=[NEAR] * n,
+        out_specs=[HOME] * n,
         out_shape=shapes,
-        scratch_shapes=[pltpu.VMEM(v.shape, v.dtype) for v in shapes]
-        + [pltpu.SMEM((k, bcols, brows), jnp.int32), COPIES((k + n,))],
+        scratch_shapes=[pltpu.VMEM(v.shape, v.dtype) for v in shapes * 2]
+        + [pltpu.SMEM((k, bcols, brows), jnp.int32), COPIES((k + len(strips),)), COPIES((len(strips),))],
         cost_estimate=SMALL,
     )(*(v[1] for v in sources.values()), *(v[2] for v in sources.values()))
 
@@ -128,62 +139,52 @@
 
 def last_slot(first, keep_mask, total, late, mine, other, product=None):
     rows, cols = total.shape
-    tall, depth = mine.shape
+    (tall, depth), tile = mine.shape, other[0].shape[0]
     size = rows // keep_mask.shape[1]
-    tile = 256
     per, steps = tile // size, tall // tile
     given = () if product is None else (product,)
 
-    def body(keep_hbm, total_hbm, late_hbm, mine_hbm, other_hbm, *refs):
-        out_hbm, keep_ref, total_ref, late_ref, held, out_ref, sems, out_sems = refs[len(given) :]
-        moves = [
-            (late_hbm, late_ref),
-            (mine_hbm, held.at[0]),
-            (other_hbm, held.at[1]),
-            (total_hbm.at[first : first + tall], total_ref),
-            (keep_hbm, keep_ref),
-        ]
-        copies = [pltpu.make_async_copy(s, d, sems.at[i]) for i, (s, d) in enumerate(moves)]
-        for copy in copies:
+    def body(keep_hbm, total_ref, late_ref, mine_ref, *refs):
+        others, (out_ref, keep_ref, sem) = refs[:steps], refs[-3:]
+        step = pl.program_id(0)
+        copy = pltpu.make_async_copy(keep_hbm, keep_ref, sem)
+
+        @pl.when(step == 0)
+        def _():
             copy.start()
+
         core = lax.axis_index("col") % 2
-        for copy in copies:
+        near = late_ref[pl.ds(pl.multiple_of(core * depth, depth), depth), :]
+        far = late_ref[pl.ds(pl.multiple_of((1 - core) * depth, depth), depth), :]
+        other_now = others[0][...]
+        for i in range(1, steps):
+            other_now = jnp.where(step == i, others[i][...], other_now)
+        sums = total_ref[...] + jnp.dot(mine_ref[...], near, preferred_element_type=jnp.float32)
+        sums += jnp.dot(other_now, far, preferred_element_type=jnp.float32)
+
+        @pl.when(step == 0)
+        def _():
             copy.wait()
-        writes = []
-        for m in range(steps):
-            some = slice(m * tile, (m + 1) * tile)
-            near = late_ref[pl.ds(pl.multiple_of(core * depth, depth), depth), :]
-            far = late_ref[pl.ds(pl.multiple_of((1 - core) * depth, depth), depth), :]
-            sums = total_ref[some, :] + jnp.dot(held[0, some, :], near, preferred_element_type=jnp.float32)
-            sums += jnp.dot(held[1, some, :], far, preferred_element_type=jnp.float32)
-            for p, q, at in cells(per, cols // size, size):
-                kept = keep_ref[q, first // size + m * per + p].astype(jnp.float32)
-                out_ref[m * tile + at[0].start : m * tile + at[0].stop, at[1]] = (sums[at] * kept).astype(out_ref.dtype)
-            there = slice(first + m * tile, first + (m + 1) * tile)
-            write = pltpu.make_async_copy(out_ref.at[some], out_hbm.at[there], out_sems.at[m])
-            write.start()
-            writes.append(write)
-        for write in writes:
-            write.wait()
-
+
+        for p, q, at in cells(per, cols // size, size):
+            kept = keep_ref[q, first // size + step * per + p].astype(jnp.float32)
+            out_ref[at] = (sums[at] * kept).astype(out_ref.dtype)
+
+    here = pl.BlockSpec((tile, cols), lambda i: (first // tile + i, 0))
+    whole = lambda v: pl.BlockSpec(v.shape, lambda i: (0, 0))
     return pl.pallas_call(
         body,
-        in_specs=[FAR] + [HOME] * 2 + [FAR] * 2 + [HOME] * len(given),
-        out_specs=HOME,
+        grid=(steps,),
+        in_specs=[FAR, here, whole(late), pl.BlockSpec((tile, depth), lambda i: (i, 0))]
+        + [whole(v) for v in other]
+        + [HOME] * len(given),
+        out_specs=here,
         out_shape=jax.ShapeDtypeStruct((rows, cols), jnp.bfloat16),
-        scratch_shapes=[
-            pltpu.SMEM(keep_mask.shape, jnp.int32),
-            pltpu.VMEM((tall, cols), total.dtype),
-            pltpu.VMEM(late.shape, late.dtype),
-            pltpu.VMEM((2, tall, depth), late.dtype),
-            pltpu.VMEM((tall, cols), jnp.bfloat16),
-            COPIES((5,)),
-            COPIES((steps,)),
-        ],
-        input_output_aliases={5: 0} if given else {},
+        scratch_shapes=[pltpu.SMEM(keep_mask.shape, jnp.int32), COPIES(())],
+        input_output_aliases={4 + steps: 0} if given else {},
         compiler_params=pltpu.CompilerParams(vmem_limit_bytes=10 * MIB),
         cost_estimate=SMALL,
-    )(keep_mask, total, late, mine, other, *given)
+    )(keep_mask, total, late, mine, *other, *given)
 
 
 def on_grid(left, right, a_pattern, b_pattern, keep_mask):
@@ -213,13 +214,15 @@
     r3 = [on(r2[0])]
     e1.append(cross(r1[1]))
     r2[1], e1[1], r2[0], *bd = tied(r2[1], e1[1], r2[0], *bd)
+    quarter = half // 2
+    parts = lambda v: [v[:quarter], v[quarter:]]
     r3.append(on(r2[1]))
     e2 = [cross(v) for v in r2]
     r3[0], *e2 = tied(r3[0], *e2)
     total, late = early_slots((((a0, a1), ea), (r1, e1), (r2, e2)), ((b,), (bx,), (by,), bd))
-    r3[1], total, late = tied(r3[1], total, late)
-    product = last_slot(0, keep_mask.T, total, late, r3[0], cross(r3[0]))
-    return last_slot(half, keep_mask.T, total, late, r3[1], cross(r3[1]), product)
+    product = last_slot(0, keep_mask.T, total, late, r3[0], [cross(v) for v in parts(r3[0])])
+    r3[1], product = tied(r3[1], product)
+    return last_slot(half, keep_mask.T, total, late, r3[1], [cross(v) for v in parts(r3[1])], product)
 
 
 def on_any(left, right, a_pattern, b_pattern, keep_mask):

time: 79.2 us -> 78.3 us (0.989)
  Pallas kernels: 14.5 us -> 12.7 us
  starting transfers between devices: 18.9 us -> 19.7 us
    ppermute x8 -> x10, waiting for transfers between devices: 0.02 us -> 1.42 us  [on_grid(): cross = lambda v: lax.ppermute(v, 'col', [(i, i ^ 1) for i in range(8)])]
    pallas_call x4, Pallas kernels: 9.34 us -> 8.18 us  [the longest x2 4.23 us: masked(): pl.pallas_call(body, in_specs=[FAR] * (2 * k), out_specs=[HOME] * n, out_...]
    ppermute x8 -> x10, starting transfers between devices: 0.53 us -> 1.65 us  [on_grid(): cross = lambda v: lax.ppermute(v, 'col', [(i, i ^ 1) for i in range(8)])]
  transfers between devices with their start and end apart: 18 -> 20, of which waited for: 10 -> 12; matrix products, arithmetic and copies ran while one was open for 0% -> 0% of each run, Pallas kernels for 13% -> 11%
where the time goes in v5:
time: 78.3 us; the launch traced here: 78.2 us
  waiting for transfers between devices  45.5 us (58%)
  starting transfers between devices  19.7 us (25%)
  Pallas kernels  12.7 us (16%)
    ppermute x6, waiting for transfers between devices, on_grid(): on = lambda v: lax.ppermute(v, 'col', ring)  32.1 us
    ppermute x6, starting transfers between devices, on_grid(): on = lambda v: lax.ppermute(v, 'col', ring)  12.8 us
    ppermute x2, waiting for transfers between devices, on_grid(): to_y = lambda v: lax.ppermute(v, 'row', [(i, i ^ 2) for i in range(4)])  7.52 us
    pallas_call x1, Pallas kernels, early_slots(): pl.pallas_call(body, in_specs=specs, out_specs=[NEAR, NEAR], out_shape=[j...  4.49 us
    ppermute x2, waiting for transfers between devices, on_grid(): to_x = lambda v: lax.ppermute(v, 'row', [(i, i ^ 1) for i in range(4)])  4.4 us
    pallas_call x2, Pallas kernels, masked(): pl.pallas_call(body, in_specs=[FAR] * (2 * k), out_specs=[HOME] * n, out_...  4.23 us
    pallas_call x2, Pallas kernels, last_slot(): pl.pallas_call(body, grid=(steps,), in_specs=[FAR, here, whole(late), pl....  3.95 us
    ppermute x2, starting transfers between devices, on_grid(): to_y = lambda v: lax.ppermute(v, 'row', [(i, i ^ 2) for i in range(4)])  3.1 us
  transfers between devices with their start and end apart: 20, of which 12 were waited for; matrix products, arithmetic and copies ran while one was open for 0% of the time, Pallas kernels for 11%

profile of v5, /device:TPU:0, one launch (start us, length us, event | category | flops | bytes accessed | tf_op | source)
XLA Modules:
  0.0 78.2 jit_solution(15365096581120613809)
XLA Ops:
  0.0 1.9 %shard_map.55.refs_5_ = bf16[512,512]{1,0:T(8,128)(2,1)} custom-call(bf16[1024,512]{1,0:T(8,128)(2,1)} %refs_0_.2, s32[4,8]{1,0:T(4,128)} %bitcast.5), custom_call_target="tpu_custom_call" | custom-call | flops 1 | bytes 1 | tf_op jit(solution)/shard_map/pallas_call | solution.py:60
  1.9 3.1 %collective-permute-start.1 = (bf16[512,512]{1,0:T(8,128)(2,1)}, bf16[512,512]{1,0:T(8,128)(2,1)S(1)}, u32[]{:S(2)}, u32[]{:S(2)}) collective-permute-start(bf16[512,512]{1,0:T(8,128)(2,1)} %shard_map.55.refs_5_), channel_id=1, source_target_pairs={{0,2},{1,3},{2,6},{3,7},{6,4},{7,5},{4,0},{5,1},{8,10},{9,11},{10,... | collective-permute-start | bytes 1572872 | tf_op jit(solution)/shard_map/ppermute | solution.py:192
  4.9 0.0 collective-permute-start.2
  4.9 2.4 %shard_map.56 = (bf16[512,512]{1,0:T(8,128)(2,1)}, bf16[1024,512]{1,0:T(8,128)(2,1)}) custom-call(bf16[1024,512]{1,0:T(8,128)(2,1)} %refs_0_.2, bf16[1024,512]{1,0:T(8,128)(2,1)} %refs_1_.1, s32[4,8]{1,0:T(4,128)} %bitcast.6, s32[4,8]{1,0:T(4,128)} %bitcast.7), custom_call_target="tpu_custom_call" | custom-call | flops 1 | bytes 1 | tf_op jit(solution)/shard_map/pallas_call | solution.py:60
  7.3 0.0 copy-start
  7.3 0.0 copy-start.1
  7.3 0.0 copy-start.2
  7.4 1.6 %collective-permute-start.4 = (bf16[1024,512]{1,0:T(8,128)(2,1)}, bf16[1024,512]{1,0:T(8,128)(2,1)S(1)}, u32[]{:S(2)}, u32[]{:S(2)}) collective-permute-start(bf16[1024,512]{1,0:T(8,128)(2,1)} %get-tuple-element.33.refs_0_), channel_id=1, source_target_pairs={{0,8},{8,0},{16,24},{24,16},{1,9},{9,1},{17,25},{25,17},{2,10},{10... | collective-permute-start | bytes 3145736 | tf_op jit(solution)/shard_map/ppermute | solution.py:194
  8.9 1.5 %collective-permute-start.5 = (bf16[1024,512]{1,0:T(8,128)(2,1)}, bf16[1024,512]{1,0:T(8,128)(2,1)S(1)}, u32[]{:S(2)}, u32[]{:S(2)}) collective-permute-start(bf16[1024,512]{1,0:T(8,128)(2,1)} %get-tuple-element.33.refs_0_), channel_id=1, source_target_pairs={{0,16},{8,24},{16,0},{24,8},{1,17},{9,25},{17,1},{25,9},{2,18},{10... | collective-permute-start | bytes 3145736 | tf_op jit(solution)/shard_map/ppermute | solution.py:195
  10.4 2.6 %collective-permute-start = (bf16[512,512]{1,0:T(8,128)(2,1)}, bf16[512,512]{1,0:T(8,128)(2,1)S(1)}, u32[]{:S(2)}, u32[]{:S(2)}) collective-permute-start(bf16[512,512]{1,0:T(8,128)(2,1)} %get-tuple-element.36.refs_6_), channel_id=1, source_target_pairs={{0,2},{1,3},{2,6},{3,7},{6,4},{7,5},{4,0},{5,1},{8,10},{9,11},{10,... | collective-permute-start | bytes 1572872 | tf_op jit(solution)/shard_map/ppermute | solution.py:192
  13.0 5.9 %collective-permute-done.1.refs_9_ = bf16[512,512]{1,0:T(8,128)(2,1)S(1)} collective-permute-done((bf16[512,512]{1,0:T(8,128)(2,1)}, bf16[512,512]{1,0:T(8,128)(2,1)S(1)}, u32[]{:S(2)}, u32[]{:S(2)}) %collective-permute-start.1) | collective-permute-done | bytes 524320 | tf_op jit(solution)/shard_map/ppermute | solution.py:192
  18.9 0.0 collective-permute-done.2.refs_7_
  18.9 0.0 collective-permute-start.3
  18.9 1.3 %collective-permute-start.7 = (bf16[512,512]{1,0:T(8,128)(2,1)S(1)}, bf16[512,512]{1,0:T(8,128)(2,1)S(1)}, u32[]{:S(2)}, u32[]{:S(2)}) collective-permute-start(bf16[512,512]{1,0:T(8,128)(2,1)S(1)} %collective-permute-done.1.refs_9_), channel_id=1, source_target_pairs={{0,2},{1,3},{2,6},{3,7},{6,4},{7,5},{4,0},{5,1},{8,10},{9,11},{10,... | collective-permute-start | bytes 1572872 | tf_op jit(solution)/shard_map/ppermute | solution.py:192
  20.2 10.0 %collective-permute-done.refs_10_ = bf16[512,512]{1,0:T(8,128)(2,1)S(1)} collective-permute-done((bf16[512,512]{1,0:T(8,128)(2,1)}, bf16[512,512]{1,0:T(8,128)(2,1)S(1)}, u32[]{:S(2)}, u32[]{:S(2)}) %collective-permute-start) | collective-permute-done | bytes 524320 | tf_op jit(solution)/shard_map/ppermute | solution.py:192
  30.2 0.0 collective-permute-done.3.refs_8_
  30.2 3.1 %collective-permute-done.4.refs_1_ = bf16[1024,512]{1,0:T(8,128)(2,1)S(1)} collective-permute-done((bf16[1024,512]{1,0:T(8,128)(2,1)}, bf16[1024,512]{1,0:T(8,128)(2,1)S(1)}, u32[]{:S(2)}, u32[]{:S(2)}) %collective-permute-start.4) | collective-permute-done | bytes 1048608 | tf_op jit(solution)/shard_map/ppermute | solution.py:194
  33.2 1.2 %collective-permute-done.5.refs_2_ = bf16[1024,512]{1,0:T(8,128)(2,1)S(1)} collective-permute-done((bf16[1024,512]{1,0:T(8,128)(2,1)}, bf16[1024,512]{1,0:T(8,128)(2,1)S(1)}, u32[]{:S(2)}, u32[]{:S(2)}) %collective-permute-start.5) | collective-permute-done | bytes 1048608 | tf_op jit(solution)/shard_map/ppermute | solution.py:195
  34.4 0.0 collective-permute-start.8
  34.5 1.6 %collective-permute-start.10 = (bf16[512,512]{1,0:T(8,128)(2,1)S(1)}, bf16[512,512]{1,0:T(8,128)(2,1)S(1)}, u32[]{:S(2)}, u32[]{:S(2)}) collective-permute-start(bf16[512,512]{1,0:T(8,128)(2,1)S(1)} %slice.18), channel_id=1, source_target_pairs={{0,16},{8,24},{16,0},{24,8},{1,17},{9,25},{17,1},{25,9},{2,18},{10... | collective-permute-start | bytes 1572872 | tf_op jit(solution)/shard_map/ppermute | solution.py:195
  36.1 0.6 collective-permute-start.11
  36.7 2.6 %collective-permute-start.6 = (bf16[512,512]{1,0:T(8,128)(2,1)S(1)}, bf16[512,512]{1,0:T(8,128)(2,1)S(1)}, u32[]{:S(2)}, u32[]{:S(2)}) collective-permute-start(bf16[512,512]{1,0:T(8,128)(2,1)S(1)} %collective-permute-done.refs_10_), channel_id=1, source_target_pairs={{0,2},{1,3},{2,6},{3,7},{6,4},{7,5},{4,0},{5,1},{8,10},{9,11},{10,... | collective-permute-start | bytes 1572872 | tf_op jit(solution)/shard_map/ppermute | solution.py:192
  39.3 1.7 %collective-permute-done.7.refs_13_ = bf16[512,512]{1,0:T(8,128)(2,1)S(1)} collective-permute-done((bf16[512,512]{1,0:T(8,128)(2,1)S(1)}, bf16[512,512]{1,0:T(8,128)(2,1)S(1)}, u32[]{:S(2)}, u32[]{:S(2)}) %collective-permute-start.7) | collective-permute-done | bytes 524320 | tf_op jit(solution)/shard_map/ppermute | solution.py:192
  40.9 0.0 collective-permute-done.8.refs_11_
  40.9 0.0 collective-permute-start.9
  40.9 1.6 %collective-permute-start.12 = (bf16[512,512]{1,0:T(8,128)(2,1)S(1)}, bf16[512,512]{1,0:T(8,128)(2,1)S(1)}, u32[]{:S(2)}, u32[]{:S(2)}) collective-permute-start(bf16[512,512]{1,0:T(8,128)(2,1)S(1)} %collective-permute-done.7.refs_13_), channel_id=1, source_target_pairs={{0,2},{1,3},{2,6},{3,7},{6,4},{7,5},{4,0},{5,1},{8,10},{9,11},{10,... | collective-permute-start | bytes 1572872 | tf_op jit(solution)/shard_map/ppermute | solution.py:192
  42.5 6.3 %collective-permute-done.10.refs_3_ = bf16[512,512]{1,0:T(8,128)(2,1)S(1)} collective-permute-done((bf16[512,512]{1,0:T(8,128)(2,1)S(1)}, bf16[512,512]{1,0:T(8,128)(2,1)S(1)}, u32[]{:S(2)}, u32[]{:S(2)}) %collective-permute-start.10) | collective-permute-done | bytes 524320 | tf_op jit(solution)/shard_map/ppermute | solution.py:195
  48.9 1.3 %collective-permute-done.11.refs_4_ = bf16[512,512]{1,0:T(8,128)(2,1)S(1)} collective-permute-done((bf16[512,512]{1,0:T(8,128)(2,1)S(1)}, bf16[512,512]{1,0:T(8,128)(2,1)S(1)}, u32[]{:S(2)}, u32[]{:S(2)}) %collective-permute-start.11) | collective-permute-done | bytes 524320 | tf_op jit(solution)/shard_map/ppermute | solution.py:194
  50.2 2.2 %collective-permute-done.6.refs_14_ = bf16[512,512]{1,0:T(8,128)(2,1)S(1)} collective-permute-done((bf16[512,512]{1,0:T(8,128)(2,1)S(1)}, bf16[512,512]{1,0:T(8,128)(2,1)S(1)}, u32[]{:S(2)}, u32[]{:S(2)}) %collective-permute-start.6) | collective-permute-done | bytes 524320 | tf_op jit(solution)/shard_map/ppermute | solution.py:192
  52.4 0.0 collective-permute-done.9.refs_12_
  52.4 0.0 collective-permute-start.13
  52.4 0.5 collective-permute-start.14
  52.9 1.7 %collective-permute-start.15 = (bf16[512,512]{1,0:T(8,128)(2,1)S(1)}, bf16[512,512]{1,0:T(8,128)(2,1)S(1)}, u32[]{:S(2)}, u32[]{:S(2)}) collective-permute-start(bf16[512,512]{1,0:T(8,128)(2,1)S(1)} %collective-permute-done.6.refs_14_), channel_id=1, source_target_pairs={{0,2},{1,3},{2,6},{3,7},{6,4},{7,5},{4,0},{5,1},{8,10},{9,11},{10,... | collective-permute-start | bytes 1572872 | tf_op jit(solution)/shard_map/ppermute | solution.py:192
  54.6 9.0 %collective-permute-done.12.mine_ref = bf16[512,512]{1,0:T(8,128)(2,1)S(1)} collective-permute-done((bf16[512,512]{1,0:T(8,128)(2,1)S(1)}, bf16[512,512]{1,0:T(8,128)(2,1)S(1)}, u32[]{:S(2)}, u32[]{:S(2)}) %collective-permute-start.12) | collective-permute-done | bytes 524320 | tf_op jit(solution)/shard_map/ppermute | solution.py:192
  63.6 0.0 collective-permute-done.13.refs_15_
  63.6 0.0 collective-permute-done.14.refs_16_
  63.7 0.1 collective-permute-start.16
  63.7 0.0 copy-start.3
  63.8 0.5 collective-permute-start.17
  64.2 0.0 copy-done
  64.2 0.0 copy-done.1
  64.2 0.0 copy-done.2
  64.2 4.5 %shard_map.57 = (f32[1024,512]{1,0:T(8,128)S(1)}, bf16[1024,512]{1,0:T(8,128)(2,1)S(1)}) custom-call(bf16[1024,512]{1,0:T(8,128)(2,1)S(1)} %copy-done.1, bf16[1024,512]{1,0:T(8,128)(2,1)S(1)} %collective-permute-done.4.refs_1_, bf16[1024,512]{1,0:T(8,128)(2,1)S(1)} %collective-permute-done.5.refs_2_, bf16[512,512]{1,0:T(8,128)(2,1)S(1)} %collective-permute-done.10.refs_3_, ...), custom_call_target="tpu_custom_call" | custom-call | flops 1 | bytes 1 | tf_op jit(solution)/shard_map/pallas_call | solution.py:125
  68.7 0.0 collective-permute-done.16.refs_0_
  68.8 0.0 collective-permute-done.17.refs_1_
  68.8 0.0 copy-done.3
  68.8 2.1 %shard_map.58.refs_2_ = bf16[1024,512]{1,0:T(8,128)(2,1)} custom-call(s32[4,8]{1,0:T(4,128)S(1)} %bitcast.3, f32[1024,512]{1,0:T(8,128)S(1)} %get-tuple-element.54.total_ref, bf16[1024,512]{1,0:T(8,128)(2,1)S(1)} %get-tuple-element.55.late_ref, bf16[512,512]{1,0:T(8,128)(2,1)S(1)} %collective-permute-done.12.mine_ref, ...), custom_call_target="tpu_custom_call" | custom-call | flops 1 | bytes 1 | tf_op jit(solution)/shard_map/pallas_call | solution.py:175
  70.9 3.4 %collective-permute-done.15.mine_ref = bf16[512,512]{1,0:T(8,128)(2,1)S(1)} collective-permute-done((bf16[512,512]{1,0:T(8,128)(2,1)S(1)}, bf16[512,512]{1,0:T(8,128)(2,1)S(1)}, u32[]{:S(2)}, u32[]{:S(2)}) %collective-permute-start.15) | collective-permute-done | bytes 524320 | tf_op jit(solution)/shard_map/ppermute | solution.py:192
  74.3 0.1 collective-permute-start.18
  74.4 0.5 collective-permute-start.19
  74.9 1.0 %collective-permute-done.18.refs_0_ = bf16[256,512]{1,0:T(8,128)(2,1)S(1)} collective-permute-done((bf16[256,512]{1,0:T(8,128)(2,1)S(1)}, bf16[256,512]{1,0:T(8,128)(2,1)S(1)}, u32[]{:S(2)}, u32[]{:S(2)}) %collective-permute-start.18) | collective-permute-done | bytes 262176 | tf_op jit(solution)/shard_map/ppermute | solution.py:193
  75.9 0.4 collective-permute-done.19.refs_1_
  76.3 1.9 %shard_map.59 = bf16[1024,512]{1,0:T(8,128)(2,1)} custom-call(s32[4,8]{1,0:T(4,128)S(1)} %bitcast.4, f32[1024,512]{1,0:T(8,128)S(1)} %get-tuple-element.54.total_ref, bf16[1024,512]{1,0:T(8,128)(2,1)S(1)} %get-tuple-element.55.late_ref, bf16[512,512]{1,0:T(8,128)(2,1)S(1)} %collective-permute-done.15.mine_ref, ...), custom_call_target="tpu_custom_call", output_to_operand_aliasing={{}: (6, {})} | custom-call | flops 1 | bytes 1 | tf_op jit(solution)/shard_map/pallas_call | solution.py:175
  (4 shorter events, 0.1 us)
Async XLA Ops:
  1.9 17.1 %collective-permute-start.1 = (bf16[512,512]{1,0:T(8,128)(2,1)}, bf16[512,512]{1,0:T(8,128)(2,1)S(1)}, u32[]{:S(2)}, u32[]{:S(2)}) collective-permute-start(bf16[512,512]{1,0:T(8,128)(2,1)} %shard_map.55.refs_5_), channel_id=1, source_target_pairs={{0,2},{1,3},{2,6},{3,7},{6,4},{7,5},{4,0},{5,1},{8,10},{9,11},{10,... | collective-permute-start | bytes 1572872 | tf_op jit(solution)/shard_map/ppermute | solution.py:192
  4.9 14.0 %collective-permute-start.2 = (bf16[512,512]{1,0:T(8,128)(2,1)}, bf16[512,512]{1,0:T(8,128)(2,1)S(1)}, u32[]{:S(2)}, u32[]{:S(2)}) collective-permute-start(bf16[512,512]{1,0:T(8,128)(2,1)} %shard_map.55.refs_5_), channel_id=1, source_target_pairs={{0,1},{1,0},{2,3},{3,2},{4,5},{5,4},{6,7},{7,6},{8,9},{9,8},{10,11... | collective-permute-start | bytes 1572872 | tf_op jit(solution)/shard_map/ppermute | solution.py:193
  7.3 56.9 %copy-start = (bf16[512,512]{1,0:T(8,128)(2,1)S(1)}, bf16[512,512]{1,0:T(8,128)(2,1)}, u32[]{:S(2)}) copy-start(bf16[512,512]{1,0:T(8,128)(2,1)} %shard_map.55.refs_5_) | copy-start | bytes 1572868
  7.3 56.9 %copy-start.1 = (bf16[1024,512]{1,0:T(8,128)(2,1)S(1)}, bf16[1024,512]{1,0:T(8,128)(2,1)}, u32[]{:S(2)}) copy-start(bf16[1024,512]{1,0:T(8,128)(2,1)} %get-tuple-element.33.refs_0_) | copy-start | bytes 3145732
  7.3 56.9 %copy-start.2 = (bf16[512,512]{1,0:T(8,128)(2,1)S(1)}, bf16[512,512]{1,0:T(8,128)(2,1)}, u32[]{:S(2)}) copy-start(bf16[512,512]{1,0:T(8,128)(2,1)} %get-tuple-element.36.refs_6_) | copy-start | bytes 1572868
  7.4 25.8 %collective-permute-start.4 = (bf16[1024,512]{1,0:T(8,128)(2,1)}, bf16[1024,512]{1,0:T(8,128)(2,1)S(1)}, u32[]{:S(2)}, u32[]{:S(2)}) collective-permute-start(bf16[1024,512]{1,0:T(8,128)(2,1)} %get-tuple-element.33.refs_0_), channel_id=1, source_target_pairs={{0,8},{8,0},{16,24},{24,16},{1,9},{9,1},{17,25},{25,17},{2,10},{10... | collective-permute-start | bytes 3145736 | tf_op jit(solution)/shard_map/ppermute | solution.py:194
  8.9 25.5 %collective-permute-start.5 = (bf16[1024,512]{1,0:T(8,128)(2,1)}, bf16[1024,512]{1,0:T(8,128)(2,1)S(1)}, u32[]{:S(2)}, u32[]{:S(2)}) collective-permute-start(bf16[1024,512]{1,0:T(8,128)(2,1)} %get-tuple-element.33.refs_0_), channel_id=1, source_target_pairs={{0,16},{8,24},{16,0},{24,8},{1,17},{9,25},{17,1},{25,9},{2,18},{10... | collective-permute-start | bytes 3145736 | tf_op jit(solution)/shard_map/ppermute | solution.py:195
  10.4 19.7 %collective-permute-start = (bf16[512,512]{1,0:T(8,128)(2,1)}, bf16[512,512]{1,0:T(8,128)(2,1)S(1)}, u32[]{:S(2)}, u32[]{:S(2)}) collective-permute-start(bf16[512,512]{1,0:T(8,128)(2,1)} %get-tuple-element.36.refs_6_), channel_id=1, source_target_pairs={{0,2},{1,3},{2,6},{3,7},{6,4},{7,5},{4,0},{5,1},{8,10},{9,11},{10,... | collective-permute-start | bytes 1572872 | tf_op jit(solution)/shard_map/ppermute | solution.py:192
  18.9 11.2 %collective-permute-start.3 = (bf16[512,512]{1,0:T(8,128)(2,1)}, bf16[512,512]{1,0:T(8,128)(2,1)S(1)}, u32[]{:S(2)}, u32[]{:S(2)}) collective-permute-start(bf16[512,512]{1,0:T(8,128)(2,1)} %get-tuple-element.36.refs_6_), channel_id=1, source_target_pairs={{0,1},{1,0},{2,3},{3,2},{4,5},{5,4},{6,7},{7,6},{8,9},{9,8},{10,11... | collective-permute-start | bytes 1572872 | tf_op jit(solution)/shard_map/ppermute | solution.py:193
  18.9 22.0 %collective-permute-start.7 = (bf16[512,512]{1,0:T(8,128)(2,1)S(1)}, bf16[512,512]{1,0:T(8,128)(2,1)S(1)}, u32[]{:S(2)}, u32[]{:S(2)}) collective-permute-start(bf16[512,512]{1,0:T(8,128)(2,1)S(1)} %collective-permute-done.1.refs_9_), channel_id=1, source_target_pairs={{0,2},{1,3},{2,6},{3,7},{6,4},{7,5},{4,0},{5,1},{8,10},{9,11},{10,... | collective-permute-start | bytes 1572872 | tf_op jit(solution)/shard_map/ppermute | solution.py:192
  34.4 6.5 %collective-permute-start.8 = (bf16[512,512]{1,0:T(8,128)(2,1)S(1)}, bf16[512,512]{1,0:T(8,128)(2,1)S(1)}, u32[]{:S(2)}, u32[]{:S(2)}) collective-permute-start(bf16[512,512]{1,0:T(8,128)(2,1)S(1)} %collective-permute-done.1.refs_9_), channel_id=1, source_target_pairs={{0,1},{1,0},{2,3},{3,2},{4,5},{5,4},{6,7},{7,6},{8,9},{9,8},{10,11... | collective-permute-start | bytes 1572872 | tf_op jit(solution)/shard_map/ppermute | solution.py:193
  34.5 14.4 %collective-permute-start.10 = (bf16[512,512]{1,0:T(8,128)(2,1)S(1)}, bf16[512,512]{1,0:T(8,128)(2,1)S(1)}, u32[]{:S(2)}, u32[]{:S(2)}) collective-permute-start(bf16[512,512]{1,0:T(8,128)(2,1)S(1)} %slice.18), channel_id=1, source_target_pairs={{0,16},{8,24},{16,0},{24,8},{1,17},{9,25},{17,1},{25,9},{2,18},{10... | collective-permute-start | bytes 1572872 | tf_op jit(solution)/shard_map/ppermute | solution.py:195
  36.1 14.1 %collective-permute-start.11 = (bf16[512,512]{1,0:T(8,128)(2,1)S(1)}, bf16[512,512]{1,0:T(8,128)(2,1)S(1)}, u32[]{:S(2)}, u32[]{:S(2)}) collective-permute-start(bf16[512,512]{1,0:T(8,128)(2,1)S(1)} %slice.19), channel_id=1, source_target_pairs={{0,8},{8,0},{16,24},{24,16},{1,9},{9,1},{17,25},{25,17},{2,10},{10... | collective-permute-start | bytes 1572872 | tf_op jit(solution)/shard_map/ppermute | solution.py:194
  36.7 15.7 %collective-permute-start.6 = (bf16[512,512]{1,0:T(8,128)(2,1)S(1)}, bf16[512,512]{1,0:T(8,128)(2,1)S(1)}, u32[]{:S(2)}, u32[]{:S(2)}) collective-permute-start(bf16[512,512]{1,0:T(8,128)(2,1)S(1)} %collective-permute-done.refs_10_), channel_id=1, source_target_pairs={{0,2},{1,3},{2,6},{3,7},{6,4},{7,5},{4,0},{5,1},{8,10},{9,11},{10,... | collective-permute-start | bytes 1572872 | tf_op jit(solution)/shard_map/ppermute | solution.py:192
  40.9 11.5 %collective-permute-start.9 = (bf16[512,512]{1,0:T(8,128)(2,1)S(1)}, bf16[512,512]{1,0:T(8,128)(2,1)S(1)}, u32[]{:S(2)}, u32[]{:S(2)}) collective-permute-start(bf16[512,512]{1,0:T(8,128)(2,1)S(1)} %collective-permute-done.refs_10_), channel_id=1, source_target_pairs={{0,1},{1,0},{2,3},{3,2},{4,5},{5,4},{6,7},{7,6},{8,9},{9,8},{10,11... | collective-permute-start | bytes 1572872 | tf_op jit(solution)/shard_map/ppermute | solution.py:193
  40.9 22.7 %collective-permute-start.12 = (bf16[512,512]{1,0:T(8,128)(2,1)S(1)}, bf16[512,512]{1,0:T(8,128)(2,1)S(1)}, u32[]{:S(2)}, u32[]{:S(2)}) collective-permute-start(bf16[512,512]{1,0:T(8,128)(2,1)S(1)} %collective-permute-done.7.refs_13_), channel_id=1, source_target_pairs={{0,2},{1,3},{2,6},{3,7},{6,4},{7,5},{4,0},{5,1},{8,10},{9,11},{10,... | collective-permute-start | bytes 1572872 | tf_op jit(solution)/shard_map/ppermute | solution.py:192
  52.4 11.2 %collective-permute-start.13 = (bf16[512,512]{1,0:T(8,128)(2,1)S(1)}, bf16[512,512]{1,0:T(8,128)(2,1)S(1)}, u32[]{:S(2)}, u32[]{:S(2)}) collective-permute-start(bf16[512,512]{1,0:T(8,128)(2,1)S(1)} %collective-permute-done.7.refs_13_), channel_id=1, source_target_pairs={{0,1},{1,0},{2,3},{3,2},{4,5},{5,4},{6,7},{7,6},{8,9},{9,8},{10,11... | collective-permute-start | bytes 1572872 | tf_op jit(solution)/shard_map/ppermute | solution.py:193
  52.4 11.2 %collective-permute-start.14 = (bf16[512,512]{1,0:T(8,128)(2,1)S(1)}, bf16[512,512]{1,0:T(8,128)(2,1)S(1)}, u32[]{:S(2)}, u32[]{:S(2)}) collective-permute-start(bf16[512,512]{1,0:T(8,128)(2,1)S(1)} %collective-permute-done.6.refs_14_), channel_id=1, source_target_pairs={{0,1},{1,0},{2,3},{3,2},{4,5},{5,4},{6,7},{7,6},{8,9},{9,8},{10,11... | collective-permute-start | bytes 1572872 | tf_op jit(solution)/shard_map/ppermute | solution.py:193
  52.9 21.4 %collective-permute-start.15 = (bf16[512,512]{1,0:T(8,128)(2,1)S(1)}, bf16[512,512]{1,0:T(8,128)(2,1)S(1)}, u32[]{:S(2)}, u32[]{:S(2)}) collective-permute-start(bf16[512,512]{1,0:T(8,128)(2,1)S(1)} %collective-permute-done.6.refs_14_), channel_id=1, source_target_pairs={{0,2},{1,3},{2,6},{3,7},{6,4},{7,5},{4,0},{5,1},{8,10},{9,11},{10,... | collective-permute-start | bytes 1572872 | tf_op jit(solution)/shard_map/ppermute | solution.py:192
  63.7 5.1 %collective-permute-start.16 = (bf16[256,512]{1,0:T(8,128)(2,1)S(1)}, bf16[256,512]{1,0:T(8,128)(2,1)S(1)}, u32[]{:S(2)}, u32[]{:S(2)}) collective-permute-start(bf16[256,512]{1,0:T(8,128)(2,1)S(1)} %get-tuple-element.62), channel_id=1, source_target_pairs={{0,1},{1,0},{2,3},{3,2},{4,5},{5,4},{6,7},{7,6},{8,9},{9,8},{10,11... | collective-permute-start | bytes 786440 | tf_op jit(solution)/shard_map/ppermute | solution.py:193
  63.7 5.0 %copy-start.3 = (s32[8,4]{0,1:T(4,128)S(1)}, s32[8,4]{0,1:T(4,128)}, u32[]{:S(2)}) copy-start(s32[8,4]{0,1:T(4,128)} %param.9) | copy-start | bytes 388
  63.8 5.0 %collective-permute-start.17 = (bf16[256,512]{1,0:T(8,128)(2,1)S(1)}, bf16[256,512]{1,0:T(8,128)(2,1)S(1)}, u32[]{:S(2)}, u32[]{:S(2)}) collective-permute-start(bf16[256,512]{1,0:T(8,128)(2,1)S(1)} %get-tuple-element.61), channel_id=1, source_target_pairs={{0,1},{1,0},{2,3},{3,2},{4,5},{5,4},{6,7},{7,6},{8,9},{9,8},{10,11... | collective-permute-start | bytes 786440 | tf_op jit(solution)/shard_map/ppermute | solution.py:193
  74.3 1.6 %collective-permute-start.18 = (bf16[256,512]{1,0:T(8,128)(2,1)S(1)}, bf16[256,512]{1,0:T(8,128)(2,1)S(1)}, u32[]{:S(2)}, u32[]{:S(2)}) collective-permute-start(bf16[256,512]{1,0:T(8,128)(2,1)S(1)} %get-tuple-element.60), channel_id=1, source_target_pairs={{0,1},{1,0},{2,3},{3,2},{4,5},{5,4},{6,7},{7,6},{8,9},{9,8},{10,11... | collective-permute-start | bytes 786440 | tf_op jit(solution)/shard_map/ppermute | solution.py:193
  74.4 1.9 %collective-permute-start.19 = (bf16[256,512]{1,0:T(8,128)(2,1)S(1)}, bf16[256,512]{1,0:T(8,128)(2,1)S(1)}, u32[]{:S(2)}, u32[]{:S(2)}) collective-permute-start(bf16[256,512]{1,0:T(8,128)(2,1)S(1)} %get-tuple-element.59), channel_id=1, source_target_pairs={{0,1},{1,0},{2,3},{3,2},{4,5},{5,4},{6,7},{7,6},{8,9},{9,8},{10,11... | collective-permute-start | bytes 786440 | tf_op jit(solution)/shard_map/ppermute | solution.py:193

commit v6 on v5

--- a/solution.py
+++ b/solution.py
@@ -139,13 +139,13 @@
 
 def last_slot(first, keep_mask, total, late, mine, other, product=None):
     rows, cols = total.shape
-    (tall, depth), tile = mine.shape, other[0].shape[0]
+    (tile, depth), steps = mine[0].shape, len(mine)
     size = rows // keep_mask.shape[1]
-    per, steps = tile // size, tall // tile
+    per = tile // size
     given = () if product is None else (product,)
 
-    def body(keep_hbm, total_ref, late_ref, mine_ref, *refs):
-        others, (out_ref, keep_ref, sem) = refs[:steps], refs[-3:]
+    def body(keep_hbm, total_ref, late_ref, *refs):
+        pieces, (out_ref, keep_ref, sem) = refs[: 2 * steps], refs[-3:]
         step = pl.program_id(0)
         copy = pltpu.make_async_copy(keep_hbm, keep_ref, sem)
 
@@ -154,13 +154,13 @@
             copy.start()
 
         core = lax.axis_index("col") % 2
-        near = late_ref[pl.ds(pl.multiple_of(core * depth, depth), depth), :]
-        far = late_ref[pl.ds(pl.multiple_of((1 - core) * depth, depth), depth), :]
-        other_now = others[0][...]
-        for i in range(1, steps):
-            other_now = jnp.where(step == i, others[i][...], other_now)
-        sums = total_ref[...] + jnp.dot(mine_ref[...], near, preferred_element_type=jnp.float32)
-        sums += jnp.dot(other_now, far, preferred_element_type=jnp.float32)
+        sums = total_ref[...]
+        for w, c in ((0, core), (1, 1 - core)):
+            now = pieces[w * steps][...]
+            for i in range(1, steps):
+                now = jnp.where(step == i, pieces[w * steps + i][...], now)
+            part = late_ref[pl.ds(pl.multiple_of(c * depth, depth), depth), :]
+            sums += jnp.dot(now, part, preferred_element_type=jnp.float32)
 
         @pl.when(step == 0)
         def _():
@@ -175,16 +175,14 @@
     return pl.pallas_call(
         body,
         grid=(steps,),
-        in_specs=[FAR, here, whole(late), pl.BlockSpec((tile, depth), lambda i: (i, 0))]
-        + [whole(v) for v in other]
-        + [HOME] * len(given),
+        in_specs=[FAR, here, whole(late)] + [whole(v) for v in (*mine, *other)] + [HOME] * len(given),
         out_specs=here,
         out_shape=jax.ShapeDtypeStruct((rows, cols), jnp.bfloat16),
         scratch_shapes=[pltpu.SMEM(keep_mask.shape, jnp.int32), COPIES(())],
-        input_output_aliases={4 + steps: 0} if given else {},
+        input_output_aliases={3 + 2 * steps: 0} if given else {},
         compiler_params=pltpu.CompilerParams(vmem_limit_bytes=10 * MIB),
         cost_estimate=SMALL,
-    )(keep_mask, total, late, mine, *other, *given)
+    )(keep_mask, total, late, *mine, *other, *given)
 
 
 def on_grid(left, right, a_pattern, b_pattern, keep_mask):
@@ -211,18 +209,24 @@
     e1 = [cross(r1[0])]
     bd = [to_y(bx[:half]), to_x(by[half:])]
     r2[0], e1[0], r1[1] = tied(r2[0], e1[0], r1[1])
-    r3 = [on(r2[0])]
+    quarter = half // 2
+    parts = lambda v: [v[:quarter], v[quarter:]]
+    r3 = [on(v) for v in parts(r2[0])]
     e1.append(cross(r1[1]))
     r2[1], e1[1], r2[0], *bd = tied(r2[1], e1[1], r2[0], *bd)
-    quarter = half // 2
-    parts = lambda v: [v[:quarter], v[quarter:]]
-    r3.append(on(r2[1]))
+    r3 += [on(v) for v in parts(r2[1])]
     e2 = [cross(v) for v in r2]
-    r3[0], *e2 = tied(r3[0], *e2)
+    e3 = [cross(r3[0])]
+    r3[1], e3[0], *e2 = tied(r3[1], e3[0], *e2)
+    e3.append(cross(r3[1]))
     total, late = early_slots((((a0, a1), ea), (r1, e1), (r2, e2)), ((b,), (bx,), (by,), bd))
-    product = last_slot(0, keep_mask.T, total, late, r3[0], [cross(v) for v in parts(r3[0])])
-    r3[1], product = tied(r3[1], product)
-    return last_slot(half, keep_mask.T, total, late, r3[1], [cross(v) for v in parts(r3[1])], product)
+    r3[2], e3[1], total, late = tied(r3[2], e3[1], total, late)
+    e3.append(cross(r3[2]))
+    keep = keep_mask.T
+    product = last_slot(0, keep, total, late, r3[:2], e3[:2])
+    r3[3], e3[2], product = tied(r3[3], e3[2], product)
+    product = last_slot(half, keep, total, late, r3[2:3], e3[2:3], product)
+    return last_slot(half + quarter, keep, total, late, r3[3:], [cross(r3[3])], product)
 
 
 def on_any(left, right, a_pattern, b_pattern, keep_mask):

time: 78.3 us -> 77.5 us (0.990)
  waiting for transfers between devices: 45.5 us -> 41.1 us
  starting transfers between devices: 19.7 us -> 22.4 us
  Pallas kernels: 12.7 us -> 13.5 us
    ppermute x6 -> x8, starting transfers between devices: 12.8 us -> 16.3 us  [on_grid(): on = lambda v: lax.ppermute(v, 'col', ring)]
    ppermute x6 -> x8, waiting for transfers between devices: 32.1 us -> 29.2 us  [on_grid(): on = lambda v: lax.ppermute(v, 'col', ring)]
    ppermute x10, waiting for transfers between devices: 1.42 us -> 0.09 us  [on_grid(): cross = lambda v: lax.ppermute(v, 'col', [(i, i ^ 1) for i in range(8)])]
    pallas_call x2 -> x3, Pallas kernels: 3.95 us -> 4.77 us  [last_slot(): pl.pallas_call(body, grid=(steps,), in_specs=[FAR, here, whole(late)] + [...]
    ppermute x10, starting transfers between devices: 1.65 us -> 0.83 us  [on_grid(): cross = lambda v: lax.ppermute(v, 'col', [(i, i ^ 1) for i in range(8)])]
  transfers between devices with their start and end apart: 20 -> 22, of which waited for: 12 -> 12; matrix products, arithmetic and copies ran while one was open for 0% -> 0% of each run, Pallas kernels for 11% -> 13%
where the time goes in v6:
time: 77.5 us; the launch traced here: 77.3 us
  waiting for transfers between devices  41.1 us (53%)
  starting transfers between devices  22.4 us (29%)
  Pallas kernels  13.5 us (17%)
    ppermute x8, waiting for transfers between devices, on_grid(): on = lambda v: lax.ppermute(v, 'col', ring)  29.2 us
    ppermute x8, starting transfers between devices, on_grid(): on = lambda v: lax.ppermute(v, 'col', ring)  16.3 us
    ppermute x2, waiting for transfers between devices, on_grid(): to_y = lambda v: lax.ppermute(v, 'row', [(i, i ^ 2) for i in range(4)])  7.4 us
    pallas_call x3, Pallas kernels, last_slot(): pl.pallas_call(body, grid=(steps,), in_specs=[FAR, here, whole(late)] + [...  4.77 us
    pallas_call x1, Pallas kernels, early_slots(): pl.pallas_call(body, in_specs=specs, out_specs=[NEAR, NEAR], out_shape=[j...  4.49 us
    ppermute x2, waiting for transfers between devices, on_grid(): to_x = lambda v: lax.ppermute(v, 'row', [(i, i ^ 1) for i in range(4)])  4.36 us
    pallas_call x2, Pallas kernels, masked(): pl.pallas_call(body, in_specs=[FAR] * (2 * k), out_specs=[HOME] * n, out_...  4.23 us
    ppermute x2, starting transfers between devices, on_grid(): to_y = lambda v: lax.ppermute(v, 'row', [(i, i ^ 2) for i in range(4)])  3.1 us
  transfers between devices with their start and end apart: 22, of which 12 were waited for; matrix products, arithmetic and copies ran while one was open for 0% of the time, Pallas kernels for 13%

profile of v6, /device:TPU:0, one launch (start us, length us, event | category | flops | bytes accessed | tf_op | source)
XLA Modules:
  0.0 77.3 jit_solution(6892914153215556017)
XLA Ops:
  0.0 1.9 %shard_map.55.refs_5_ = bf16[512,512]{1,0:T(8,128)(2,1)} custom-call(bf16[1024,512]{1,0:T(8,128)(2,1)} %refs_0_.2, s32[4,8]{1,0:T(4,128)} %bitcast.6), custom_call_target="tpu_custom_call" | custom-call | flops 1 | bytes 1 | tf_op jit(solution)/shard_map/pallas_call | solution.py:60
  1.9 3.1 %collective-permute-start.1 = (bf16[512,512]{1,0:T(8,128)(2,1)}, bf16[512,512]{1,0:T(8,128)(2,1)S(1)}, u32[]{:S(2)}, u32[]{:S(2)}) collective-permute-start(bf16[512,512]{1,0:T(8,128)(2,1)} %shard_map.55.refs_5_), channel_id=1, source_target_pairs={{0,2},{1,3},{2,6},{3,7},{6,4},{7,5},{4,0},{5,1},{8,10},{9,11},{10,... | collective-permute-start | bytes 1572872 | tf_op jit(solution)/shard_map/ppermute | solution.py:190
  4.9 0.0 collective-permute-start.2
  4.9 2.4 %shard_map.56 = (bf16[512,512]{1,0:T(8,128)(2,1)}, bf16[1024,512]{1,0:T(8,128)(2,1)}) custom-call(bf16[1024,512]{1,0:T(8,128)(2,1)} %refs_0_.2, bf16[1024,512]{1,0:T(8,128)(2,1)} %refs_1_.1, s32[4,8]{1,0:T(4,128)} %bitcast.7, s32[4,8]{1,0:T(4,128)} %bitcast.8), custom_call_target="tpu_custom_call" | custom-call | flops 1 | bytes 1 | tf_op jit(solution)/shard_map/pallas_call | solution.py:60
  7.3 1.6 %collective-permute-start.4 = (bf16[1024,512]{1,0:T(8,128)(2,1)}, bf16[1024,512]{1,0:T(8,128)(2,1)S(1)}, u32[]{:S(2)}, u32[]{:S(2)}) collective-permute-start(bf16[1024,512]{1,0:T(8,128)(2,1)} %get-tuple-element.42.refs_0_), channel_id=1, source_target_pairs={{0,8},{8,0},{16,24},{24,16},{1,9},{9,1},{17,25},{25,17},{2,10},{10... | collective-permute-start | bytes 3145736 | tf_op jit(solution)/shard_map/ppermute | solution.py:192
  8.9 1.5 %collective-permute-start.5 = (bf16[1024,512]{1,0:T(8,128)(2,1)}, bf16[1024,512]{1,0:T(8,128)(2,1)S(1)}, u32[]{:S(2)}, u32[]{:S(2)}) collective-permute-start(bf16[1024,512]{1,0:T(8,128)(2,1)} %get-tuple-element.42.refs_0_), channel_id=1, source_target_pairs={{0,16},{8,24},{16,0},{24,8},{1,17},{9,25},{17,1},{25,9},{2,18},{10... | collective-permute-start | bytes 3145736 | tf_op jit(solution)/shard_map/ppermute | solution.py:193
  10.4 0.0 copy-start
  10.4 0.0 copy-start.1
  10.4 0.0 copy-start.2
  10.4 2.6 %collective-permute-start = (bf16[512,512]{1,0:T(8,128)(2,1)}, bf16[512,512]{1,0:T(8,128)(2,1)S(1)}, u32[]{:S(2)}, u32[]{:S(2)}) collective-permute-start(bf16[512,512]{1,0:T(8,128)(2,1)} %get-tuple-element.41.refs_6_), channel_id=1, source_target_pairs={{0,2},{1,3},{2,6},{3,7},{6,4},{7,5},{4,0},{5,1},{8,10},{9,11},{10,... | collective-permute-start | bytes 1572872 | tf_op jit(solution)/shard_map/ppermute | solution.py:190
  13.0 5.9 %collective-permute-done.1.refs_9_ = bf16[512,512]{1,0:T(8,128)(2,1)S(1)} collective-permute-done((bf16[512,512]{1,0:T(8,128)(2,1)}, bf16[512,512]{1,0:T(8,128)(2,1)S(1)}, u32[]{:S(2)}, u32[]{:S(2)}) %collective-permute-start.1) | collective-permute-done | bytes 524320 | tf_op jit(solution)/shard_map/ppermute | solution.py:190
  18.9 0.0 collective-permute-done.2.refs_7_
  18.9 0.0 collective-permute-start.3
  18.9 1.3 %collective-permute-start.7 = (bf16[512,512]{1,0:T(8,128)(2,1)S(1)}, bf16[512,512]{1,0:T(8,128)(2,1)S(1)}, u32[]{:S(2)}, u32[]{:S(2)}) collective-permute-start(bf16[512,512]{1,0:T(8,128)(2,1)S(1)} %collective-permute-done.1.refs_9_), channel_id=1, source_target_pairs={{0,2},{1,3},{2,6},{3,7},{6,4},{7,5},{4,0},{5,1},{8,10},{9,11},{10,... | collective-permute-start | bytes 1572872 | tf_op jit(solution)/shard_map/ppermute | solution.py:190
  20.2 10.0 %collective-permute-done.refs_10_ = bf16[512,512]{1,0:T(8,128)(2,1)S(1)} collective-permute-done((bf16[512,512]{1,0:T(8,128)(2,1)}, bf16[512,512]{1,0:T(8,128)(2,1)S(1)}, u32[]{:S(2)}, u32[]{:S(2)}) %collective-permute-start) | collective-permute-done | bytes 524320 | tf_op jit(solution)/shard_map/ppermute | solution.py:190
  30.2 0.0 collective-permute-done.3.refs_8_
  30.2 3.0 %collective-permute-done.4.refs_1_ = bf16[1024,512]{1,0:T(8,128)(2,1)S(1)} collective-permute-done((bf16[1024,512]{1,0:T(8,128)(2,1)}, bf16[1024,512]{1,0:T(8,128)(2,1)S(1)}, u32[]{:S(2)}, u32[]{:S(2)}) %collective-permute-start.4) | collective-permute-done | bytes 1048608 | tf_op jit(solution)/shard_map/ppermute | solution.py:192
  33.2 1.2 %collective-permute-done.5.refs_2_ = bf16[1024,512]{1,0:T(8,128)(2,1)S(1)} collective-permute-done((bf16[1024,512]{1,0:T(8,128)(2,1)}, bf16[1024,512]{1,0:T(8,128)(2,1)S(1)}, u32[]{:S(2)}, u32[]{:S(2)}) %collective-permute-start.5) | collective-permute-done | bytes 1048608 | tf_op jit(solution)/shard_map/ppermute | solution.py:193
  34.4 0.0 collective-permute-start.8
  34.4 1.6 %collective-permute-start.10 = (bf16[512,512]{1,0:T(8,128)(2,1)S(1)}, bf16[512,512]{1,0:T(8,128)(2,1)S(1)}, u32[]{:S(2)}, u32[]{:S(2)}) collective-permute-start(bf16[512,512]{1,0:T(8,128)(2,1)S(1)} %slice.18), channel_id=1, source_target_pairs={{0,16},{8,24},{16,0},{24,8},{1,17},{9,25},{17,1},{25,9},{2,18},{10... | collective-permute-start | bytes 1572872 | tf_op jit(solution)/shard_map/ppermute | solution.py:193
  36.1 0.6 collective-permute-start.11
  36.7 2.6 %collective-permute-start.6 = (bf16[512,512]{1,0:T(8,128)(2,1)S(1)}, bf16[512,512]{1,0:T(8,128)(2,1)S(1)}, u32[]{:S(2)}, u32[]{:S(2)}) collective-permute-start(bf16[512,512]{1,0:T(8,128)(2,1)S(1)} %collective-permute-done.refs_10_), channel_id=1, source_target_pairs={{0,2},{1,3},{2,6},{3,7},{6,4},{7,5},{4,0},{5,1},{8,10},{9,11},{10,... | collective-permute-start | bytes 1572872 | tf_op jit(solution)/shard_map/ppermute | solution.py:190
  39.2 1.7 %collective-permute-done.7.refs_13_ = bf16[512,512]{1,0:T(8,128)(2,1)S(1)} collective-permute-done((bf16[512,512]{1,0:T(8,128)(2,1)S(1)}, bf16[512,512]{1,0:T(8,128)(2,1)S(1)}, u32[]{:S(2)}, u32[]{:S(2)}) %collective-permute-start.7) | collective-permute-done | bytes 524320 | tf_op jit(solution)/shard_map/ppermute | solution.py:190
  41.0 0.0 collective-permute-done.8.refs_11_
  41.0 0.0 collective-permute-start.9
  41.0 1.6 %collective-permute-start.14 = (bf16[256,512]{1,0:T(8,128)(2,1)S(1)}, bf16[256,512]{1,0:T(8,128)(2,1)S(1)}, u32[]{:S(2)}, u32[]{:S(2)}) collective-permute-start(bf16[256,512]{1,0:T(8,128)(2,1)S(1)} %get-tuple-element.73), channel_id=1, source_target_pairs={{0,2},{1,3},{2,6},{3,7},{6,4},{7,5},{4,0},{5,1},{8,10},{9,11},{10,... | collective-permute-start | bytes 786440 | tf_op jit(solution)/shard_map/ppermute | solution.py:190
  42.6 6.2 %collective-permute-done.10.refs_3_ = bf16[512,512]{1,0:T(8,128)(2,1)S(1)} collective-permute-done((bf16[512,512]{1,0:T(8,128)(2,1)S(1)}, bf16[512,512]{1,0:T(8,128)(2,1)S(1)}, u32[]{:S(2)}, u32[]{:S(2)}) %collective-permute-start.10) | collective-permute-done | bytes 524320 | tf_op jit(solution)/shard_map/ppermute | solution.py:193
  48.8 1.3 %collective-permute-done.11.refs_4_ = bf16[512,512]{1,0:T(8,128)(2,1)S(1)} collective-permute-done((bf16[512,512]{1,0:T(8,128)(2,1)S(1)}, bf16[512,512]{1,0:T(8,128)(2,1)S(1)}, u32[]{:S(2)}, u32[]{:S(2)}) %collective-permute-start.11) | collective-permute-done | bytes 524320 | tf_op jit(solution)/shard_map/ppermute | solution.py:192
  50.2 2.2 %collective-permute-done.6.refs_14_ = bf16[512,512]{1,0:T(8,128)(2,1)S(1)} collective-permute-done((bf16[512,512]{1,0:T(8,128)(2,1)S(1)}, bf16[512,512]{1,0:T(8,128)(2,1)S(1)}, u32[]{:S(2)}, u32[]{:S(2)}) %collective-permute-start.6) | collective-permute-done | bytes 524320 | tf_op jit(solution)/shard_map/ppermute | solution.py:190
  52.3 0.0 collective-permute-done.9.refs_12_
  52.4 0.0 collective-permute-start.16
  52.4 0.5 collective-permute-start.17
  52.9 1.7 %collective-permute-start.13 = (bf16[256,512]{1,0:T(8,128)(2,1)S(1)}, bf16[256,512]{1,0:T(8,128)(2,1)S(1)}, u32[]{:S(2)}, u32[]{:S(2)}) collective-permute-start(bf16[256,512]{1,0:T(8,128)(2,1)S(1)} %get-tuple-element.74), channel_id=1, source_target_pairs={{0,2},{1,3},{2,6},{3,7},{6,4},{7,5},{4,0},{5,1},{8,10},{9,11},{10,... | collective-permute-start | bytes 786440 | tf_op jit(solution)/shard_map/ppermute | solution.py:190
  54.6 3.4 %collective-permute-done.14.refs_0_ = bf16[256,512]{1,0:T(8,128)(2,1)S(1)} collective-permute-done((bf16[256,512]{1,0:T(8,128)(2,1)S(1)}, bf16[256,512]{1,0:T(8,128)(2,1)S(1)}, u32[]{:S(2)}, u32[]{:S(2)}) %collective-permute-start.14) | collective-permute-done | bytes 262176 | tf_op jit(solution)/shard_map/ppermute | solution.py:190
  58.0 0.0 collective-permute-start.15
  58.0 1.7 %collective-permute-start.12 = (bf16[256,512]{1,0:T(8,128)(2,1)S(1)}, bf16[256,512]{1,0:T(8,128)(2,1)S(1)}, u32[]{:S(2)}, u32[]{:S(2)}) collective-permute-start(bf16[256,512]{1,0:T(8,128)(2,1)S(1)} %get-tuple-element.72), channel_id=1, source_target_pairs={{0,2},{1,3},{2,6},{3,7},{6,4},{7,5},{4,0},{5,1},{8,10},{9,11},{10,... | collective-permute-start | bytes 786440 | tf_op jit(solution)/shard_map/ppermute | solution.py:190
  59.8 3.8 %collective-permute-done.13.refs_1_ = bf16[256,512]{1,0:T(8,128)(2,1)S(1)} collective-permute-done((bf16[256,512]{1,0:T(8,128)(2,1)S(1)}, bf16[256,512]{1,0:T(8,128)(2,1)S(1)}, u32[]{:S(2)}, u32[]{:S(2)}) %collective-permute-start.13) | collective-permute-done | bytes 262176 | tf_op jit(solution)/shard_map/ppermute | solution.py:190
  63.6 0.0 collective-permute-done.15.refs_2_
  63.6 0.0 collective-permute-done.16.refs_15_
  63.6 0.0 collective-permute-done.17.refs_16_
  63.6 0.1 collective-permute-start.18
  63.7 0.0 copy-start.3
  63.7 1.7 %collective-permute-start.19 = (bf16[256,512]{1,0:T(8,128)(2,1)S(1)}, bf16[256,512]{1,0:T(8,128)(2,1)S(1)}, u32[]{:S(2)}, u32[]{:S(2)}) collective-permute-start(bf16[256,512]{1,0:T(8,128)(2,1)S(1)} %get-tuple-element.71), channel_id=1, source_target_pairs={{0,2},{1,3},{2,6},{3,7},{6,4},{7,5},{4,0},{5,1},{8,10},{9,11},{10,... | collective-permute-start | bytes 786440 | tf_op jit(solution)/shard_map/ppermute | solution.py:190
  65.4 0.0 copy-done
  65.4 0.0 copy-done.1
  65.4 0.0 copy-done.2
  65.4 4.5 %shard_map.57 = (f32[1024,512]{1,0:T(8,128)S(1)}, bf16[1024,512]{1,0:T(8,128)(2,1)S(1)}) custom-call(bf16[1024,512]{1,0:T(8,128)(2,1)S(1)} %copy-done.1, bf16[1024,512]{1,0:T(8,128)(2,1)S(1)} %collective-permute-done.4.refs_1_, bf16[1024,512]{1,0:T(8,128)(2,1)S(1)} %collective-permute-done.5.refs_2_, bf16[512,512]{1,0:T(8,128)(2,1)S(1)} %collective-permute-done.10.refs_3_, ...), custom_call_target="tpu_custom_call" | custom-call | flops 1 | bytes 1 | tf_op jit(solution)/shard_map/pallas_call | solution.py:125
  69.9 0.0 collective-permute-done.12.refs_0_
  69.9 0.0 collective-permute-done.18.refs_3_
  70.0 0.2 collective-permute-start.20
  70.2 0.0 copy-done.3
  70.2 1.9 %shard_map.58.refs_2_ = bf16[1024,512]{1,0:T(8,128)(2,1)} custom-call(s32[4,8]{1,0:T(4,128)S(1)} %bitcast.3, f32[1024,512]{1,0:T(8,128)S(1)} %get-tuple-element.63.total_ref, bf16[1024,512]{1,0:T(8,128)(2,1)S(1)} %get-tuple-element.64.late_ref, bf16[256,512]{1,0:T(8,128)(2,1)S(1)} %collective-permute-done.14.refs_0_, ...), custom_call_target="tpu_custom_call" | custom-call | flops 1 | bytes 1 | tf_op jit(solution)/shard_map/pallas_call | solution.py:175
  72.0 2.2 %collective-permute-done.19.refs_0_ = bf16[256,512]{1,0:T(8,128)(2,1)S(1)} collective-permute-done((bf16[256,512]{1,0:T(8,128)(2,1)S(1)}, bf16[256,512]{1,0:T(8,128)(2,1)S(1)}, u32[]{:S(2)}, u32[]{:S(2)}) %collective-permute-start.19) | collective-permute-done | bytes 262176 | tf_op jit(solution)/shard_map/ppermute | solution.py:190
  74.3 0.0 collective-permute-done.20.refs_1_
  74.3 0.0 collective-permute-start.21
  74.3 1.5 %shard_map.59.refs_2_ = bf16[1024,512]{1,0:T(8,128)(2,1)} custom-call(s32[4,8]{1,0:T(4,128)S(1)} %bitcast.4, f32[1024,512]{1,0:T(8,128)S(1)} %get-tuple-element.63.total_ref, bf16[1024,512]{1,0:T(8,128)(2,1)S(1)} %get-tuple-element.64.late_ref, bf16[256,512]{1,0:T(8,128)(2,1)S(1)} %collective-permute-done.12.refs_0_, ...), custom_call_target="tpu_custom_call", output_to_operand_aliasing={{}: (5, {})} | custom-call | flops 1 | bytes 1 | tf_op jit(solution)/shard_map/pallas_call | solution.py:175
  75.7 0.1 collective-permute-done.21.refs_1_
  75.8 1.5 %shard_map.60 = bf16[1024,512]{1,0:T(8,128)(2,1)} custom-call(s32[4,8]{1,0:T(4,128)S(1)} %bitcast.5, f32[1024,512]{1,0:T(8,128)S(1)} %get-tuple-element.63.total_ref, bf16[1024,512]{1,0:T(8,128)(2,1)S(1)} %get-tuple-element.64.late_ref, bf16[256,512]{1,0:T(8,128)(2,1)S(1)} %collective-permute-done.19.refs_0_, ...), custom_call_target="tpu_custom_call", output_to_operand_aliasing={{}: (5, {})} | custom-call | flops 1 | bytes 1 | tf_op jit(solution)/shard_map/pallas_call | solution.py:175
  (4 shorter events, 0.1 us)
Async XLA Ops:
  1.9 17.1 %collective-permute-start.1 = (bf16[512,512]{1,0:T(8,128)(2,1)}, bf16[512,512]{1,0:T(8,128)(2,1)S(1)}, u32[]{:S(2)}, u32[]{:S(2)}) collective-permute-start(bf16[512,512]{1,0:T(8,128)(2,1)} %shard_map.55.refs_5_), channel_id=1, source_target_pairs={{0,2},{1,3},{2,6},{3,7},{6,4},{7,5},{4,0},{5,1},{8,10},{9,11},{10,... | collective-permute-start | bytes 1572872 | tf_op jit(solution)/shard_map/ppermute | solution.py:190
  4.9 14.0 %collective-permute-start.2 = (bf16[512,512]{1,0:T(8,128)(2,1)}, bf16[512,512]{1,0:T(8,128)(2,1)S(1)}, u32[]{:S(2)}, u32[]{:S(2)}) collective-permute-start(bf16[512,512]{1,0:T(8,128)(2,1)} %shard_map.55.refs_5_), channel_id=1, source_target_pairs={{0,1},{1,0},{2,3},{3,2},{4,5},{5,4},{6,7},{7,6},{8,9},{9,8},{10,11... | collective-permute-start | bytes 1572872 | tf_op jit(solution)/shard_map/ppermute | solution.py:191
  7.3 25.8 %collective-permute-start.4 = (bf16[1024,512]{1,0:T(8,128)(2,1)}, bf16[1024,512]{1,0:T(8,128)(2,1)S(1)}, u32[]{:S(2)}, u32[]{:S(2)}) collective-permute-start(bf16[1024,512]{1,0:T(8,128)(2,1)} %get-tuple-element.42.refs_0_), channel_id=1, source_target_pairs={{0,8},{8,0},{16,24},{24,16},{1,9},{9,1},{17,25},{25,17},{2,10},{10... | collective-permute-start | bytes 3145736 | tf_op jit(solution)/shard_map/ppermute | solution.py:192
  8.9 25.5 %collective-permute-start.5 = (bf16[1024,512]{1,0:T(8,128)(2,1)}, bf16[1024,512]{1,0:T(8,128)(2,1)S(1)}, u32[]{:S(2)}, u32[]{:S(2)}) collective-permute-start(bf16[1024,512]{1,0:T(8,128)(2,1)} %get-tuple-element.42.refs_0_), channel_id=1, source_target_pairs={{0,16},{8,24},{16,0},{24,8},{1,17},{9,25},{17,1},{25,9},{2,18},{10... | collective-permute-start | bytes 3145736 | tf_op jit(solution)/shard_map/ppermute | solution.py:193
  10.4 55.0 %copy-start = (bf16[512,512]{1,0:T(8,128)(2,1)S(1)}, bf16[512,512]{1,0:T(8,128)(2,1)}, u32[]{:S(2)}) copy-start(bf16[512,512]{1,0:T(8,128)(2,1)} %shard_map.55.refs_5_) | copy-start | bytes 1572868
  10.4 55.0 %copy-start.1 = (bf16[1024,512]{1,0:T(8,128)(2,1)S(1)}, bf16[1024,512]{1,0:T(8,128)(2,1)}, u32[]{:S(2)}) copy-start(bf16[1024,512]{1,0:T(8,128)(2,1)} %get-tuple-element.42.refs_0_) | copy-start | bytes 3145732
  10.4 55.0 %copy-start.2 = (bf16[512,512]{1,0:T(8,128)(2,1)S(1)}, bf16[512,512]{1,0:T(8,128)(2,1)}, u32[]{:S(2)}) copy-start(bf16[512,512]{1,0:T(8,128)(2,1)} %get-tuple-element.41.refs_6_) | copy-start | bytes 1572868
  10.4 19.7 %collective-permute-start = (bf16[512,512]{1,0:T(8,128)(2,1)}, bf16[512,512]{1,0:T(8,128)(2,1)S(1)}, u32[]{:S(2)}, u32[]{:S(2)}) collective-permute-start(bf16[512,512]{1,0:T(8,128)(2,1)} %get-tuple-element.41.refs_6_), channel_id=1, source_target_pairs={{0,2},{1,3},{2,6},{3,7},{6,4},{7,5},{4,0},{5,1},{8,10},{9,11},{10,... | collective-permute-start | bytes 1572872 | tf_op jit(solution)/shard_map/ppermute | solution.py:190
  18.9 11.2 %collective-permute-start.3 = (bf16[512,512]{1,0:T(8,128)(2,1)}, bf16[512,512]{1,0:T(8,128)(2,1)S(1)}, u32[]{:S(2)}, u32[]{:S(2)}) collective-permute-start(bf16[512,512]{1,0:T(8,128)(2,1)} %get-tuple-element.41.refs_6_), channel_id=1, source_target_pairs={{0,1},{1,0},{2,3},{3,2},{4,5},{5,4},{6,7},{7,6},{8,9},{9,8},{10,11... | collective-permute-start | bytes 1572872 | tf_op jit(solution)/shard_map/ppermute | solution.py:191
  18.9 22.0 %collective-permute-start.7 = (bf16[512,512]{1,0:T(8,128)(2,1)S(1)}, bf16[512,512]{1,0:T(8,128)(2,1)S(1)}, u32[]{:S(2)}, u32[]{:S(2)}) collective-permute-start(bf16[512,512]{1,0:T(8,128)(2,1)S(1)} %collective-permute-done.1.refs_9_), channel_id=1, source_target_pairs={{0,2},{1,3},{2,6},{3,7},{6,4},{7,5},{4,0},{5,1},{8,10},{9,11},{10,... | collective-permute-start | bytes 1572872 | tf_op jit(solution)/shard_map/ppermute | solution.py:190
  34.4 6.6 %collective-permute-start.8 = (bf16[512,512]{1,0:T(8,128)(2,1)S(1)}, bf16[512,512]{1,0:T(8,128)(2,1)S(1)}, u32[]{:S(2)}, u32[]{:S(2)}) collective-permute-start(bf16[512,512]{1,0:T(8,128)(2,1)S(1)} %collective-permute-done.1.refs_9_), channel_id=1, source_target_pairs={{0,1},{1,0},{2,3},{3,2},{4,5},{5,4},{6,7},{7,6},{8,9},{9,8},{10,11... | collective-permute-start | bytes 1572872 | tf_op jit(solution)/shard_map/ppermute | solution.py:191
  34.4 14.4 %collective-permute-start.10 = (bf16[512,512]{1,0:T(8,128)(2,1)S(1)}, bf16[512,512]{1,0:T(8,128)(2,1)S(1)}, u32[]{:S(2)}, u32[]{:S(2)}) collective-permute-start(bf16[512,512]{1,0:T(8,128)(2,1)S(1)} %slice.18), channel_id=1, source_target_pairs={{0,16},{8,24},{16,0},{24,8},{1,17},{9,25},{17,1},{25,9},{2,18},{10... | collective-permute-start | bytes 1572872 | tf_op jit(solution)/shard_map/ppermute | solution.py:193
  36.1 14.1 %collective-permute-start.11 = (bf16[512,512]{1,0:T(8,128)(2,1)S(1)}, bf16[512,512]{1,0:T(8,128)(2,1)S(1)}, u32[]{:S(2)}, u32[]{:S(2)}) collective-permute-start(bf16[512,512]{1,0:T(8,128)(2,1)S(1)} %slice.19), channel_id=1, source_target_pairs={{0,8},{8,0},{16,24},{24,16},{1,9},{9,1},{17,25},{25,17},{2,10},{10... | collective-permute-start | bytes 1572872 | tf_op jit(solution)/shard_map/ppermute | solution.py:192
  36.7 15.7 %collective-permute-start.6 = (bf16[512,512]{1,0:T(8,128)(2,1)S(1)}, bf16[512,512]{1,0:T(8,128)(2,1)S(1)}, u32[]{:S(2)}, u32[]{:S(2)}) collective-permute-start(bf16[512,512]{1,0:T(8,128)(2,1)S(1)} %collective-permute-done.refs_10_), channel_id=1, source_target_pairs={{0,2},{1,3},{2,6},{3,7},{6,4},{7,5},{4,0},{5,1},{8,10},{9,11},{10,... | collective-permute-start | bytes 1572872 | tf_op jit(solution)/shard_map/ppermute | solution.py:190
  41.0 11.4 %collective-permute-start.9 = (bf16[512,512]{1,0:T(8,128)(2,1)S(1)}, bf16[512,512]{1,0:T(8,128)(2,1)S(1)}, u32[]{:S(2)}, u32[]{:S(2)}) collective-permute-start(bf16[512,512]{1,0:T(8,128)(2,1)S(1)} %collective-permute-done.refs_10_), channel_id=1, source_target_pairs={{0,1},{1,0},{2,3},{3,2},{4,5},{5,4},{6,7},{7,6},{8,9},{9,8},{10,11... | collective-permute-start | bytes 1572872 | tf_op jit(solution)/shard_map/ppermute | solution.py:191
  41.0 17.0 %collective-permute-start.14 = (bf16[256,512]{1,0:T(8,128)(2,1)S(1)}, bf16[256,512]{1,0:T(8,128)(2,1)S(1)}, u32[]{:S(2)}, u32[]{:S(2)}) collective-permute-start(bf16[256,512]{1,0:T(8,128)(2,1)S(1)} %get-tuple-element.73), channel_id=1, source_target_pairs={{0,2},{1,3},{2,6},{3,7},{6,4},{7,5},{4,0},{5,1},{8,10},{9,11},{10,... | collective-permute-start | bytes 786440 | tf_op jit(solution)/shard_map/ppermute | solution.py:190
  52.4 11.2 %collective-permute-start.16 = (bf16[512,512]{1,0:T(8,128)(2,1)S(1)}, bf16[512,512]{1,0:T(8,128)(2,1)S(1)}, u32[]{:S(2)}, u32[]{:S(2)}) collective-permute-start(bf16[512,512]{1,0:T(8,128)(2,1)S(1)} %collective-permute-done.7.refs_13_), channel_id=1, source_target_pairs={{0,1},{1,0},{2,3},{3,2},{4,5},{5,4},{6,7},{7,6},{8,9},{9,8},{10,11... | collective-permute-start | bytes 1572872 | tf_op jit(solution)/shard_map/ppermute | solution.py:191
  52.4 11.2 %collective-permute-start.17 = (bf16[512,512]{1,0:T(8,128)(2,1)S(1)}, bf16[512,512]{1,0:T(8,128)(2,1)S(1)}, u32[]{:S(2)}, u32[]{:S(2)}) collective-permute-start(bf16[512,512]{1,0:T(8,128)(2,1)S(1)} %collective-permute-done.6.refs_14_), channel_id=1, source_target_pairs={{0,1},{1,0},{2,3},{3,2},{4,5},{5,4},{6,7},{7,6},{8,9},{9,8},{10,11... | collective-permute-start | bytes 1572872 | tf_op jit(solution)/shard_map/ppermute | solution.py:191
  52.9 10.7 %collective-permute-start.13 = (bf16[256,512]{1,0:T(8,128)(2,1)S(1)}, bf16[256,512]{1,0:T(8,128)(2,1)S(1)}, u32[]{:S(2)}, u32[]{:S(2)}) collective-permute-start(bf16[256,512]{1,0:T(8,128)(2,1)S(1)} %get-tuple-element.74), channel_id=1, source_target_pairs={{0,2},{1,3},{2,6},{3,7},{6,4},{7,5},{4,0},{5,1},{8,10},{9,11},{10,... | collective-permute-start | bytes 786440 | tf_op jit(solution)/shard_map/ppermute | solution.py:190
  58.0 5.6 %collective-permute-start.15 = (bf16[256,512]{1,0:T(8,128)(2,1)S(1)}, bf16[256,512]{1,0:T(8,128)(2,1)S(1)}, u32[]{:S(2)}, u32[]{:S(2)}) collective-permute-start(bf16[256,512]{1,0:T(8,128)(2,1)S(1)} %collective-permute-done.14.refs_0_), channel_id=1, source_target_pairs={{0,1},{1,0},{2,3},{3,2},{4,5},{5,4},{6,7},{7,6},{8,9},{9,8},{10,11... | collective-permute-start | bytes 786440 | tf_op jit(solution)/shard_map/ppermute | solution.py:191
  58.0 11.9 %collective-permute-start.12 = (bf16[256,512]{1,0:T(8,128)(2,1)S(1)}, bf16[256,512]{1,0:T(8,128)(2,1)S(1)}, u32[]{:S(2)}, u32[]{:S(2)}) collective-permute-start(bf16[256,512]{1,0:T(8,128)(2,1)S(1)} %get-tuple-element.72), channel_id=1, source_target_pairs={{0,2},{1,3},{2,6},{3,7},{6,4},{7,5},{4,0},{5,1},{8,10},{9,11},{10,... | collective-permute-start | bytes 786440 | tf_op jit(solution)/shard_map/ppermute | solution.py:190
  63.6 6.4 %collective-permute-start.18 = (bf16[256,512]{1,0:T(8,128)(2,1)S(1)}, bf16[256,512]{1,0:T(8,128)(2,1)S(1)}, u32[]{:S(2)}, u32[]{:S(2)}) collective-permute-start(bf16[256,512]{1,0:T(8,128)(2,1)S(1)} %collective-permute-done.13.refs_1_), channel_id=1, source_target_pairs={{0,1},{1,0},{2,3},{3,2},{4,5},{5,4},{6,7},{7,6},{8,9},{9,8},{10,11... | collective-permute-start | bytes 786440 | tf_op jit(solution)/shard_map/ppermute | solution.py:191
  63.7 6.5 %copy-start.3 = (s32[8,4]{0,1:T(4,128)S(1)}, s32[8,4]{0,1:T(4,128)}, u32[]{:S(2)}) copy-start(s32[8,4]{0,1:T(4,128)} %param.9) | copy-start | bytes 388
  63.7 10.6 %collective-permute-start.19 = (bf16[256,512]{1,0:T(8,128)(2,1)S(1)}, bf16[256,512]{1,0:T(8,128)(2,1)S(1)}, u32[]{:S(2)}, u32[]{:S(2)}) collective-permute-start(bf16[256,512]{1,0:T(8,128)(2,1)S(1)} %get-tuple-element.71), channel_id=1, source_target_pairs={{0,2},{1,3},{2,6},{3,7},{6,4},{7,5},{4,0},{5,1},{8,10},{9,11},{10,... | collective-permute-start | bytes 786440 | tf_op jit(solution)/shard_map/ppermute | solution.py:190
  70.0 4.3 %collective-permute-start.20 = (bf16[256,512]{1,0:T(8,128)(2,1)S(1)}, bf16[256,512]{1,0:T(8,128)(2,1)S(1)}, u32[]{:S(2)}, u32[]{:S(2)}) collective-permute-start(bf16[256,512]{1,0:T(8,128)(2,1)S(1)} %collective-permute-done.12.refs_0_), channel_id=1, source_target_pairs={{0,1},{1,0},{2,3},{3,2},{4,5},{5,4},{6,7},{7,6},{8,9},{9,8},{10,11... | collective-permute-start | bytes 786440 | tf_op jit(solution)/shard_map/ppermute | solution.py:191
  74.3 1.5 %collective-permute-start.21 = (bf16[256,512]{1,0:T(8,128)(2,1)S(1)}, bf16[256,512]{1,0:T(8,128)(2,1)S(1)}, u32[]{:S(2)}, u32[]{:S(2)}) collective-permute-start(bf16[256,512]{1,0:T(8,128)(2,1)S(1)} %collective-permute-done.19.refs_0_), channel_id=1, source_target_pairs={{0,1},{1,0},{2,3},{3,2},{4,5},{5,4},{6,7},{7,6},{8,9},{9,8},{10,11... | collective-permute-start | bytes 786440 | tf_op jit(solution)/shard_map/ppermute | solution.py:191

commit v7 on v6

--- a/solution.py
+++ b/solution.py
@@ -75,7 +75,7 @@
     return row, core, (z, before, 3 - z, 3 - before)
 
 
-def early_slots(slots, b):
+def early_slots(slots, b, keep_mask, cut):
     depth = slots[0][0][0].shape[1]
     rows, cols = sum(v.shape[0] for v in b[0]), b[0][0].shape[1]
     dtype = b[0][0].dtype
@@ -84,7 +84,8 @@
     flat = [*(v for shard in b for v in shard), *(v for slot in slots for panel in slot for v in panel)]
 
     def body(*refs):
-        ins, (total_ref, late_ref), (panels, held, sems) = refs[: len(flat)], refs[-5:-3], refs[-3:]
+        ins, (keep_hbm, *totals, near_ref, far_ref, kept_ref) = refs[: len(flat)], refs[len(flat) : -4]
+        panels, held, keep_ref, sems = refs[-4:]
         moves = []
         for i, shard in enumerate(b):
             first = 0
@@ -101,6 +102,7 @@
                     moves.append((ins[len(moves)], panels.at[s, which, first:last]))
                     first = last
             ends.append(len(moves))
+        moves.append((keep_hbm, keep_ref))
         copies = [pltpu.make_async_copy(s, d, sems.at[i]) for i, (s, d) in enumerate(moves)]
         for copy in copies:
             copy.start()
@@ -114,37 +116,53 @@
             here = zs[s] ^ row
             for m in range(rows // tile):
                 some = slice(m * tile, (m + 1) * tile)
-                sums = jnp.zeros((tile, cols), jnp.float32) if s == 0 else total_ref[some, :]
+                low = m * tile >= cut
+                there = totals[low].at[m * tile - low * cut : (m + 1) * tile - low * cut]
+                sums = jnp.zeros((tile, cols), jnp.float32) if s == 0 else there[...]
                 for which in (0, 1):
                     first = pl.multiple_of((core if which == 0 else 1 - core) * depth, depth)
                     part = held[here, pl.ds(first, depth), :]
                     sums += jnp.dot(panels[s, which, some, :], part, preferred_element_type=jnp.float32)
-                total_ref[some, :] = sums
-        late_ref[...] = held[zs[3] ^ row]
+                there[...] = sums
+        here = zs[3] ^ row
+        near_ref[...] = held[here, pl.ds(pl.multiple_of(core * depth, depth), depth), :]
+        far_ref[...] = held[here, pl.ds(pl.multiple_of((1 - core) * depth, depth), depth), :]
+        copies[-1].wait()
+        size = rows // keep_mask.shape[1]
+        for p, q, at in cells((rows - cut) // size, cols // size, size):
+            kept = keep_ref[q, cut // size + p].astype(jnp.float32)
+            kept_ref[at] = jnp.full((size, size), kept, jnp.float32)
 
     return pl.pallas_call(
         body,
-        in_specs=specs,
-        out_specs=[NEAR, NEAR],
-        out_shape=[jax.ShapeDtypeStruct((rows, cols), jnp.float32), jax.ShapeDtypeStruct((rows, cols), dtype)],
+        in_specs=specs + [FAR],
+        out_specs=[NEAR] * 5,
+        out_shape=[
+            jax.ShapeDtypeStruct((cut, cols), jnp.float32),
+            jax.ShapeDtypeStruct((rows - cut, cols), jnp.float32),
+            jax.ShapeDtypeStruct((depth, cols), dtype),
+            jax.ShapeDtypeStruct((depth, cols), dtype),
+            jax.ShapeDtypeStruct((rows - cut, cols), jnp.float32),
+        ],
         scratch_shapes=[
             pltpu.VMEM((len(slots), 2, rows, depth), dtype),
             pltpu.VMEM((4, rows, cols), dtype),
-            COPIES((len(flat),)),
+            pltpu.SMEM(keep_mask.shape, jnp.int32),
+            COPIES((len(flat) + 1,)),
         ],
         compiler_params=pltpu.CompilerParams(vmem_limit_bytes=20 * MIB),
         cost_estimate=SMALL,
-    )(*flat)
-
-
-def last_slot(first, keep_mask, total, late, mine, other, product=None):
-    rows, cols = total.shape
-    (tile, depth), steps = mine[0].shape, len(mine)
-    size = rows // keep_mask.shape[1]
+    )(*flat, keep_mask)
+
+
+def last_slot(first, keep_mask, total, parts, mine, other, product=None):
+    (tile, _), steps, cols = mine[0].shape, len(mine), total.shape[1]
+    size = cols // keep_mask.shape[0]
+    rows = size * keep_mask.shape[1]
     per = tile // size
     given = () if product is None else (product,)
 
-    def body(keep_hbm, total_ref, late_ref, *refs):
+    def body(keep_hbm, total_ref, near_ref, far_ref, *refs):
         pieces, (out_ref, keep_ref, sem) = refs[: 2 * steps], refs[-3:]
         step = pl.program_id(0)
         copy = pltpu.make_async_copy(keep_hbm, keep_ref, sem)
@@ -153,14 +171,12 @@
         def _():
             copy.start()
 
-        core = lax.axis_index("col") % 2
         sums = total_ref[...]
-        for w, c in ((0, core), (1, 1 - core)):
+        for w, part in ((0, near_ref), (1, far_ref)):
             now = pieces[w * steps][...]
             for i in range(1, steps):
                 now = jnp.where(step == i, pieces[w * steps + i][...], now)
-            part = late_ref[pl.ds(pl.multiple_of(c * depth, depth), depth), :]
-            sums += jnp.dot(now, part, preferred_element_type=jnp.float32)
+            sums += jnp.dot(now, part[...], preferred_element_type=jnp.float32)
 
         @pl.when(step == 0)
         def _():
@@ -175,14 +191,14 @@
     return pl.pallas_call(
         body,
         grid=(steps,),
-        in_specs=[FAR, here, whole(late)] + [whole(v) for v in (*mine, *other)] + [HOME] * len(given),
+        in_specs=[FAR, here] + [whole(v) for v in (*parts, *mine, *other)] + [HOME] * len(given),
         out_specs=here,
         out_shape=jax.ShapeDtypeStruct((rows, cols), jnp.bfloat16),
         scratch_shapes=[pltpu.SMEM(keep_mask.shape, jnp.int32), COPIES(())],
-        input_output_aliases={3 + 2 * steps: 0} if given else {},
+        input_output_aliases={4 + 2 * steps: 0} if given else {},
         compiler_params=pltpu.CompilerParams(vmem_limit_bytes=10 * MIB),
         cost_estimate=SMALL,
-    )(keep_mask, total, late, *mine, *other, *given)
+    )(keep_mask, total, *parts, *mine, *other, *given)
 
 
 def on_grid(left, right, a_pattern, b_pattern, keep_mask):
@@ -219,14 +235,17 @@
     e3 = [cross(r3[0])]
     r3[1], e3[0], *e2 = tied(r3[1], e3[0], *e2)
     e3.append(cross(r3[1]))
-    total, late = early_slots((((a0, a1), ea), (r1, e1), (r2, e2)), ((b,), (bx,), (by,), bd))
-    r3[2], e3[1], total, late = tied(r3[2], e3[1], total, late)
-    e3.append(cross(r3[2]))
-    keep = keep_mask.T
+    keep, cut = keep_mask.T, half + quarter
+    total, rest, *late, kept = early_slots((((a0, a1), ea), (r1, e1), (r2, e2)), ((b,), (bx,), (by,), bd), keep, cut)
+    r3[2], e3[1], total, rest, kept, *late = tied(r3[2], e3[1], total, rest, kept, *late)
+    eighth = quarter // 2
+    e3 += [cross(r3[2][:eighth]), cross(r3[2][eighth:])]
     product = last_slot(0, keep, total, late, r3[:2], e3[:2])
-    r3[3], e3[2], product = tied(r3[3], e3[2], product)
-    product = last_slot(half, keep, total, late, r3[2:3], e3[2:3], product)
-    return last_slot(half + quarter, keep, total, late, r3[3:], [cross(r3[3])], product)
+    product = last_slot(half, keep, total, late, [r3[2][:eighth], r3[2][eighth:]], e3[2:], product)
+    r3[3], product = tied(r3[3], product)
+    rest += jnp.dot(r3[3], late[0], preferred_element_type=jnp.float32)
+    rest += jnp.dot(cross(r3[3]), late[1], preferred_element_type=jnp.float32)
+    return lax.dynamic_update_slice(product, (rest * kept).astype(jnp.bfloat16), (cut, 0))
 
 
 def on_any(left, right, a_pattern, b_pattern, keep_mask):

time: 77.5 us -> 77.2 us (level)
  waiting for transfers between devices: 41.1 us -> 39.9 us
  Pallas kernels: 13.5 us -> 12.3 us
  other arithmetic: 0 us -> 0.89 us
    ppermute x8, waiting for transfers between devices: 29.2 us -> 27 us  [on_grid(): on = lambda v: lax.ppermute(v, 'col', ring)]
    pallas_call x4 -> x3, Pallas kernels: 9.26 us -> 8.06 us  [the longest x1 4.57 us: early_slots(): pl.pallas_call(body, in_specs=specs + [FAR], out_specs=[NEAR] * 5, out_sh...]
    ppermute x10 -> x11, waiting for transfers between devices: 0.09 us -> 1.1 us  [on_grid(): cross = lambda v: lax.ppermute(v, 'col', [(i, i ^ 1) for i in range(8)])]
    dynamic_update_slice x0 -> x1, other arithmetic: none -> 0.89 us  [on_grid(): lax.dynamic_update_slice(product, (rest * kept).astype(jnp.bfloat16), (cu...]
  transfers between devices with their start and end apart: 22 -> 23, of which waited for: 12 -> 12; matrix products, arithmetic and copies ran while one was open for 0% -> 1% of each run, Pallas kernels for 13% -> 14%
where the time goes in v7:
time: 77.2 us; the launch traced here: 77 us
  waiting for transfers between devices  39.9 us (52%)
  starting transfers between devices  23 us (30%)
  Pallas kernels  12.3 us (16%)
  other arithmetic  0.89 us (1%)
    ppermute x8, waiting for transfers between devices, on_grid(): on = lambda v: lax.ppermute(v, 'col', ring)  27 us
    ppermute x8, starting transfers between devices, on_grid(): on = lambda v: lax.ppermute(v, 'col', ring)  16.4 us
    ppermute x2, waiting for transfers between devices, on_grid(): to_y = lambda v: lax.ppermute(v, 'row', [(i, i ^ 2) for i in range(4)])  7.45 us
    pallas_call x1, Pallas kernels, early_slots(): pl.pallas_call(body, in_specs=specs + [FAR], out_specs=[NEAR] * 5, out_sh...  4.57 us
    ppermute x2, waiting for transfers between devices, on_grid(): to_x = lambda v: lax.ppermute(v, 'row', [(i, i ^ 1) for i in range(4)])  4.36 us
    pallas_call x2, Pallas kernels, masked(): pl.pallas_call(body, in_specs=[FAR] * (2 * k), out_specs=[HOME] * n, out_...  4.23 us
    pallas_call x2, Pallas kernels, last_slot(): pl.pallas_call(body, grid=(steps,), in_specs=[FAR, here] + [whole(v) for...  3.49 us
    ppermute x2, starting transfers between devices, on_grid(): to_y = lambda v: lax.ppermute(v, 'row', [(i, i ^ 2) for i in range(4)])  3.1 us
  transfers between devices with their start and end apart: 23, of which 12 were waited for; matrix products, arithmetic and copies ran while one was open for 1% of the time, Pallas kernels for 14%

profile of v7, /device:TPU:0, one launch (start us, length us, event | category | flops | bytes accessed | tf_op | source)
XLA Modules:
  0.0 77.0 jit_solution(1342205171664109968)
XLA Ops:
  0.0 1.9 %shard_map.55.refs_5_ = bf16[512,512]{1,0:T(8,128)(2,1)} custom-call(bf16[1024,512]{1,0:T(8,128)(2,1)} %refs_0_.2, s32[4,8]{1,0:T(4,128)} %bitcast.10), custom_call_target="tpu_custom_call" | custom-call | flops 1 | bytes 1 | tf_op jit(solution)/shard_map/pallas_call | solution.py:60
  1.9 3.1 %collective-permute-start.1 = (bf16[512,512]{1,0:T(8,128)(2,1)}, bf16[512,512]{1,0:T(8,128)(2,1)S(1)}, u32[]{:S(2)}, u32[]{:S(2)}) collective-permute-start(bf16[512,512]{1,0:T(8,128)(2,1)} %shard_map.55.refs_5_), channel_id=1, source_target_pairs={{0,2},{1,3},{2,6},{3,7},{6,4},{7,5},{4,0},{5,1},{8,10},{9,11},{10,... | collective-permute-start | bytes 1572872 | tf_op jit(solution)/shard_map/ppermute | solution.py:206
  4.9 0.0 collective-permute-start.2
  4.9 2.4 %shard_map.56 = (bf16[512,512]{1,0:T(8,128)(2,1)}, bf16[1024,512]{1,0:T(8,128)(2,1)}) custom-call(bf16[1024,512]{1,0:T(8,128)(2,1)} %refs_0_.2, bf16[1024,512]{1,0:T(8,128)(2,1)} %refs_1_.1, s32[4,8]{1,0:T(4,128)} %bitcast.11, s32[4,8]{1,0:T(4,128)} %bitcast.12), custom_call_target="tpu_custom_call" | custom-call | flops 1 | bytes 1 | tf_op jit(solution)/shard_map/pallas_call | solution.py:60
  7.3 1.6 %collective-permute-start.4 = (bf16[1024,512]{1,0:T(8,128)(2,1)}, bf16[1024,512]{1,0:T(8,128)(2,1)S(1)}, u32[]{:S(2)}, u32[]{:S(2)}) collective-permute-start(bf16[1024,512]{1,0:T(8,128)(2,1)} %get-tuple-element.47.refs_0_), channel_id=1, source_target_pairs={{0,8},{8,0},{16,24},{24,16},{1,9},{9,1},{17,25},{25,17},{2,10},{10... | collective-permute-start | bytes 3145736 | tf_op jit(solution)/shard_map/ppermute | solution.py:208
  8.9 1.5 %collective-permute-start.5 = (bf16[1024,512]{1,0:T(8,128)(2,1)}, bf16[1024,512]{1,0:T(8,128)(2,1)S(1)}, u32[]{:S(2)}, u32[]{:S(2)}) collective-permute-start(bf16[1024,512]{1,0:T(8,128)(2,1)} %get-tuple-element.47.refs_0_), channel_id=1, source_target_pairs={{0,16},{8,24},{16,0},{24,8},{1,17},{9,25},{17,1},{25,9},{2,18},{10... | collective-permute-start | bytes 3145736 | tf_op jit(solution)/shard_map/ppermute | solution.py:209
  10.4 2.6 %collective-permute-start = (bf16[512,512]{1,0:T(8,128)(2,1)}, bf16[512,512]{1,0:T(8,128)(2,1)S(1)}, u32[]{:S(2)}, u32[]{:S(2)}) collective-permute-start(bf16[512,512]{1,0:T(8,128)(2,1)} %get-tuple-element.46.refs_6_), channel_id=1, source_target_pairs={{0,2},{1,3},{2,6},{3,7},{6,4},{7,5},{4,0},{5,1},{8,10},{9,11},{10,... | collective-permute-start | bytes 1572872 | tf_op jit(solution)/shard_map/ppermute | solution.py:206
  13.0 5.9 %collective-permute-done.1.refs_9_ = bf16[512,512]{1,0:T(8,128)(2,1)S(1)} collective-permute-done((bf16[512,512]{1,0:T(8,128)(2,1)}, bf16[512,512]{1,0:T(8,128)(2,1)S(1)}, u32[]{:S(2)}, u32[]{:S(2)}) %collective-permute-start.1) | collective-permute-done | bytes 524320 | tf_op jit(solution)/shard_map/ppermute | solution.py:206
  18.9 0.0 collective-permute-done.2.refs_7_
  18.9 0.0 collective-permute-start.3
  18.9 1.3 %collective-permute-start.7 = (bf16[512,512]{1,0:T(8,128)(2,1)S(1)}, bf16[512,512]{1,0:T(8,128)(2,1)S(1)}, u32[]{:S(2)}, u32[]{:S(2)}) collective-permute-start(bf16[512,512]{1,0:T(8,128)(2,1)S(1)} %collective-permute-done.1.refs_9_), channel_id=1, source_target_pairs={{0,2},{1,3},{2,6},{3,7},{6,4},{7,5},{4,0},{5,1},{8,10},{9,11},{10,... | collective-permute-start | bytes 1572872 | tf_op jit(solution)/shard_map/ppermute | solution.py:206
  20.2 10.0 %collective-permute-done.refs_10_ = bf16[512,512]{1,0:T(8,128)(2,1)S(1)} collective-permute-done((bf16[512,512]{1,0:T(8,128)(2,1)}, bf16[512,512]{1,0:T(8,128)(2,1)S(1)}, u32[]{:S(2)}, u32[]{:S(2)}) %collective-permute-start) | collective-permute-done | bytes 524320 | tf_op jit(solution)/shard_map/ppermute | solution.py:206
  30.1 0.0 collective-permute-done.3.refs_8_
  30.2 3.0 %collective-permute-done.4.refs_1_ = bf16[1024,512]{1,0:T(8,128)(2,1)S(1)} collective-permute-done((bf16[1024,512]{1,0:T(8,128)(2,1)}, bf16[1024,512]{1,0:T(8,128)(2,1)S(1)}, u32[]{:S(2)}, u32[]{:S(2)}) %collective-permute-start.4) | collective-permute-done | bytes 1048608 | tf_op jit(solution)/shard_map/ppermute | solution.py:208
  33.2 1.2 %collective-permute-done.5.refs_2_ = bf16[1024,512]{1,0:T(8,128)(2,1)S(1)} collective-permute-done((bf16[1024,512]{1,0:T(8,128)(2,1)}, bf16[1024,512]{1,0:T(8,128)(2,1)S(1)}, u32[]{:S(2)}, u32[]{:S(2)}) %collective-permute-start.5) | collective-permute-done | bytes 1048608 | tf_op jit(solution)/shard_map/ppermute | solution.py:209
  34.4 0.0 collective-permute-start.8
  34.4 0.0 copy-start
  34.4 0.0 copy-start.1
  34.5 0.0 copy-start.2
  34.5 0.0 copy-start.3
  34.5 1.6 %collective-permute-start.10 = (bf16[512,512]{1,0:T(8,128)(2,1)S(1)}, bf16[512,512]{1,0:T(8,128)(2,1)S(1)}, u32[]{:S(2)}, u32[]{:S(2)}) collective-permute-start(bf16[512,512]{1,0:T(8,128)(2,1)S(1)} %slice.26), channel_id=1, source_target_pairs={{0,16},{8,24},{16,0},{24,8},{1,17},{9,25},{17,1},{25,9},{2,18},{10... | collective-permute-start | bytes 1572872 | tf_op jit(solution)/shard_map/ppermute | solution.py:209
  36.1 0.6 collective-permute-start.11
  36.7 2.6 %collective-permute-start.6 = (bf16[512,512]{1,0:T(8,128)(2,1)S(1)}, bf16[512,512]{1,0:T(8,128)(2,1)S(1)}, u32[]{:S(2)}, u32[]{:S(2)}) collective-permute-start(bf16[512,512]{1,0:T(8,128)(2,1)S(1)} %collective-permute-done.refs_10_), channel_id=1, source_target_pairs={{0,2},{1,3},{2,6},{3,7},{6,4},{7,5},{4,0},{5,1},{8,10},{9,11},{10,... | collective-permute-start | bytes 1572872 | tf_op jit(solution)/shard_map/ppermute | solution.py:206
  39.3 1.6 %collective-permute-done.7.refs_13_ = bf16[512,512]{1,0:T(8,128)(2,1)S(1)} collective-permute-done((bf16[512,512]{1,0:T(8,128)(2,1)S(1)}, bf16[512,512]{1,0:T(8,128)(2,1)S(1)}, u32[]{:S(2)}, u32[]{:S(2)}) %collective-permute-start.7) | collective-permute-done | bytes 524320 | tf_op jit(solution)/shard_map/ppermute | solution.py:206
  40.9 0.0 collective-permute-done.8.refs_11_
  40.9 0.0 collective-permute-start.9
  41.0 1.7 %collective-permute-start.15 = (bf16[256,512]{1,0:T(8,128)(2,1)S(1)}, bf16[256,512]{1,0:T(8,128)(2,1)S(1)}, u32[]{:S(2)}, u32[]{:S(2)}) collective-permute-start(bf16[256,512]{1,0:T(8,128)(2,1)S(1)} %get-tuple-element.81), channel_id=1, source_target_pairs={{0,2},{1,3},{2,6},{3,7},{6,4},{7,5},{4,0},{5,1},{8,10},{9,11},{10,... | collective-permute-start | bytes 786440 | tf_op jit(solution)/shard_map/ppermute | solution.py:206
  42.6 6.2 %collective-permute-done.10.refs_3_ = bf16[512,512]{1,0:T(8,128)(2,1)S(1)} collective-permute-done((bf16[512,512]{1,0:T(8,128)(2,1)S(1)}, bf16[512,512]{1,0:T(8,128)(2,1)S(1)}, u32[]{:S(2)}, u32[]{:S(2)}) %collective-permute-start.10) | collective-permute-done | bytes 524320 | tf_op jit(solution)/shard_map/ppermute | solution.py:209
  48.9 1.3 %collective-permute-done.11.refs_4_ = bf16[512,512]{1,0:T(8,128)(2,1)S(1)} collective-permute-done((bf16[512,512]{1,0:T(8,128)(2,1)S(1)}, bf16[512,512]{1,0:T(8,128)(2,1)S(1)}, u32[]{:S(2)}, u32[]{:S(2)}) %collective-permute-start.11) | collective-permute-done | bytes 524320 | tf_op jit(solution)/shard_map/ppermute | solution.py:208
  50.2 2.2 %collective-permute-done.6.refs_14_ = bf16[512,512]{1,0:T(8,128)(2,1)S(1)} collective-permute-done((bf16[512,512]{1,0:T(8,128)(2,1)S(1)}, bf16[512,512]{1,0:T(8,128)(2,1)S(1)}, u32[]{:S(2)}, u32[]{:S(2)}) %collective-permute-start.6) | collective-permute-done | bytes 524320 | tf_op jit(solution)/shard_map/ppermute | solution.py:206
  52.4 0.0 collective-permute-done.9.refs_12_
  52.4 0.0 collective-permute-start.17
  52.4 0.5 collective-permute-start.18
  52.9 1.7 %collective-permute-start.14 = (bf16[256,512]{1,0:T(8,128)(2,1)S(1)}, bf16[256,512]{1,0:T(8,128)(2,1)S(1)}, u32[]{:S(2)}, u32[]{:S(2)}) collective-permute-start(bf16[256,512]{1,0:T(8,128)(2,1)S(1)} %get-tuple-element.82), channel_id=1, source_target_pairs={{0,2},{1,3},{2,6},{3,7},{6,4},{7,5},{4,0},{5,1},{8,10},{9,11},{10,... | collective-permute-start | bytes 786440 | tf_op jit(solution)/shard_map/ppermute | solution.py:206
  54.6 3.4 %collective-permute-done.15.refs_0_ = bf16[256,512]{1,0:T(8,128)(2,1)S(1)} collective-permute-done((bf16[256,512]{1,0:T(8,128)(2,1)S(1)}, bf16[256,512]{1,0:T(8,128)(2,1)S(1)}, u32[]{:S(2)}, u32[]{:S(2)}) %collective-permute-start.15) | collective-permute-done | bytes 262176 | tf_op jit(solution)/shard_map/ppermute | solution.py:206
  58.0 0.0 collective-permute-start.16
  58.0 1.7 %collective-permute-start.13 = (bf16[256,512]{1,0:T(8,128)(2,1)S(1)}, bf16[256,512]{1,0:T(8,128)(2,1)S(1)}, u32[]{:S(2)}, u32[]{:S(2)}) collective-permute-start(bf16[256,512]{1,0:T(8,128)(2,1)S(1)} %get-tuple-element.83), channel_id=1, source_target_pairs={{0,2},{1,3},{2,6},{3,7},{6,4},{7,5},{4,0},{5,1},{8,10},{9,11},{10,... | collective-permute-start | bytes 786440 | tf_op jit(solution)/shard_map/ppermute | solution.py:206
  59.8 3.8 %collective-permute-done.14.refs_1_ = bf16[256,512]{1,0:T(8,128)(2,1)S(1)} collective-permute-done((bf16[256,512]{1,0:T(8,128)(2,1)S(1)}, bf16[256,512]{1,0:T(8,128)(2,1)S(1)}, u32[]{:S(2)}, u32[]{:S(2)}) %collective-permute-start.14) | collective-permute-done | bytes 262176 | tf_op jit(solution)/shard_map/ppermute | solution.py:206
  63.6 0.0 collective-permute-done.16.refs_2_
  63.6 0.0 collective-permute-done.17.refs_15_
  63.6 0.0 collective-permute-done.18.refs_16_
  63.6 0.1 collective-permute-start.19
  63.7 1.7 %collective-permute-start.12 = (bf16[256,512]{1,0:T(8,128)(2,1)S(1)}, bf16[256,512]{1,0:T(8,128)(2,1)S(1)}, u32[]{:S(2)}, u32[]{:S(2)}) collective-permute-start(bf16[256,512]{1,0:T(8,128)(2,1)S(1)} %get-tuple-element.84), channel_id=1, source_target_pairs={{0,2},{1,3},{2,6},{3,7},{6,4},{7,5},{4,0},{5,1},{8,10},{9,11},{10,... | collective-permute-start | bytes 786440 | tf_op jit(solution)/shard_map/ppermute | solution.py:206
  65.5 0.0 copy-done
  65.5 0.0 copy-done.1
  65.5 0.0 copy-done.2
  65.5 0.0 copy-done.3
  65.5 4.6 %shard_map.57 = (f32[768,512]{1,0:T(8,128)S(1)}, f32[256,512]{1,0:T(8,128)S(1)}, bf16[512,512]{1,0:T(8,128)(2,1)S(1)}, bf16[512,512]{1,0:T(8,128)(2,1)S(1)}, f32[256,512]{1,0:T(8,128)S(1)}) custom-call(bf16[1024,512]{1,0:T(8,128)(2,1)S(1)} %copy-done.1, bf16[1024,512]{1,0:T(8,128)(2,1)S(1)} %collective-permute-done.4.refs_1_, ...), custom_call_target="tpu_custom_call" | custom-call | flops 1 | bytes 1 | tf_op jit(solution)/shard_map/pallas_call | solution.py:136
  70.1 0.0 collective-permute-done.13
  70.1 0.0 collective-permute-done.19.refs_3_
  70.1 0.2 collective-permute-start.20
  70.3 0.3 collective-permute-start.21
  70.7 1.8 %shard_map.58.refs_4_ = bf16[1024,512]{1,0:T(8,128)(2,1)} custom-call(s32[4,8]{1,0:T(4,128)S(1)} %bitcast.8, f32[768,512]{1,0:T(8,128)S(1)} %get-tuple-element.71.total_ref, bf16[512,512]{1,0:T(8,128)(2,1)S(1)} %get-tuple-element.72.near_ref, bf16[512,512]{1,0:T(8,128)(2,1)S(1)} %get-tuple-element.73.far_ref, ...), custom_call_target="tpu_custom_call" | custom-call | flops 1 | bytes 1 | tf_op jit(solution)/shard_map/pallas_call | solution.py:191
  72.5 0.0 collective-permute-done.20.refs_2_
  72.5 0.0 collective-permute-done.21.refs_3_
  72.5 1.7 %shard_map.59 = bf16[1024,512]{1,0:T(8,128)(2,1)} custom-call(s32[4,8]{1,0:T(4,128)S(1)} %bitcast.9, f32[768,512]{1,0:T(8,128)S(1)} %get-tuple-element.71.total_ref, bf16[512,512]{1,0:T(8,128)(2,1)S(1)} %get-tuple-element.72.near_ref, bf16[512,512]{1,0:T(8,128)(2,1)S(1)} %get-tuple-element.73.far_ref, ...), custom_call_target="tpu_custom_call", output_to_operand_aliasing={{}: (8, {})} | custom-call | flops 1 | bytes 1 | tf_op jit(solution)/shard_map/pallas_call | solution.py:191
  74.2 0.1 collective-permute-done.12
  74.3 0.2 collective-permute-start.22
  74.4 0.3 fusion.4
  74.7 1.1 %collective-permute-done.22 = bf16[256,512]{1,0:T(8,128)(2,1)S(1)} collective-permute-done((bf16[256,512]{1,0:T(8,128)(2,1)S(1)}, bf16[256,512]{1,0:T(8,128)(2,1)S(1)}, u32[]{:S(2)}, u32[]{:S(2)}) %collective-permute-start.22) | collective-permute-done | bytes 262176 | tf_op jit(solution)/shard_map/ppermute | solution.py:207
  75.8 0.3 fusion.5
  76.1 0.9 %fusion = bf16[1024,512]{1,0:T(8,128)(2,1)} fusion(bf16[1024,512]{1,0:T(8,128)(2,1)} %shard_map.59, f32[256,512]{1,0:T(8,128)S(1)} %get-tuple-element.80, f32[256,512]{1,0:T(8,128)S(1)} %fusion.5, f32[256,512]{1,0:T(8,128)S(1)} %get-tuple-element.78, f32[256,512]{1,0:T(8,128)S(1)} %fusion.4), kind=kLoop, calls=%fused_computation.1 | loop fusion | flops 524288 | bytes 2359296 | tf_op jit(solution)/shard_map/dynamic_update_slice | solution.py:248
  (5 shorter events, 0.2 us)
Async XLA Ops:
  1.9 17.1 %collective-permute-start.1 = (bf16[512,512]{1,0:T(8,128)(2,1)}, bf16[512,512]{1,0:T(8,128)(2,1)S(1)}, u32[]{:S(2)}, u32[]{:S(2)}) collective-permute-start(bf16[512,512]{1,0:T(8,128)(2,1)} %shard_map.55.refs_5_), channel_id=1, source_target_pairs={{0,2},{1,3},{2,6},{3,7},{6,4},{7,5},{4,0},{5,1},{8,10},{9,11},{10,... | collective-permute-start | bytes 1572872 | tf_op jit(solution)/shard_map/ppermute | solution.py:206
  4.9 14.0 %collective-permute-start.2 = (bf16[512,512]{1,0:T(8,128)(2,1)}, bf16[512,512]{1,0:T(8,128)(2,1)S(1)}, u32[]{:S(2)}, u32[]{:S(2)}) collective-permute-start(bf16[512,512]{1,0:T(8,128)(2,1)} %shard_map.55.refs_5_), channel_id=1, source_target_pairs={{0,1},{1,0},{2,3},{3,2},{4,5},{5,4},{6,7},{7,6},{8,9},{9,8},{10,11... | collective-permute-start | bytes 1572872 | tf_op jit(solution)/shard_map/ppermute | solution.py:207
  7.3 25.8 %collective-permute-start.4 = (bf16[1024,512]{1,0:T(8,128)(2,1)}, bf16[1024,512]{1,0:T(8,128)(2,1)S(1)}, u32[]{:S(2)}, u32[]{:S(2)}) collective-permute-start(bf16[1024,512]{1,0:T(8,128)(2,1)} %get-tuple-element.47.refs_0_), channel_id=1, source_target_pairs={{0,8},{8,0},{16,24},{24,16},{1,9},{9,1},{17,25},{25,17},{2,10},{10... | collective-permute-start | bytes 3145736 | tf_op jit(solution)/shard_map/ppermute | solution.py:208
  8.9 25.5 %collective-permute-start.5 = (bf16[1024,512]{1,0:T(8,128)(2,1)}, bf16[1024,512]{1,0:T(8,128)(2,1)S(1)}, u32[]{:S(2)}, u32[]{:S(2)}) collective-permute-start(bf16[1024,512]{1,0:T(8,128)(2,1)} %get-tuple-element.47.refs_0_), channel_id=1, source_target_pairs={{0,16},{8,24},{16,0},{24,8},{1,17},{9,25},{17,1},{25,9},{2,18},{10... | collective-permute-start | bytes 3145736 | tf_op jit(solution)/shard_map/ppermute | solution.py:209
  10.4 19.7 %collective-permute-start = (bf16[512,512]{1,0:T(8,128)(2,1)}, bf16[512,512]{1,0:T(8,128)(2,1)S(1)}, u32[]{:S(2)}, u32[]{:S(2)}) collective-permute-start(bf16[512,512]{1,0:T(8,128)(2,1)} %get-tuple-element.46.refs_6_), channel_id=1, source_target_pairs={{0,2},{1,3},{2,6},{3,7},{6,4},{7,5},{4,0},{5,1},{8,10},{9,11},{10,... | collective-permute-start | bytes 1572872 | tf_op jit(solution)/shard_map/ppermute | solution.py:206
  18.9 11.2 %collective-permute-start.3 = (bf16[512,512]{1,0:T(8,128)(2,1)}, bf16[512,512]{1,0:T(8,128)(2,1)S(1)}, u32[]{:S(2)}, u32[]{:S(2)}) collective-permute-start(bf16[512,512]{1,0:T(8,128)(2,1)} %get-tuple-element.46.refs_6_), channel_id=1, source_target_pairs={{0,1},{1,0},{2,3},{3,2},{4,5},{5,4},{6,7},{7,6},{8,9},{9,8},{10,11... | collective-permute-start | bytes 1572872 | tf_op jit(solution)/shard_map/ppermute | solution.py:207
  18.9 22.0 %collective-permute-start.7 = (bf16[512,512]{1,0:T(8,128)(2,1)S(1)}, bf16[512,512]{1,0:T(8,128)(2,1)S(1)}, u32[]{:S(2)}, u32[]{:S(2)}) collective-permute-start(bf16[512,512]{1,0:T(8,128)(2,1)S(1)} %collective-permute-done.1.refs_9_), channel_id=1, source_target_pairs={{0,2},{1,3},{2,6},{3,7},{6,4},{7,5},{4,0},{5,1},{8,10},{9,11},{10,... | collective-permute-start | bytes 1572872 | tf_op jit(solution)/shard_map/ppermute | solution.py:206
  34.4 6.5 %collective-permute-start.8 = (bf16[512,512]{1,0:T(8,128)(2,1)S(1)}, bf16[512,512]{1,0:T(8,128)(2,1)S(1)}, u32[]{:S(2)}, u32[]{:S(2)}) collective-permute-start(bf16[512,512]{1,0:T(8,128)(2,1)S(1)} %collective-permute-done.1.refs_9_), channel_id=1, source_target_pairs={{0,1},{1,0},{2,3},{3,2},{4,5},{5,4},{6,7},{7,6},{8,9},{9,8},{10,11... | collective-permute-start | bytes 1572872 | tf_op jit(solution)/shard_map/ppermute | solution.py:207
  34.4 31.0 %copy-start = (bf16[512,512]{1,0:T(8,128)(2,1)S(1)}, bf16[512,512]{1,0:T(8,128)(2,1)}, u32[]{:S(2)}) copy-start(bf16[512,512]{1,0:T(8,128)(2,1)} %shard_map.55.refs_5_) | copy-start | bytes 1572868
  34.4 31.0 %copy-start.1 = (bf16[1024,512]{1,0:T(8,128)(2,1)S(1)}, bf16[1024,512]{1,0:T(8,128)(2,1)}, u32[]{:S(2)}) copy-start(bf16[1024,512]{1,0:T(8,128)(2,1)} %get-tuple-element.47.refs_0_) | copy-start | bytes 3145732
  34.5 31.0 %copy-start.2 = (bf16[512,512]{1,0:T(8,128)(2,1)S(1)}, bf16[512,512]{1,0:T(8,128)(2,1)}, u32[]{:S(2)}) copy-start(bf16[512,512]{1,0:T(8,128)(2,1)} %get-tuple-element.46.refs_6_) | copy-start | bytes 1572868
  34.5 31.0 %copy-start.3 = (s32[8,4]{0,1:T(4,128)S(1)}, s32[8,4]{0,1:T(4,128)}, u32[]{:S(2)}) copy-start(s32[8,4]{0,1:T(4,128)} %param.9) | copy-start | bytes 388
  34.5 14.4 %collective-permute-start.10 = (bf16[512,512]{1,0:T(8,128)(2,1)S(1)}, bf16[512,512]{1,0:T(8,128)(2,1)S(1)}, u32[]{:S(2)}, u32[]{:S(2)}) collective-permute-start(bf16[512,512]{1,0:T(8,128)(2,1)S(1)} %slice.26), channel_id=1, source_target_pairs={{0,16},{8,24},{16,0},{24,8},{1,17},{9,25},{17,1},{25,9},{2,18},{10... | collective-permute-start | bytes 1572872 | tf_op jit(solution)/shard_map/ppermute | solution.py:209
  36.1 14.1 %collective-permute-start.11 = (bf16[512,512]{1,0:T(8,128)(2,1)S(1)}, bf16[512,512]{1,0:T(8,128)(2,1)S(1)}, u32[]{:S(2)}, u32[]{:S(2)}) collective-permute-start(bf16[512,512]{1,0:T(8,128)(2,1)S(1)} %slice.27), channel_id=1, source_target_pairs={{0,8},{8,0},{16,24},{24,16},{1,9},{9,1},{17,25},{25,17},{2,10},{10... | collective-permute-start | bytes 1572872 | tf_op jit(solution)/shard_map/ppermute | solution.py:208
  36.7 15.7 %collective-permute-start.6 = (bf16[512,512]{1,0:T(8,128)(2,1)S(1)}, bf16[512,512]{1,0:T(8,128)(2,1)S(1)}, u32[]{:S(2)}, u32[]{:S(2)}) collective-permute-start(bf16[512,512]{1,0:T(8,128)(2,1)S(1)} %collective-permute-done.refs_10_), channel_id=1, source_target_pairs={{0,2},{1,3},{2,6},{3,7},{6,4},{7,5},{4,0},{5,1},{8,10},{9,11},{10,... | collective-permute-start | bytes 1572872 | tf_op jit(solution)/shard_map/ppermute | solution.py:206
  40.9 11.5 %collective-permute-start.9 = (bf16[512,512]{1,0:T(8,128)(2,1)S(1)}, bf16[512,512]{1,0:T(8,128)(2,1)S(1)}, u32[]{:S(2)}, u32[]{:S(2)}) collective-permute-start(bf16[512,512]{1,0:T(8,128)(2,1)S(1)} %collective-permute-done.refs_10_), channel_id=1, source_target_pairs={{0,1},{1,0},{2,3},{3,2},{4,5},{5,4},{6,7},{7,6},{8,9},{9,8},{10,11... | collective-permute-start | bytes 1572872 | tf_op jit(solution)/shard_map/ppermute | solution.py:207
  41.0 17.1 %collective-permute-start.15 = (bf16[256,512]{1,0:T(8,128)(2,1)S(1)}, bf16[256,512]{1,0:T(8,128)(2,1)S(1)}, u32[]{:S(2)}, u32[]{:S(2)}) collective-permute-start(bf16[256,512]{1,0:T(8,128)(2,1)S(1)} %get-tuple-element.81), channel_id=1, source_target_pairs={{0,2},{1,3},{2,6},{3,7},{6,4},{7,5},{4,0},{5,1},{8,10},{9,11},{10,... | collective-permute-start | bytes 786440 | tf_op jit(solution)/shard_map/ppermute | solution.py:206
  52.4 11.2 %collective-permute-start.17 = (bf16[512,512]{1,0:T(8,128)(2,1)S(1)}, bf16[512,512]{1,0:T(8,128)(2,1)S(1)}, u32[]{:S(2)}, u32[]{:S(2)}) collective-permute-start(bf16[512,512]{1,0:T(8,128)(2,1)S(1)} %collective-permute-done.7.refs_13_), channel_id=1, source_target_pairs={{0,1},{1,0},{2,3},{3,2},{4,5},{5,4},{6,7},{7,6},{8,9},{9,8},{10,11... | collective-permute-start | bytes 1572872 | tf_op jit(solution)/shard_map/ppermute | solution.py:207
  52.4 11.2 %collective-permute-start.18 = (bf16[512,512]{1,0:T(8,128)(2,1)S(1)}, bf16[512,512]{1,0:T(8,128)(2,1)S(1)}, u32[]{:S(2)}, u32[]{:S(2)}) collective-permute-start(bf16[512,512]{1,0:T(8,128)(2,1)S(1)} %collective-permute-done.6.refs_14_), channel_id=1, source_target_pairs={{0,1},{1,0},{2,3},{3,2},{4,5},{5,4},{6,7},{7,6},{8,9},{9,8},{10,11... | collective-permute-start | bytes 1572872 | tf_op jit(solution)/shard_map/ppermute | solution.py:207
  52.9 10.7 %collective-permute-start.14 = (bf16[256,512]{1,0:T(8,128)(2,1)S(1)}, bf16[256,512]{1,0:T(8,128)(2,1)S(1)}, u32[]{:S(2)}, u32[]{:S(2)}) collective-permute-start(bf16[256,512]{1,0:T(8,128)(2,1)S(1)} %get-tuple-element.82), channel_id=1, source_target_pairs={{0,2},{1,3},{2,6},{3,7},{6,4},{7,5},{4,0},{5,1},{8,10},{9,11},{10,... | collective-permute-start | bytes 786440 | tf_op jit(solution)/shard_map/ppermute | solution.py:206
  58.0 5.6 %collective-permute-start.16 = (bf16[256,512]{1,0:T(8,128)(2,1)S(1)}, bf16[256,512]{1,0:T(8,128)(2,1)S(1)}, u32[]{:S(2)}, u32[]{:S(2)}) collective-permute-start(bf16[256,512]{1,0:T(8,128)(2,1)S(1)} %collective-permute-done.15.refs_0_), channel_id=1, source_target_pairs={{0,1},{1,0},{2,3},{3,2},{4,5},{5,4},{6,7},{7,6},{8,9},{9,8},{10,11... | collective-permute-start | bytes 786440 | tf_op jit(solution)/shard_map/ppermute | solution.py:207
  58.0 12.0 %collective-permute-start.13 = (bf16[256,512]{1,0:T(8,128)(2,1)S(1)}, bf16[256,512]{1,0:T(8,128)(2,1)S(1)}, u32[]{:S(2)}, u32[]{:S(2)}) collective-permute-start(bf16[256,512]{1,0:T(8,128)(2,1)S(1)} %get-tuple-element.83), channel_id=1, source_target_pairs={{0,2},{1,3},{2,6},{3,7},{6,4},{7,5},{4,0},{5,1},{8,10},{9,11},{10,... | collective-permute-start | bytes 786440 | tf_op jit(solution)/shard_map/ppermute | solution.py:206
  63.6 6.4 %collective-permute-start.19 = (bf16[256,512]{1,0:T(8,128)(2,1)S(1)}, bf16[256,512]{1,0:T(8,128)(2,1)S(1)}, u32[]{:S(2)}, u32[]{:S(2)}) collective-permute-start(bf16[256,512]{1,0:T(8,128)(2,1)S(1)} %collective-permute-done.14.refs_1_), channel_id=1, source_target_pairs={{0,1},{1,0},{2,3},{3,2},{4,5},{5,4},{6,7},{7,6},{8,9},{9,8},{10,11... | collective-permute-start | bytes 786440 | tf_op jit(solution)/shard_map/ppermute | solution.py:207
  63.7 10.5 %collective-permute-start.12 = (bf16[256,512]{1,0:T(8,128)(2,1)S(1)}, bf16[256,512]{1,0:T(8,128)(2,1)S(1)}, u32[]{:S(2)}, u32[]{:S(2)}) collective-permute-start(bf16[256,512]{1,0:T(8,128)(2,1)S(1)} %get-tuple-element.84), channel_id=1, source_target_pairs={{0,2},{1,3},{2,6},{3,7},{6,4},{7,5},{4,0},{5,1},{8,10},{9,11},{10,... | collective-permute-start | bytes 786440 | tf_op jit(solution)/shard_map/ppermute | solution.py:206
  70.1 2.4 %collective-permute-start.20 = (bf16[128,512]{1,0:T(8,128)(2,1)S(1)}, bf16[128,512]{1,0:T(8,128)(2,1)S(1)}, u32[]{:S(2)}, u32[]{:S(2)}) collective-permute-start(bf16[128,512]{1,0:T(8,128)(2,1)S(1)} %get-tuple-element.86.refs_0_), channel_id=1, source_target_pairs={{0,1},{1,0},{2,3},{3,2},{4,5},{5,4},{6,7},{7,6},{8,9},{9,8},{10,11... | collective-permute-start | bytes 393224 | tf_op jit(solution)/shard_map/ppermute | solution.py:207
  70.3 2.2 %collective-permute-start.21 = (bf16[128,512]{1,0:T(8,128)(2,1)S(1)}, bf16[128,512]{1,0:T(8,128)(2,1)S(1)}, u32[]{:S(2)}, u32[]{:S(2)}) collective-permute-start(bf16[128,512]{1,0:T(8,128)(2,1)S(1)} %get-tuple-element.85.refs_1_), channel_id=1, source_target_pairs={{0,1},{1,0},{2,3},{3,2},{4,5},{5,4},{6,7},{7,6},{8,9},{9,8},{10,11... | collective-permute-start | bytes 393224 | tf_op jit(solution)/shard_map/ppermute | solution.py:207
  74.3 1.6 %collective-permute-start.22 = (bf16[256,512]{1,0:T(8,128)(2,1)S(1)}, bf16[256,512]{1,0:T(8,128)(2,1)S(1)}, u32[]{:S(2)}, u32[]{:S(2)}) collective-permute-start(bf16[256,512]{1,0:T(8,128)(2,1)S(1)} %collective-permute-done.12), channel_id=1, source_target_pairs={{0,1},{1,0},{2,3},{3,2},{4,5},{5,4},{6,7},{7,6},{8,9},{9,8},{10,11... | collective-permute-start | bytes 786440 | tf_op jit(solution)/shard_map/ppermute | solution.py:207

commit v8 on v7

--- a/solution.py
+++ b/solution.py
@@ -131,7 +131,7 @@
         size = rows // keep_mask.shape[1]
         for p, q, at in cells((rows - cut) // size, cols // size, size):
             kept = keep_ref[q, cut // size + p].astype(jnp.float32)
-            kept_ref[at] = jnp.full((size, size), kept, jnp.float32)
+            kept_ref[at] = jnp.full((size, size), kept, jnp.float32).astype(dtype)
 
     return pl.pallas_call(
         body,
@@ -142,7 +142,7 @@
             jax.ShapeDtypeStruct((rows - cut, cols), jnp.float32),
             jax.ShapeDtypeStruct((depth, cols), dtype),
             jax.ShapeDtypeStruct((depth, cols), dtype),
-            jax.ShapeDtypeStruct((rows - cut, cols), jnp.float32),
+            jax.ShapeDtypeStruct((rows - cut, cols), dtype),
         ],
         scratch_shapes=[
             pltpu.VMEM((len(slots), 2, rows, depth), dtype),
@@ -245,7 +245,7 @@
     r3[3], product = tied(r3[3], product)
     rest += jnp.dot(r3[3], late[0], preferred_element_type=jnp.float32)
     rest += jnp.dot(cross(r3[3]), late[1], preferred_element_type=jnp.float32)
-    return lax.dynamic_update_slice(product, (rest * kept).astype(jnp.bfloat16), (cut, 0))
+    return lax.dynamic_update_slice(product, rest.astype(jnp.bfloat16) * kept, (cut, 0))
 
 
 def on_any(left, right, a_pattern, b_pattern, keep_mask):

time: 77.2 us -> 77.2 us (level)
  no operation moved by 1% of the time
where the time goes in v8:
time: 77.2 us; the launch traced here: 77 us
  waiting for transfers between devices  39.9 us (52%)
  starting transfers between devices  23 us (30%)
  Pallas kernels  12.3 us (16%)
  other arithmetic  0.9 us (1%)
    ppermute x8, waiting for transfers between devices, on_grid(): on = lambda v: lax.ppermute(v, 'col', ring)  27 us
    ppermute x8, starting transfers between devices, on_grid(): on = lambda v: lax.ppermute(v, 'col', ring)  16.4 us
    ppermute x2, waiting for transfers between devices, on_grid(): to_y = lambda v: lax.ppermute(v, 'row', [(i, i ^ 2) for i in range(4)])  7.45 us
    pallas_call x1, Pallas kernels, early_slots(): pl.pallas_call(body, in_specs=specs + [FAR], out_specs=[NEAR] * 5, out_sh...  4.55 us
    ppermute x2, waiting for transfers between devices, on_grid(): to_x = lambda v: lax.ppermute(v, 'row', [(i, i ^ 1) for i in range(4)])  4.36 us
    pallas_call x2, Pallas kernels, masked(): pl.pallas_call(body, in_specs=[FAR] * (2 * k), out_specs=[HOME] * n, out_...  4.23 us
    pallas_call x2, Pallas kernels, last_slot(): pl.pallas_call(body, grid=(steps,), in_specs=[FAR, here] + [whole(v) for...  3.49 us
    ppermute x2, starting transfers between devices, on_grid(): to_y = lambda v: lax.ppermute(v, 'row', [(i, i ^ 2) for i in range(4)])  3.1 us
  transfers between devices with their start and end apart: 23, of which 12 were waited for; matrix products, arithmetic and copies ran while one was open for 1% of the time, Pallas kernels for 14%

profile of v8, /device:TPU:0, one launch (start us, length us, event | category | flops | bytes accessed | tf_op | source)
XLA Modules:
  0.0 77.0 jit_solution(15578480414538117778)
XLA Ops:
  0.0 1.9 %shard_map.55.refs_5_ = bf16[512,512]{1,0:T(8,128)(2,1)} custom-call(bf16[1024,512]{1,0:T(8,128)(2,1)} %refs_0_.2, s32[4,8]{1,0:T(4,128)} %bitcast.10), custom_call_target="tpu_custom_call" | custom-call | flops 1 | bytes 1 | tf_op jit(solution)/shard_map/pallas_call | solution.py:60
  1.9 3.1 %collective-permute-start.1 = (bf16[512,512]{1,0:T(8,128)(2,1)}, bf16[512,512]{1,0:T(8,128)(2,1)S(1)}, u32[]{:S(2)}, u32[]{:S(2)}) collective-permute-start(bf16[512,512]{1,0:T(8,128)(2,1)} %shard_map.55.refs_5_), channel_id=1, source_target_pairs={{0,2},{1,3},{2,6},{3,7},{6,4},{7,5},{4,0},{5,1},{8,10},{9,11},{10,... | collective-permute-start | bytes 1572872 | tf_op jit(solution)/shard_map/ppermute | solution.py:206
  4.9 0.0 collective-permute-start.2
  4.9 2.4 %shard_map.56 = (bf16[512,512]{1,0:T(8,128)(2,1)}, bf16[1024,512]{1,0:T(8,128)(2,1)}) custom-call(bf16[1024,512]{1,0:T(8,128)(2,1)} %refs_0_.2, bf16[1024,512]{1,0:T(8,128)(2,1)} %refs_1_.1, s32[4,8]{1,0:T(4,128)} %bitcast.11, s32[4,8]{1,0:T(4,128)} %bitcast.12), custom_call_target="tpu_custom_call" | custom-call | flops 1 | bytes 1 | tf_op jit(solution)/shard_map/pallas_call | solution.py:60
  7.3 1.6 %collective-permute-start.4 = (bf16[1024,512]{1,0:T(8,128)(2,1)}, bf16[1024,512]{1,0:T(8,128)(2,1)S(1)}, u32[]{:S(2)}, u32[]{:S(2)}) collective-permute-start(bf16[1024,512]{1,0:T(8,128)(2,1)} %get-tuple-element.47.refs_0_), channel_id=1, source_target_pairs={{0,8},{8,0},{16,24},{24,16},{1,9},{9,1},{17,25},{25,17},{2,10},{10... | collective-permute-start | bytes 3145736 | tf_op jit(solution)/shard_map/ppermute | solution.py:208
  8.9 1.5 %collective-permute-start.5 = (bf16[1024,512]{1,0:T(8,128)(2,1)}, bf16[1024,512]{1,0:T(8,128)(2,1)S(1)}, u32[]{:S(2)}, u32[]{:S(2)}) collective-permute-start(bf16[1024,512]{1,0:T(8,128)(2,1)} %get-tuple-element.47.refs_0_), channel_id=1, source_target_pairs={{0,16},{8,24},{16,0},{24,8},{1,17},{9,25},{17,1},{25,9},{2,18},{10... | collective-permute-start | bytes 3145736 | tf_op jit(solution)/shard_map/ppermute | solution.py:209
  10.4 2.6 %collective-permute-start = (bf16[512,512]{1,0:T(8,128)(2,1)}, bf16[512,512]{1,0:T(8,128)(2,1)S(1)}, u32[]{:S(2)}, u32[]{:S(2)}) collective-permute-start(bf16[512,512]{1,0:T(8,128)(2,1)} %get-tuple-element.46.refs_6_), channel_id=1, source_target_pairs={{0,2},{1,3},{2,6},{3,7},{6,4},{7,5},{4,0},{5,1},{8,10},{9,11},{10,... | collective-permute-start | bytes 1572872 | tf_op jit(solution)/shard_map/ppermute | solution.py:206
  13.0 5.9 %collective-permute-done.1.refs_9_ = bf16[512,512]{1,0:T(8,128)(2,1)S(1)} collective-permute-done((bf16[512,512]{1,0:T(8,128)(2,1)}, bf16[512,512]{1,0:T(8,128)(2,1)S(1)}, u32[]{:S(2)}, u32[]{:S(2)}) %collective-permute-start.1) | collective-permute-done | bytes 524320 | tf_op jit(solution)/shard_map/ppermute | solution.py:206
  18.9 0.0 collective-permute-done.2.refs_7_
  18.9 0.0 collective-permute-start.3
  18.9 1.3 %collective-permute-start.7 = (bf16[512,512]{1,0:T(8,128)(2,1)S(1)}, bf16[512,512]{1,0:T(8,128)(2,1)S(1)}, u32[]{:S(2)}, u32[]{:S(2)}) collective-permute-start(bf16[512,512]{1,0:T(8,128)(2,1)S(1)} %collective-permute-done.1.refs_9_), channel_id=1, source_target_pairs={{0,2},{1,3},{2,6},{3,7},{6,4},{7,5},{4,0},{5,1},{8,10},{9,11},{10,... | collective-permute-start | bytes 1572872 | tf_op jit(solution)/shard_map/ppermute | solution.py:206
  20.2 10.0 %collective-permute-done.refs_10_ = bf16[512,512]{1,0:T(8,128)(2,1)S(1)} collective-permute-done((bf16[512,512]{1,0:T(8,128)(2,1)}, bf16[512,512]{1,0:T(8,128)(2,1)S(1)}, u32[]{:S(2)}, u32[]{:S(2)}) %collective-permute-start) | collective-permute-done | bytes 524320 | tf_op jit(solution)/shard_map/ppermute | solution.py:206
  30.1 0.0 collective-permute-done.3.refs_8_
  30.2 3.0 %collective-permute-done.4.refs_1_ = bf16[1024,512]{1,0:T(8,128)(2,1)S(1)} collective-permute-done((bf16[1024,512]{1,0:T(8,128)(2,1)}, bf16[1024,512]{1,0:T(8,128)(2,1)S(1)}, u32[]{:S(2)}, u32[]{:S(2)}) %collective-permute-start.4) | collective-permute-done | bytes 1048608 | tf_op jit(solution)/shard_map/ppermute | solution.py:208
  33.2 1.2 %collective-permute-done.5.refs_2_ = bf16[1024,512]{1,0:T(8,128)(2,1)S(1)} collective-permute-done((bf16[1024,512]{1,0:T(8,128)(2,1)}, bf16[1024,512]{1,0:T(8,128)(2,1)S(1)}, u32[]{:S(2)}, u32[]{:S(2)}) %collective-permute-start.5) | collective-permute-done | bytes 1048608 | tf_op jit(solution)/shard_map/ppermute | solution.py:209
  34.4 0.0 collective-permute-start.8
  34.4 0.0 copy-start
  34.4 0.0 copy-start.1
  34.5 0.0 copy-start.2
  34.5 0.0 copy-start.3
  34.5 1.6 %collective-permute-start.10 = (bf16[512,512]{1,0:T(8,128)(2,1)S(1)}, bf16[512,512]{1,0:T(8,128)(2,1)S(1)}, u32[]{:S(2)}, u32[]{:S(2)}) collective-permute-start(bf16[512,512]{1,0:T(8,128)(2,1)S(1)} %slice.26), channel_id=1, source_target_pairs={{0,16},{8,24},{16,0},{24,8},{1,17},{9,25},{17,1},{25,9},{2,18},{10... | collective-permute-start | bytes 1572872 | tf_op jit(solution)/shard_map/ppermute | solution.py:209
  36.1 0.6 collective-permute-start.11
  36.7 2.6 %collective-permute-start.6 = (bf16[512,512]{1,0:T(8,128)(2,1)S(1)}, bf16[512,512]{1,0:T(8,128)(2,1)S(1)}, u32[]{:S(2)}, u32[]{:S(2)}) collective-permute-start(bf16[512,512]{1,0:T(8,128)(2,1)S(1)} %collective-permute-done.refs_10_), channel_id=1, source_target_pairs={{0,2},{1,3},{2,6},{3,7},{6,4},{7,5},{4,0},{5,1},{8,10},{9,11},{10,... | collective-permute-start | bytes 1572872 | tf_op jit(solution)/shard_map/ppermute | solution.py:206
  39.3 1.6 %collective-permute-done.7.refs_13_ = bf16[512,512]{1,0:T(8,128)(2,1)S(1)} collective-permute-done((bf16[512,512]{1,0:T(8,128)(2,1)S(1)}, bf16[512,512]{1,0:T(8,128)(2,1)S(1)}, u32[]{:S(2)}, u32[]{:S(2)}) %collective-permute-start.7) | collective-permute-done | bytes 524320 | tf_op jit(solution)/shard_map/ppermute | solution.py:206
  40.9 0.0 collective-permute-done.8.refs_11_
  40.9 0.0 collective-permute-start.9
  41.0 1.7 %collective-permute-start.15 = (bf16[256,512]{1,0:T(8,128)(2,1)S(1)}, bf16[256,512]{1,0:T(8,128)(2,1)S(1)}, u32[]{:S(2)}, u32[]{:S(2)}) collective-permute-start(bf16[256,512]{1,0:T(8,128)(2,1)S(1)} %get-tuple-element.81), channel_id=1, source_target_pairs={{0,2},{1,3},{2,6},{3,7},{6,4},{7,5},{4,0},{5,1},{8,10},{9,11},{10,... | collective-permute-start | bytes 786440 | tf_op jit(solution)/shard_map/ppermute | solution.py:206
  42.6 6.2 %collective-permute-done.10.refs_3_ = bf16[512,512]{1,0:T(8,128)(2,1)S(1)} collective-permute-done((bf16[512,512]{1,0:T(8,128)(2,1)S(1)}, bf16[512,512]{1,0:T(8,128)(2,1)S(1)}, u32[]{:S(2)}, u32[]{:S(2)}) %collective-permute-start.10) | collective-permute-done | bytes 524320 | tf_op jit(solution)/shard_map/ppermute | solution.py:209
  48.9 1.3 %collective-permute-done.11.refs_4_ = bf16[512,512]{1,0:T(8,128)(2,1)S(1)} collective-permute-done((bf16[512,512]{1,0:T(8,128)(2,1)S(1)}, bf16[512,512]{1,0:T(8,128)(2,1)S(1)}, u32[]{:S(2)}, u32[]{:S(2)}) %collective-permute-start.11) | collective-permute-done | bytes 524320 | tf_op jit(solution)/shard_map/ppermute | solution.py:208
  50.2 2.2 %collective-permute-done.6.refs_14_ = bf16[512,512]{1,0:T(8,128)(2,1)S(1)} collective-permute-done((bf16[512,512]{1,0:T(8,128)(2,1)S(1)}, bf16[512,512]{1,0:T(8,128)(2,1)S(1)}, u32[]{:S(2)}, u32[]{:S(2)}) %collective-permute-start.6) | collective-permute-done | bytes 524320 | tf_op jit(solution)/shard_map/ppermute | solution.py:206
  52.4 0.0 collective-permute-done.9.refs_12_
  52.4 0.0 collective-permute-start.17
  52.4 0.5 collective-permute-start.18
  52.9 1.7 %collective-permute-start.14 = (bf16[256,512]{1,0:T(8,128)(2,1)S(1)}, bf16[256,512]{1,0:T(8,128)(2,1)S(1)}, u32[]{:S(2)}, u32[]{:S(2)}) collective-permute-start(bf16[256,512]{1,0:T(8,128)(2,1)S(1)} %get-tuple-element.82), channel_id=1, source_target_pairs={{0,2},{1,3},{2,6},{3,7},{6,4},{7,5},{4,0},{5,1},{8,10},{9,11},{10,... | collective-permute-start | bytes 786440 | tf_op jit(solution)/shard_map/ppermute | solution.py:206
  54.6 3.4 %collective-permute-done.15.refs_0_ = bf16[256,512]{1,0:T(8,128)(2,1)S(1)} collective-permute-done((bf16[256,512]{1,0:T(8,128)(2,1)S(1)}, bf16[256,512]{1,0:T(8,128)(2,1)S(1)}, u32[]{:S(2)}, u32[]{:S(2)}) %collective-permute-start.15) | collective-permute-done | bytes 262176 | tf_op jit(solution)/shard_map/ppermute | solution.py:206
  58.0 0.0 collective-permute-start.16
  58.0 1.7 %collective-permute-start.13 = (bf16[256,512]{1,0:T(8,128)(2,1)S(1)}, bf16[256,512]{1,0:T(8,128)(2,1)S(1)}, u32[]{:S(2)}, u32[]{:S(2)}) collective-permute-start(bf16[256,512]{1,0:T(8,128)(2,1)S(1)} %get-tuple-element.83), channel_id=1, source_target_pairs={{0,2},{1,3},{2,6},{3,7},{6,4},{7,5},{4,0},{5,1},{8,10},{9,11},{10,... | collective-permute-start | bytes 786440 | tf_op jit(solution)/shard_map/ppermute | solution.py:206
  59.8 3.8 %collective-permute-done.14.refs_1_ = bf16[256,512]{1,0:T(8,128)(2,1)S(1)} collective-permute-done((bf16[256,512]{1,0:T(8,128)(2,1)S(1)}, bf16[256,512]{1,0:T(8,128)(2,1)S(1)}, u32[]{:S(2)}, u32[]{:S(2)}) %collective-permute-start.14) | collective-permute-done | bytes 262176 | tf_op jit(solution)/shard_map/ppermute | solution.py:206
  63.6 0.0 collective-permute-done.16.refs_2_
  63.6 0.0 collective-permute-done.17.refs_15_
  63.6 0.0 collective-permute-done.18.refs_16_
  63.6 0.1 collective-permute-start.19
  63.7 1.7 %collective-permute-start.12 = (bf16[256,512]{1,0:T(8,128)(2,1)S(1)}, bf16[256,512]{1,0:T(8,128)(2,1)S(1)}, u32[]{:S(2)}, u32[]{:S(2)}) collective-permute-start(bf16[256,512]{1,0:T(8,128)(2,1)S(1)} %get-tuple-element.84), channel_id=1, source_target_pairs={{0,2},{1,3},{2,6},{3,7},{6,4},{7,5},{4,0},{5,1},{8,10},{9,11},{10,... | collective-permute-start | bytes 786440 | tf_op jit(solution)/shard_map/ppermute | solution.py:206
  65.5 0.0 copy-done
  65.5 0.0 copy-done.1
  65.5 0.0 copy-done.2
  65.5 0.0 copy-done.3
  65.5 4.6 %shard_map.57 = (f32[768,512]{1,0:T(8,128)S(1)}, f32[256,512]{1,0:T(8,128)S(1)}, bf16[512,512]{1,0:T(8,128)(2,1)S(1)}, bf16[512,512]{1,0:T(8,128)(2,1)S(1)}, bf16[256,512]{1,0:T(8,128)(2,1)S(1)}) custom-call(bf16[1024,512]{1,0:T(8,128)(2,1)S(1)} %copy-done.1, bf16[1024,512]{1,0:T(8,128)(2,1)S(1)} %collective-permute-done.4.refs_1_, ...), custom_call_target="tpu_custom_call" | custom-call | flops 1 | bytes 1 | tf_op jit(solution)/shard_map/pallas_call | solution.py:136
  70.0 0.0 collective-permute-done.13
  70.0 0.0 collective-permute-done.19.refs_3_
  70.1 0.2 collective-permute-start.20
  70.3 0.3 collective-permute-start.21
  70.7 1.8 %shard_map.58.refs_4_ = bf16[1024,512]{1,0:T(8,128)(2,1)} custom-call(s32[4,8]{1,0:T(4,128)S(1)} %bitcast.8, f32[768,512]{1,0:T(8,128)S(1)} %get-tuple-element.71.total_ref, bf16[512,512]{1,0:T(8,128)(2,1)S(1)} %get-tuple-element.72.near_ref, bf16[512,512]{1,0:T(8,128)(2,1)S(1)} %get-tuple-element.73.far_ref, ...), custom_call_target="tpu_custom_call" | custom-call | flops 1 | bytes 1 | tf_op jit(solution)/shard_map/pallas_call | solution.py:191
  72.5 0.0 collective-permute-done.20.refs_2_
  72.5 0.0 collective-permute-done.21.refs_3_
  72.5 1.6 %shard_map.59 = bf16[1024,512]{1,0:T(8,128)(2,1)} custom-call(s32[4,8]{1,0:T(4,128)S(1)} %bitcast.9, f32[768,512]{1,0:T(8,128)S(1)} %get-tuple-element.71.total_ref, bf16[512,512]{1,0:T(8,128)(2,1)S(1)} %get-tuple-element.72.near_ref, bf16[512,512]{1,0:T(8,128)(2,1)S(1)} %get-tuple-element.73.far_ref, ...), custom_call_target="tpu_custom_call", output_to_operand_aliasing={{}: (8, {})} | custom-call | flops 1 | bytes 1 | tf_op jit(solution)/shard_map/pallas_call | solution.py:191
  74.2 0.1 collective-permute-done.12
  74.3 0.2 collective-permute-start.22
  74.4 0.3 fusion.5
  74.7 1.1 %collective-permute-done.22 = bf16[256,512]{1,0:T(8,128)(2,1)S(1)} collective-permute-done((bf16[256,512]{1,0:T(8,128)(2,1)S(1)}, bf16[256,512]{1,0:T(8,128)(2,1)S(1)}, u32[]{:S(2)}, u32[]{:S(2)}) %collective-permute-start.22) | collective-permute-done | bytes 262176 | tf_op jit(solution)/shard_map/ppermute | solution.py:207
  75.8 0.3 fusion.6
  76.1 0.9 %fusion.1 = bf16[1024,512]{1,0:T(8,128)(2,1)} fusion(bf16[1024,512]{1,0:T(8,128)(2,1)} %shard_map.59, bf16[256,512]{1,0:T(8,128)(2,1)S(1)} %get-tuple-element.80, f32[256,512]{1,0:T(8,128)S(1)} %fusion.6, f32[256,512]{1,0:T(8,128)S(1)} %get-tuple-element.78, f32[256,512]{1,0:T(8,128)S(1)} %fusion.5), kind=kLoop, calls=%fused_computation.2 | loop fusion | flops 917504 | bytes 2097152 | tf_op jit(solution)/shard_map/dynamic_update_slice | solution.py:248
  (5 shorter events, 0.2 us)
Async XLA Ops:
  1.9 17.1 %collective-permute-start.1 = (bf16[512,512]{1,0:T(8,128)(2,1)}, bf16[512,512]{1,0:T(8,128)(2,1)S(1)}, u32[]{:S(2)}, u32[]{:S(2)}) collective-permute-start(bf16[512,512]{1,0:T(8,128)(2,1)} %shard_map.55.refs_5_), channel_id=1, source_target_pairs={{0,2},{1,3},{2,6},{3,7},{6,4},{7,5},{4,0},{5,1},{8,10},{9,11},{10,... | collective-permute-start | bytes 1572872 | tf_op jit(solution)/shard_map/ppermute | solution.py:206
  4.9 14.0 %collective-permute-start.2 = (bf16[512,512]{1,0:T(8,128)(2,1)}, bf16[512,512]{1,0:T(8,128)(2,1)S(1)}, u32[]{:S(2)}, u32[]{:S(2)}) collective-permute-start(bf16[512,512]{1,0:T(8,128)(2,1)} %shard_map.55.refs_5_), channel_id=1, source_target_pairs={{0,1},{1,0},{2,3},{3,2},{4,5},{5,4},{6,7},{7,6},{8,9},{9,8},{10,11... | collective-permute-start | bytes 1572872 | tf_op jit(solution)/shard_map/ppermute | solution.py:207
  7.3 25.8 %collective-permute-start.4 = (bf16[1024,512]{1,0:T(8,128)(2,1)}, bf16[1024,512]{1,0:T(8,128)(2,1)S(1)}, u32[]{:S(2)}, u32[]{:S(2)}) collective-permute-start(bf16[1024,512]{1,0:T(8,128)(2,1)} %get-tuple-element.47.refs_0_), channel_id=1, source_target_pairs={{0,8},{8,0},{16,24},{24,16},{1,9},{9,1},{17,25},{25,17},{2,10},{10... | collective-permute-start | bytes 3145736 | tf_op jit(solution)/shard_map/ppermute | solution.py:208
  8.9 25.5 %collective-permute-start.5 = (bf16[1024,512]{1,0:T(8,128)(2,1)}, bf16[1024,512]{1,0:T(8,128)(2,1)S(1)}, u32[]{:S(2)}, u32[]{:S(2)}) collective-permute-start(bf16[1024,512]{1,0:T(8,128)(2,1)} %get-tuple-element.47.refs_0_), channel_id=1, source_target_pairs={{0,16},{8,24},{16,0},{24,8},{1,17},{9,25},{17,1},{25,9},{2,18},{10... | collective-permute-start | bytes 3145736 | tf_op jit(solution)/shard_map/ppermute | solution.py:209
  10.4 19.7 %collective-permute-start = (bf16[512,512]{1,0:T(8,128)(2,1)}, bf16[512,512]{1,0:T(8,128)(2,1)S(1)}, u32[]{:S(2)}, u32[]{:S(2)}) collective-permute-start(bf16[512,512]{1,0:T(8,128)(2,1)} %get-tuple-element.46.refs_6_), channel_id=1, source_target_pairs={{0,2},{1,3},{2,6},{3,7},{6,4},{7,5},{4,0},{5,1},{8,10},{9,11},{10,... | collective-permute-start | bytes 1572872 | tf_op jit(solution)/shard_map/ppermute | solution.py:206
  18.9 11.2 %collective-permute-start.3 = (bf16[512,512]{1,0:T(8,128)(2,1)}, bf16[512,512]{1,0:T(8,128)(2,1)S(1)}, u32[]{:S(2)}, u32[]{:S(2)}) collective-permute-start(bf16[512,512]{1,0:T(8,128)(2,1)} %get-tuple-element.46.refs_6_), channel_id=1, source_target_pairs={{0,1},{1,0},{2,3},{3,2},{4,5},{5,4},{6,7},{7,6},{8,9},{9,8},{10,11... | collective-permute-start | bytes 1572872 | tf_op jit(solution)/shard_map/ppermute | solution.py:207
  18.9 22.0 %collective-permute-start.7 = (bf16[512,512]{1,0:T(8,128)(2,1)S(1)}, bf16[512,512]{1,0:T(8,128)(2,1)S(1)}, u32[]{:S(2)}, u32[]{:S(2)}) collective-permute-start(bf16[512,512]{1,0:T(8,128)(2,1)S(1)} %collective-permute-done.1.refs_9_), channel_id=1, source_target_pairs={{0,2},{1,3},{2,6},{3,7},{6,4},{7,5},{4,0},{5,1},{8,10},{9,11},{10,... | collective-permute-start | bytes 1572872 | tf_op jit(solution)/shard_map/ppermute | solution.py:206
  34.4 6.5 %collective-permute-start.8 = (bf16[512,512]{1,0:T(8,128)(2,1)S(1)}, bf16[512,512]{1,0:T(8,128)(2,1)S(1)}, u32[]{:S(2)}, u32[]{:S(2)}) collective-permute-start(bf16[512,512]{1,0:T(8,128)(2,1)S(1)} %collective-permute-done.1.refs_9_), channel_id=1, source_target_pairs={{0,1},{1,0},{2,3},{3,2},{4,5},{5,4},{6,7},{7,6},{8,9},{9,8},{10,11... | collective-permute-start | bytes 1572872 | tf_op jit(solution)/shard_map/ppermute | solution.py:207
  34.4 31.0 %copy-start = (bf16[512,512]{1,0:T(8,128)(2,1)S(1)}, bf16[512,512]{1,0:T(8,128)(2,1)}, u32[]{:S(2)}) copy-start(bf16[512,512]{1,0:T(8,128)(2,1)} %shard_map.55.refs_5_) | copy-start | bytes 1572868
  34.4 31.0 %copy-start.1 = (bf16[1024,512]{1,0:T(8,128)(2,1)S(1)}, bf16[1024,512]{1,0:T(8,128)(2,1)}, u32[]{:S(2)}) copy-start(bf16[1024,512]{1,0:T(8,128)(2,1)} %get-tuple-element.47.refs_0_) | copy-start | bytes 3145732
  34.5 31.0 %copy-start.2 = (bf16[512,512]{1,0:T(8,128)(2,1)S(1)}, bf16[512,512]{1,0:T(8,128)(2,1)}, u32[]{:S(2)}) copy-start(bf16[512,512]{1,0:T(8,128)(2,1)} %get-tuple-element.46.refs_6_) | copy-start | bytes 1572868
  34.5 31.0 %copy-start.3 = (s32[8,4]{0,1:T(4,128)S(1)}, s32[8,4]{0,1:T(4,128)}, u32[]{:S(2)}) copy-start(s32[8,4]{0,1:T(4,128)} %param.9) | copy-start | bytes 388
  34.5 14.4 %collective-permute-start.10 = (bf16[512,512]{1,0:T(8,128)(2,1)S(1)}, bf16[512,512]{1,0:T(8,128)(2,1)S(1)}, u32[]{:S(2)}, u32[]{:S(2)}) collective-permute-start(bf16[512,512]{1,0:T(8,128)(2,1)S(1)} %slice.26), channel_id=1, source_target_pairs={{0,16},{8,24},{16,0},{24,8},{1,17},{9,25},{17,1},{25,9},{2,18},{10... | collective-permute-start | bytes 1572872 | tf_op jit(solution)/shard_map/ppermute | solution.py:209
  36.1 14.1 %collective-permute-start.11 = (bf16[512,512]{1,0:T(8,128)(2,1)S(1)}, bf16[512,512]{1,0:T(8,128)(2,1)S(1)}, u32[]{:S(2)}, u32[]{:S(2)}) collective-permute-start(bf16[512,512]{1,0:T(8,128)(2,1)S(1)} %slice.27), channel_id=1, source_target_pairs={{0,8},{8,0},{16,24},{24,16},{1,9},{9,1},{17,25},{25,17},{2,10},{10... | collective-permute-start | bytes 1572872 | tf_op jit(solution)/shard_map/ppermute | solution.py:208
  36.7 15.7 %collective-permute-start.6 = (bf16[512,512]{1,0:T(8,128)(2,1)S(1)}, bf16[512,512]{1,0:T(8,128)(2,1)S(1)}, u32[]{:S(2)}, u32[]{:S(2)}) collective-permute-start(bf16[512,512]{1,0:T(8,128)(2,1)S(1)} %collective-permute-done.refs_10_), channel_id=1, source_target_pairs={{0,2},{1,3},{2,6},{3,7},{6,4},{7,5},{4,0},{5,1},{8,10},{9,11},{10,... | collective-permute-start | bytes 1572872 | tf_op jit(solution)/shard_map/ppermute | solution.py:206
  40.9 11.5 %collective-permute-start.9 = (bf16[512,512]{1,0:T(8,128)(2,1)S(1)}, bf16[512,512]{1,0:T(8,128)(2,1)S(1)}, u32[]{:S(2)}, u32[]{:S(2)}) collective-permute-start(bf16[512,512]{1,0:T(8,128)(2,1)S(1)} %collective-permute-done.refs_10_), channel_id=1, source_target_pairs={{0,1},{1,0},{2,3},{3,2},{4,5},{5,4},{6,7},{7,6},{8,9},{9,8},{10,11... | collective-permute-start | bytes 1572872 | tf_op jit(solution)/shard_map/ppermute | solution.py:207
  41.0 17.1 %collective-permute-start.15 = (bf16[256,512]{1,0:T(8,128)(2,1)S(1)}, bf16[256,512]{1,0:T(8,128)(2,1)S(1)}, u32[]{:S(2)}, u32[]{:S(2)}) collective-permute-start(bf16[256,512]{1,0:T(8,128)(2,1)S(1)} %get-tuple-element.81), channel_id=1, source_target_pairs={{0,2},{1,3},{2,6},{3,7},{6,4},{7,5},{4,0},{5,1},{8,10},{9,11},{10,... | collective-permute-start | bytes 786440 | tf_op jit(solution)/shard_map/ppermute | solution.py:206
  52.4 11.2 %collective-permute-start.17 = (bf16[512,512]{1,0:T(8,128)(2,1)S(1)}, bf16[512,512]{1,0:T(8,128)(2,1)S(1)}, u32[]{:S(2)}, u32[]{:S(2)}) collective-permute-start(bf16[512,512]{1,0:T(8,128)(2,1)S(1)} %collective-permute-done.7.refs_13_), channel_id=1, source_target_pairs={{0,1},{1,0},{2,3},{3,2},{4,5},{5,4},{6,7},{7,6},{8,9},{9,8},{10,11... | collective-permute-start | bytes 1572872 | tf_op jit(solution)/shard_map/ppermute | solution.py:207
  52.4 11.2 %collective-permute-start.18 = (bf16[512,512]{1,0:T(8,128)(2,1)S(1)}, bf16[512,512]{1,0:T(8,128)(2,1)S(1)}, u32[]{:S(2)}, u32[]{:S(2)}) collective-permute-start(bf16[512,512]{1,0:T(8,128)(2,1)S(1)} %collective-permute-done.6.refs_14_), channel_id=1, source_target_pairs={{0,1},{1,0},{2,3},{3,2},{4,5},{5,4},{6,7},{7,6},{8,9},{9,8},{10,11... | collective-permute-start | bytes 1572872 | tf_op jit(solution)/shard_map/ppermute | solution.py:207
  52.9 10.7 %collective-permute-start.14 = (bf16[256,512]{1,0:T(8,128)(2,1)S(1)}, bf16[256,512]{1,0:T(8,128)(2,1)S(1)}, u32[]{:S(2)}, u32[]{:S(2)}) collective-permute-start(bf16[256,512]{1,0:T(8,128)(2,1)S(1)} %get-tuple-element.82), channel_id=1, source_target_pairs={{0,2},{1,3},{2,6},{3,7},{6,4},{7,5},{4,0},{5,1},{8,10},{9,11},{10,... | collective-permute-start | bytes 786440 | tf_op jit(solution)/shard_map/ppermute | solution.py:206
  58.0 5.6 %collective-permute-start.16 = (bf16[256,512]{1,0:T(8,128)(2,1)S(1)}, bf16[256,512]{1,0:T(8,128)(2,1)S(1)}, u32[]{:S(2)}, u32[]{:S(2)}) collective-permute-start(bf16[256,512]{1,0:T(8,128)(2,1)S(1)} %collective-permute-done.15.refs_0_), channel_id=1, source_target_pairs={{0,1},{1,0},{2,3},{3,2},{4,5},{5,4},{6,7},{7,6},{8,9},{9,8},{10,11... | collective-permute-start | bytes 786440 | tf_op jit(solution)/shard_map/ppermute | solution.py:207
  58.0 12.0 %collective-permute-start.13 = (bf16[256,512]{1,0:T(8,128)(2,1)S(1)}, bf16[256,512]{1,0:T(8,128)(2,1)S(1)}, u32[]{:S(2)}, u32[]{:S(2)}) collective-permute-start(bf16[256,512]{1,0:T(8,128)(2,1)S(1)} %get-tuple-element.83), channel_id=1, source_target_pairs={{0,2},{1,3},{2,6},{3,7},{6,4},{7,5},{4,0},{5,1},{8,10},{9,11},{10,... | collective-permute-start | bytes 786440 | tf_op jit(solution)/shard_map/ppermute | solution.py:206
  63.6 6.4 %collective-permute-start.19 = (bf16[256,512]{1,0:T(8,128)(2,1)S(1)}, bf16[256,512]{1,0:T(8,128)(2,1)S(1)}, u32[]{:S(2)}, u32[]{:S(2)}) collective-permute-start(bf16[256,512]{1,0:T(8,128)(2,1)S(1)} %collective-permute-done.14.refs_1_), channel_id=1, source_target_pairs={{0,1},{1,0},{2,3},{3,2},{4,5},{5,4},{6,7},{7,6},{8,9},{9,8},{10,11... | collective-permute-start | bytes 786440 | tf_op jit(solution)/shard_map/ppermute | solution.py:207
  63.7 10.5 %collective-permute-start.12 = (bf16[256,512]{1,0:T(8,128)(2,1)S(1)}, bf16[256,512]{1,0:T(8,128)(2,1)S(1)}, u32[]{:S(2)}, u32[]{:S(2)}) collective-permute-start(bf16[256,512]{1,0:T(8,128)(2,1)S(1)} %get-tuple-element.84), channel_id=1, source_target_pairs={{0,2},{1,3},{2,6},{3,7},{6,4},{7,5},{4,0},{5,1},{8,10},{9,11},{10,... | collective-permute-start | bytes 786440 | tf_op jit(solution)/shard_map/ppermute | solution.py:206
  70.1 2.4 %collective-permute-start.20 = (bf16[128,512]{1,0:T(8,128)(2,1)S(1)}, bf16[128,512]{1,0:T(8,128)(2,1)S(1)}, u32[]{:S(2)}, u32[]{:S(2)}) collective-permute-start(bf16[128,512]{1,0:T(8,128)(2,1)S(1)} %get-tuple-element.86.refs_0_), channel_id=1, source_target_pairs={{0,1},{1,0},{2,3},{3,2},{4,5},{5,4},{6,7},{7,6},{8,9},{9,8},{10,11... | collective-permute-start | bytes 393224 | tf_op jit(solution)/shard_map/ppermute | solution.py:207
  70.3 2.2 %collective-permute-start.21 = (bf16[128,512]{1,0:T(8,128)(2,1)S(1)}, bf16[128,512]{1,0:T(8,128)(2,1)S(1)}, u32[]{:S(2)}, u32[]{:S(2)}) collective-permute-start(bf16[128,512]{1,0:T(8,128)(2,1)S(1)} %get-tuple-element.85.refs_1_), channel_id=1, source_target_pairs={{0,1},{1,0},{2,3},{3,2},{4,5},{5,4},{6,7},{7,6},{8,9},{9,8},{10,11... | collective-permute-start | bytes 393224 | tf_op jit(solution)/shard_map/ppermute | solution.py:207
  74.3 1.5 %collective-permute-start.22 = (bf16[256,512]{1,0:T(8,128)(2,1)S(1)}, bf16[256,512]{1,0:T(8,128)(2,1)S(1)}, u32[]{:S(2)}, u32[]{:S(2)}) collective-permute-start(bf16[256,512]{1,0:T(8,128)(2,1)S(1)} %collective-permute-done.12), channel_id=1, source_target_pairs={{0,1},{1,0},{2,3},{3,2},{4,5},{5,4},{6,7},{7,6},{8,9},{9,8},{10,11... | collective-permute-start | bytes 786440 | tf_op jit(solution)/shard_map/ppermute | solution.py:207
